TPU v7x, 32 devices: a whole 2x2x4 slice. The times are simulated.
32 devices in a mesh: dp: 8 (over y, x, core), mp: 4 (over z).
Axes of the slice: x: 2, y: 2, z: 4, core: 2. Of those that a mesh axis runs over, the one named last changes fastest.
Arguments:
- node_state: bfloat16 [5568, 128], P('dp', 'mp'), may hold values from -6 to 6
- edge_feat: bfloat16 [16, 155904], P(None, 'dp'), may hold values from -6 to 6
- sender: int32 [155904], P('dp'), may hold values from 0 to 28, as said below
- receiver: int32 [155904], P('dp'), may hold values from 0 to 28, as said below
- edge_mask: int32 [155904], P('dp'), may hold values from 0 to 1, as said below
- node_mask: int32 [5568], P('dp'), may hold values from 0 to 1, as said below
- out_grad: float32 [5568, 128], P('dp', 'mp'), may hold values from -6 to 6
- edge_in: float32 [16, 128], P(None, 'dp'), may hold values from -1.5 to 1.5
- edge_out: float32 [128, 16384], P('dp', 'mp'), may hold values from -0.0078125 to 0.0078125
- gru_weight: float32 [2, 3, 128, 128], P(None, None, 'dp', 'mp'), may hold values from -0.5 to 0.5
- edge_in_m1: float32 [16, 128], P(None, 'dp'), may hold values from -96 to 96
- edge_in_m2: float32 [16, 128], P(None, 'dp'), may hold values from 222.72 to 890.88
- edge_out_m1: float32 [128, 16384], P('dp', 'mp'), may hold values from -448 to 448
- edge_out_m2: float32 [128, 16384], P('dp', 'mp'), may hold values from 5612.544 to 22450.176
- gru_m1: float32 [2, 3, 128, 128], P(None, None, 'dp', 'mp'), may hold values from -56 to 56
- gru_m2: float32 [2, 3, 128, 128], P(None, None, 'dp', 'mp'), may hold values from 94.656 to 378.624
Outputs:
- out_state: float32 [5568, 128], P('dp', 'mp')
- grad_state: float32 [5568, 128], P('dp', 'mp')
- grad_edges: float32 [16, 155904], P(None, 'dp')
- edge_in_m1_new: float32 [16, 128], P(None, 'dp')
- edge_in_m2_new: float32 [16, 128], P(None, 'dp')
- edge_in_new: float32 [16, 128], P(None, 'dp')
- edge_in_low: bfloat16 [16, 128], P(None, 'dp')
- edge_out_m1_new: float32 [128, 16384], P('dp', 'mp')
- edge_out_m2_new: float32 [128, 16384], P('dp', 'mp')
- edge_out_new: float32 [128, 16384], P('dp', 'mp')
- edge_out_low: bfloat16 [128, 16384], P('dp', 'mp')
- gru_m1_new: float32 [2, 3, 128, 128], P(None, None, 'dp', 'mp')
- gru_m2_new: float32 [2, 3, 128, 128], P(None, None, 'dp', 'mp')
- gru_new: float32 [2, 3, 128, 128], P(None, None, 'dp', 'mp')
- gru_low: bfloat16 [2, 3, 128, 128], P(None, None, 'dp', 'mp')
Inputs may be any that keep to these rules, and one draw needn't show every extreme that they name: In every molecule the 812 edges are all ordered pairs of distinct atoms, each once, in an order drawn from the seed; sender and receiver differ. `receiver`: in every molecule the 812 edges are all ordered pairs of distinct atoms, each once. `edge_mask`: 0 wherever the sender or the receiver is a padded atom. `node_mask`: in each molecule a run of ones followed by zeros, with at least 10 ones.
All inputs are finite; a program needn't handle non-finite values.
Results may differ from a plain program's by a relative error of at most 0.018.
Values may be sent and summed in bfloat16 or wider, within the bound.
A program may use at most 128 MiB of HBM per device.

v0:
```python
import jax
import jax.numpy as jnp
from jax import lax
from jax.sharding import PartitionSpec as P

HID = 128
EFEAT = 16
MOL_ATOMS = 29
MOL_EDGES = 812
MOL_MB = 8
MICRO = 3
STEP = 5


highest = lax.Precision.HIGHEST
beta_one = 0.5
beta_two = 0.5
learn_rate = 0.05
decay_rate = 0.01
epsilon = 1e-08


def adam_update(weight, gradient, first_moment, second_moment):
    first_new = beta_one * first_moment + (1.0 - beta_one) * gradient
    second_new = beta_two * second_moment + (1.0 - beta_two) * gradient * gradient
    mean_hat = first_new / (1.0 - beta_one**STEP)
    square_hat = second_new / (1.0 - beta_two**STEP)
    weight_new = weight - learn_rate * (
        mean_hat / (jnp.sqrt(square_hat) + epsilon) + decay_rate * weight
    )
    return (first_new, second_new, weight_new, weight_new.astype(jnp.bfloat16))


def atom_table(indices, number_type):
    atom_iota = jnp.arange(MOL_ATOMS, dtype=jnp.int32)
    return (indices[:, None] == atom_iota[None, :]).astype(number_type)


def silu_slope(preact):
    logistic = jax.nn.sigmoid(preact)
    return logistic * (1.0 + preact * (1.0 - logistic))


def first_dims():
    return (((0,), (0,)), ((), ()))


def edge_network(features_m, senders_m, states_m, w_in, w_out):
    preact = lax.dot_general(features_m, w_in, first_dims(), preferred_element_type=jnp.float32)
    hidden = jax.nn.silu(preact).astype(jnp.bfloat16)
    matrices = jnp.dot(hidden, w_out, preferred_element_type=jnp.float32).astype(jnp.bfloat16)
    gathered = jnp.dot(
        atom_table(senders_m, jnp.bfloat16), states_m, preferred_element_type=jnp.float32
    ).astype(jnp.bfloat16)
    return (preact, hidden, matrices, gathered)


def body(
    node_state,
    edge_feat,
    sender,
    receiver,
    edge_mask,
    node_mask,
    out_grad,
    edge_in,
    edge_out,
    gru_weight,
    edge_in_m1,
    edge_in_m2,
    edge_out_m1,
    edge_out_m2,
    gru_m1,
    gru_m2,
):
    atoms_mb = MOL_MB * MOL_ATOMS
    edges_mb = MOL_MB * MOL_EDGES
    rows_out = edge_out.shape[1] // HID
    state_full = lax.all_gather(node_state, "mp", axis=1, tiled=True)
    shard_sums = (
        jnp.zeros(edge_in.shape, jnp.float32),
        jnp.zeros(edge_out.shape, jnp.float32),
        jnp.zeros(gru_weight.shape, jnp.float32),
    )
    out_parts = []
    state_parts = []
    feature_parts = []
    for batch_index in range(MICRO):
        w_in, w_out, w_gru = (
            lax.all_gather(edge_in.astype(jnp.bfloat16), "dp", axis=1, tiled=True),
            lax.all_gather(edge_out.astype(jnp.bfloat16), "dp", axis=0, tiled=True),
            lax.all_gather(gru_weight.astype(jnp.bfloat16), "dp", axis=2, tiled=True),
        )
        atom_start = batch_index * atoms_mb
        edge_start = batch_index * edges_mb
        states_mb = state_full[atom_start : atom_start + atoms_mb]
        own_state = node_state[atom_start : atom_start + atoms_mb].astype(jnp.float32)
        atom_live = node_mask[atom_start : atom_start + atoms_mb].astype(jnp.float32)[:, None]
        features = (
            edge_feat[:, edge_start : edge_start + edges_mb]
            .reshape(EFEAT, MOL_MB, MOL_EDGES)
            .transpose(1, 0, 2)
        )
        senders = sender[edge_start : edge_start + edges_mb].reshape(MOL_MB, MOL_EDGES)
        receivers = receiver[edge_start : edge_start + edges_mb].reshape(MOL_MB, MOL_EDGES)
        edge_live = (
            edge_mask[edge_start : edge_start + edges_mb]
            .reshape(MOL_MB, MOL_EDGES)
            .astype(jnp.float32)
        )
        per_states = states_mb.reshape(MOL_MB, MOL_ATOMS, HID)

        def forward_one(running, pieces):
            features_m, senders_m, receivers_m, live_m, states_m = pieces
            preact, hidden, matrices, gathered = edge_network(
                features_m, senders_m, states_m, w_in, w_out
            )
            message = (
                jnp.einsum(
                    "erk,ek->er",
                    matrices.reshape(MOL_EDGES, rows_out, HID),
                    gathered,
                    preferred_element_type=jnp.float32,
                )
                * live_m[:, None]
            )
            summed = lax.dot_general(
                atom_table(receivers_m, jnp.float32), message, first_dims(), precision=highest
            )
            return (running, summed)

        unused, summed = lax.scan(
            forward_one, 0, (features, senders, receivers, edge_live, per_states)
        )
        messages = summed.reshape(atoms_mb, rows_out).astype(jnp.bfloat16)
        message_full = lax.all_gather(messages, "mp", axis=1, tiled=True)
        gate_in = jnp.einsum(
            "ai,gij->gaj", message_full, w_gru[0], preferred_element_type=jnp.float32
        )
        gate_state = jnp.einsum(
            "ai,gij->gaj", states_mb, w_gru[1], preferred_element_type=jnp.float32
        )
        reset_gate = jax.nn.sigmoid(gate_in[0] + gate_state[0])
        update = jax.nn.sigmoid(gate_in[1] + gate_state[1])
        candidate = jnp.tanh(gate_in[2] + reset_gate * gate_state[2])
        out_parts.append(atom_live * ((1.0 - update) * candidate + update * own_state))
        cotangent = out_grad[atom_start : atom_start + atoms_mb] * atom_live
        cand_pre = cotangent * (1.0 - update) * (1.0 - candidate * candidate)
        update_pre = cotangent * (own_state - candidate) * update * (1.0 - update)
        reset_pre = cand_pre * gate_state[2] * reset_gate * (1.0 - reset_gate)
        grad_in_gate = jnp.stack([reset_pre, update_pre, cand_pre]).astype(jnp.bfloat16)
        grad_state_gate = jnp.stack([reset_pre, update_pre, cand_pre * reset_gate]).astype(
            jnp.bfloat16
        )
        grad_gru = jnp.stack(
            [
                jnp.einsum(
                    "ai,gaj->gij", message_full, grad_in_gate, preferred_element_type=jnp.float32
                ),
                jnp.einsum(
                    "ai,gaj->gij", states_mb, grad_state_gate, preferred_element_type=jnp.float32
                ),
            ]
        )
        message_part = jnp.einsum(
            "gaj,gij->ai", grad_in_gate, w_gru[0], preferred_element_type=jnp.float32
        )
        state_part = jnp.einsum(
            "gaj,gij->ai", grad_state_gate, w_gru[1], preferred_element_type=jnp.float32
        )
        message_grad = lax.psum_scatter(
            message_part.astype(jnp.bfloat16), "mp", scatter_dimension=1, tiled=True
        )
        per_grads = message_grad.reshape(MOL_MB, MOL_ATOMS, rows_out)

        def backward_one(running, pieces):
            out_total, in_total = running
            features_m, senders_m, receivers_m, live_m, states_m, grad_mol = pieces
            preact, hidden, matrices, gathered = edge_network(
                features_m, senders_m, states_m, w_in, w_out
            )
            edge_grad = (
                jnp.dot(
                    atom_table(receivers_m, jnp.bfloat16),
                    grad_mol,
                    preferred_element_type=jnp.float32,
                )
                * live_m[:, None]
            ).astype(jnp.bfloat16)
            matrix_grad = (
                (
                    edge_grad.astype(jnp.float32)[:, :, None]
                    * gathered.astype(jnp.float32)[:, None, :]
                )
                .astype(jnp.bfloat16)
                .reshape(MOL_EDGES, rows_out * HID)
            )
            out_total = out_total + lax.dot_general(
                hidden, matrix_grad, first_dims(), preferred_element_type=jnp.float32
            )
            hidden_grad = lax.dot_general(
                matrix_grad, w_out, (((1,), (1,)), ((), ())), preferred_element_type=jnp.float32
            )
            preact_grad = (hidden_grad * silu_slope(preact)).astype(jnp.bfloat16)
            in_total = in_total + jnp.dot(
                features_m, preact_grad, preferred_element_type=jnp.float32
            )
            feature_grad = lax.dot_general(
                w_in, preact_grad, (((1,), (1,)), ((), ())), preferred_element_type=jnp.float32
            )
            gathered_grad = jnp.einsum(
                "erk,er->ek",
                matrices.reshape(MOL_EDGES, rows_out, HID),
                edge_grad,
                preferred_element_type=jnp.float32,
            )
            sender_grad = lax.dot_general(
                atom_table(senders_m, jnp.float32), gathered_grad, first_dims(), precision=highest
            )
            return ((out_total, in_total), (feature_grad, sender_grad))

        start_sums = (
            jnp.zeros((HID, rows_out * HID), jnp.float32),
            jnp.zeros((EFEAT, HID), jnp.float32),
        )
        (out_total, in_total), (feature_grads, sender_grads) = lax.scan(
            backward_one,
            start_sums,
            (features, senders, receivers, edge_live, per_states, per_grads),
        )
        state_back = lax.psum_scatter(
            (state_part + sender_grads.reshape(atoms_mb, HID)).astype(jnp.bfloat16),
            "mp",
            scatter_dimension=1,
            tiled=True,
        ).astype(jnp.float32)
        state_parts.append(state_back + cotangent * update)
        feature_parts.append(feature_grads.transpose(1, 0, 2).reshape(EFEAT, edges_mb))
        gradients = (in_total, out_total, grad_gru)
        shard_sums = jax.tree.map(
            jnp.add,
            shard_sums,
            (
                lax.psum_scatter(gradients[0], "dp", scatter_dimension=1, tiled=True),
                lax.psum_scatter(gradients[1], "dp", scatter_dimension=0, tiled=True),
                lax.psum_scatter(gradients[2], "dp", scatter_dimension=2, tiled=True),
            ),
        )
    grad_in, grad_edges = (
        lax.psum(shard_sums[0].astype(jnp.bfloat16), "mp").astype(jnp.float32),
        lax.psum(jnp.concatenate(feature_parts, axis=1).astype(jnp.bfloat16), "mp").astype(
            jnp.float32
        ),
    )
    in_first, in_second, in_new, in_low = adam_update(edge_in, grad_in, edge_in_m1, edge_in_m2)
    out_first, out_second, out_new, out_low = adam_update(
        edge_out, shard_sums[1], edge_out_m1, edge_out_m2
    )
    gru_first, gru_second, gru_new, gru_low = adam_update(gru_weight, shard_sums[2], gru_m1, gru_m2)
    out_state = jnp.concatenate(out_parts, axis=0)
    grad_state = jnp.concatenate(state_parts, axis=0)
    return (
        out_state,
        grad_state,
        grad_edges,
        in_first,
        in_second,
        in_new,
        in_low,
        out_first,
        out_second,
        out_new,
        out_low,
        gru_first,
        gru_second,
        gru_new,
        gru_low,
    )


def solution(mesh):
    placed = (
        P("dp", "mp"),
        P(None, "dp"),
        P("dp"),
        P("dp"),
        P("dp"),
        P("dp"),
        P("dp", "mp"),
        P(None, "dp"),
        P("dp", "mp"),
        P(None, None, "dp", "mp"),
        P(None, "dp"),
        P(None, "dp"),
        P("dp", "mp"),
        P("dp", "mp"),
        P(None, None, "dp", "mp"),
        P(None, None, "dp", "mp"),
    )
    return jax.shard_map(
        body,
        mesh=mesh,
        in_specs=placed,
        out_specs=(
            P("dp", "mp"),
            P("dp", "mp"),
            P(None, "dp"),
            P(None, "dp"),
            P(None, "dp"),
            P(None, "dp"),
            P(None, "dp"),
            P("dp", "mp"),
            P("dp", "mp"),
            P("dp", "mp"),
            P("dp", "mp"),
            P(None, None, "dp", "mp"),
            P(None, None, "dp", "mp"),
            P(None, None, "dp", "mp"),
            P(None, None, "dp", "mp"),
        ),
        check_vma=False,
    )
```

profile of v0, /device:TPU:0, one launch (start us, length us, event | category | flops | bytes accessed | tf_op | source)
XLA Modules:
  0.0 1769.1 jit_solution(2706276727443297511)
XLA Ops:
  9.0 15.7 all_gather.29
  25.7 9.1 all_gather.27
  40.4 9.3 all_gather.31
  54.9 126.3 %while.81 = (s32[]{:T(128)}, bf16[8,29,32]{2,1,0:T(8,128)(2,1)S(1)}, s32[8,812]{1,0:T(8,128)S(1)}, bf16[8,16,812]{2,1,0:T(8,128)(2,1)S(1)}, bf16[16,128]{1,0:T(8...) while((s32[]{:T(128)}, ...), condition=%wide.region_1.2_spmd, body=%wide.region_0.1_spmd.sunk | while | flops 880514944 | bytes 28747416 | solution.py:132
  181.3 13.3 all_gather.30
  194.7 126.3 %while.83 = (s32[]{:T(128)}, bf16[8,29,32]{2,1,0:T(8,128)(2,1)S(1)}, s32[8,812]{1,0:T(8,128)S(1)}, bf16[8,16,812]{2,1,0:T(8,128)(2,1)S(1)}, bf16[16,128]{1,0:T(8...) while((s32[]{:T(128)}, ...), condition=%wide.region_5.6_spmd, body=%wide.region_4.5_spmd.sunk | while | flops 880514944 | bytes 28747416 | solution.py:132
  321.2 13.3 all_gather.33
  334.8 143.9 %while.82 = (s32[]{:T(128)}, bf16[8,29,32]{2,1,0:T(8,128)(2,1)S(1)}, s32[8,812]{1,0:T(8,128)}, bf16[8,16,812]{2,1,0:T(8,128)(2,1)S(1)}, bf16[16,128]{1,0:T(8,128...) while((s32[]{:T(128)}, ...), condition=%wide.region_3.4_spmd, body=%wide.region_2.3_spmd.sunk | while | flops 880514944 | bytes 28747076 | solution.py:132
  478.8 13.1 all_gather.32
  498.3 15.3 reduce-scatter.15.cloned.1.call-done
  516.7 337.9 %while.85 = (s32[]{:T(128)}, f32[128,4096]{1,0:T(8,128)}, f32[16,128]{1,0:T(8,128)S(1)}, bf16[8,16,812]{2,1,0:T(8,128)(2,1)}, f32[8,29,128]{2,1,0:T(8,128)}, /*i...) while((s32[]{:T(128)}, f32[128,4096]{1,0:T(8,128)}, ...), condition=%wide.region_12.13_spmd.clone, body=%wide.region_11.12_spmd.clone.sunk | while | flops 2628001792 | bytes 112396880 | solution.py:226
  521.3 6.6 multiply_convert_fusion.35
  529.0 9.5 copy.274
  563.0 6.6 multiply_convert_fusion.35
  570.7 9.5 copy.274
  605.3 6.6 multiply_convert_fusion.35
  613.0 9.5 copy.274
  647.5 6.6 multiply_convert_fusion.35
  655.3 9.5 copy.274
  689.8 6.6 multiply_convert_fusion.35
  697.6 9.5 copy.274
  732.1 6.6 multiply_convert_fusion.35
  739.8 9.5 copy.274
  774.3 6.6 multiply_convert_fusion.35
  782.1 9.5 copy.274
  816.6 6.6 multiply_convert_fusion.35
  824.3 9.5 copy.274
  857.6 373.6 %while.86 = (s32[]{:T(128)}, f32[128,4096]{1,0:T(8,128)}, f32[16,128]{1,0:T(8,128)}, bf16[8,16,812]{2,1,0:T(8,128)(2,1)}, f32[8,29,128]{2,1,0:T(8,128)}, /*index...) while((s32[]{:T(128)}, f32[128,4096]{1,0:T(8,128)}, ...), condition=%wide.region_16.17_spmd.clone, body=%wide.region_15.16_spmd.clone.sunk | while | flops 2628001792 | bytes 110799952 | solution.py:226
  874.5 6.6 multiply_convert_fusion.38
  882.3 9.5 copy.279
  917.5 6.6 multiply_convert_fusion.38
  925.2 9.5 copy.279
  961.1 6.6 multiply_convert_fusion.38
  968.8 9.5 copy.279
  1004.7 6.6 multiply_convert_fusion.38
  1012.4 9.5 copy.279
  1048.2 6.6 multiply_convert_fusion.38
  1056.0 9.5 copy.279
  1091.8 6.6 multiply_convert_fusion.38
  1099.6 9.5 copy.279
  1135.4 6.6 multiply_convert_fusion.38
  1143.2 9.5 copy.279
  1179.0 6.6 multiply_convert_fusion.38
  1186.7 9.5 copy.279
  1234.2 344.0 %while.84 = (s32[]{:T(128)}, f32[128,4096]{1,0:T(8,128)}, f32[16,128]{1,0:T(8,128)S(1)}, bf16[8,16,812]{2,1,0:T(8,128)(2,1)}, f32[8,29,128]{2,1,0:T(8,128)}, /*i...) while((s32[]{:T(128)}, f32[128,4096]{1,0:T(8,128)}, ...), condition=%wide.region_8.9_spmd.clone, body=%wide.region_7.8_spmd.clone.sunk | while | flops 2628001792 | bytes 110734352 | solution.py:226
  1238.4 6.6 multiply_convert_fusion.32
  1246.1 9.5 copy.269
  1280.8 6.6 multiply_convert_fusion.32
  1288.6 9.5 copy.269
  1323.9 6.6 multiply_convert_fusion.32
  1331.6 9.5 copy.269
  1366.9 6.6 multiply_convert_fusion.32
  1374.7 9.5 copy.269
  1417.7 9.5 copy.269
  1460.8 9.5 copy.269
  1503.8 9.5 copy.269
  1546.9 9.5 copy.269
  1600.7 11.6 reduce-scatter.25.cloned.1.call-done
  1613.1 11.7 psum.15
  1625.4 8.8 reduce-scatter.17.cloned.1.call-done
  1634.2 20.1 %reduce-scatter.21.cloned.1.call-done = bf16[232,32]{0,1:T(8,128)(2,1)} async-done(((bf16[232,128]{0,1:T(8,128)(2,1)}), bf16[232,32]{0,1:T(8,128)(2,1)}) %reduce-scatter.21.cloned.1.call-update) | async-done | bytes 14864 | tf_op jit(solution)/shard_map/reduce_scatter | solution.py:231
  1654.3 20.0 %reduce-scatter.13.cloned.1.call-done = bf16[232,32]{0,1:T(8,128)(2,1)} async-done(((bf16[232,128]{0,1:T(8,128)(2,1)}), bf16[232,32]{0,1:T(8,128)(2,1)}) %reduce-scatter.13.cloned.1.call-update) | async-done | bytes 14864 | tf_op jit(solution)/shard_map/reduce_scatter | solution.py:231
  1676.0 39.8 %all-reduce.4.cloned.1.call-done = bf16[16,19488]{1,0:T(8,128)(2,1)} async-done(((bf16[16,19488]{1,0:T(8,128)(2,1)}), bf16[16,19488]{1,0:T(8,128)(2,1)}) %all-reduce.4.cloned.1.call-update) | async-done | bytes 623632 | tf_op jit(solution)/shard_map/psum | solution.py:251
  1717.9 42.4 %reduce-scatter.23.cloned.1.call-done = f32[16,4096]{1,0:T(8,128)} async-done(((f32[128,4096]{1,0:T(8,128)}), f32[16,4096]{1,0:T(8,128)}) %reduce-scatter.23.cloned.1.call-update) | async-done | bytes 262160 | tf_op jit(solution)/shard_map/reduce_scatter | solution.py:245
  (1127 shorter events, 1121.2 us)
Async XLA Ops:
  7.2 47.0 %copy-start.63 = (s32[696]{0:T(1024)S(1)}, s32[696]{0:T(1024)}, u32[]{:S(2)}) copy-start(s32[696]{0:T(1024)} %param.33) | copy-start | bytes 8356
  7.2 47.6 %all-gather.2.cloned.1.call-start = ((), (), s32[]{:S(2)}) async-start(), calls=%async_computation.8 | async-start | bytes 1179648 | tf_op jit(solution)/shard_map/all_gather | solution.py:91
  8.9 504.7 %reduce-scatter.15.cloned.1.call-start = ((), (), s32[]{:S(2)}) async-start(), calls=%async_computation.11 | async-start | bytes 81920 | tf_op jit(solution)/shard_map/reduce_scatter | solution.py:171
  54.2 438.3 %copy-start.55 = (f32[232]{0:T(256)}, f32[232]{0:T(256)S(1)}, u32[]{:S(2)}) copy-start(f32[232]{0:T(256)S(1)} %get-tuple-element.993) | copy-start | bytes 2788
  54.2 438.3 %copy-start.57 = (f32[232]{0:T(256)}, f32[232]{0:T(256)S(1)}, u32[]{:S(2)}) copy-start(f32[232]{0:T(256)S(1)} %get-tuple-element.994) | copy-start | bytes 2788
  54.2 438.3 %copy-start.59 = (f32[232]{0:T(256)}, f32[232]{0:T(256)S(1)}, u32[]{:S(2)}) copy-start(f32[232]{0:T(256)S(1)} %get-tuple-element.995) | copy-start | bytes 2788
  181.2 13.5 copy-start.10
  181.2 13.5 copy-start.18
  181.2 13.5 copy-start.40
  181.2 13.5 copy-start.42
  181.2 13.5 copy-start.43
  321.0 13.8 copy-start.11
  321.0 13.8 copy-start.19
  321.0 13.8 copy-start.41
  321.0 13.8 copy-start.44
  321.1 13.8 copy-start.45
  334.8 157.4 %copy-start.16 = (f32[696,32]{0,1:T(8,128)S(1)}, f32[696,32]{0,1:T(8,128)}, u32[]{:S(2)}) copy-start(f32[696,32]{0,1:T(8,128)} %param.34) | copy-start | bytes 267268
  334.8 157.8 %copy-start.33 = (bf16[696,32]{0,1:T(8,128)(2,1)S(1)}, bf16[696,32]{0,1:T(8,128)(2,1)}, u32[]{:S(2)}) copy-start(bf16[696,32]{0,1:T(8,128)(2,1)} %param.28) | copy-start | bytes 133636
  492.2 24.4 %copy-start.26 = (f32[232,32]{0,1:T(8,128)}, f32[232,32]{0,1:T(8,128)S(1)}, u32[]{:S(2)}) copy-start(f32[232,32]{0,1:T(8,128)S(1)} %get-tuple-element.936) | copy-start | bytes 89092
  492.2 24.4 %copy-start.28 = (f32[232,32]{0,1:T(8,128)}, f32[232,32]{0,1:T(8,128)S(1)}, u32[]{:S(2)}) copy-start(f32[232,32]{0,1:T(8,128)S(1)} %get-tuple-element.977) | copy-start | bytes 89092
  492.2 24.4 %copy-start.49 = (bf16[1,232,32]{1,2,0:T(8,128)(2,1)}, bf16[1,232,32]{1,2,0:T(8,128)(2,1)S(1)}, u32[]{:S(2)}) copy-start(bf16[1,232,32]{1,2,0:T(8,128)(2,1)S(1)} %get-tuple-element.933) | copy-start | bytes 44548
  492.2 24.3 %copy-start.50 = (bf16[1,232,32]{1,2,0:T(8,128)(2,1)}, bf16[1,232,32]{1,2,0:T(8,128)(2,1)S(1)}, u32[]{:S(2)}) copy-start(bf16[1,232,32]{1,2,0:T(8,128)(2,1)S(1)} %get-tuple-element.974) | copy-start | bytes 44548
  492.3 24.3 %copy-start.35 = (bf16[1,232,32]{1,2,0:T(8,128)(2,1)}, bf16[1,232,32]{1,2,0:T(8,128)(2,1)S(1)}, u32[]{:S(2)}) copy-start(bf16[1,232,32]{1,2,0:T(8,128)(2,1)S(1)} %get-tuple-element.991) | copy-start | bytes 44548
  492.3 24.3 %copy-start.34 = (bf16[1,232,32]{1,2,0:T(8,128)(2,1)}, bf16[1,232,32]{1,2,0:T(8,128)(2,1)S(1)}, u32[]{:S(2)}) copy-start(bf16[1,232,32]{1,2,0:T(8,128)(2,1)S(1)} %get-tuple-element.987) | copy-start | bytes 44548
  492.4 24.2 %copy-start.51 = (bf16[1,232,32]{1,2,0:T(8,128)(2,1)}, bf16[1,232,32]{1,2,0:T(8,128)(2,1)S(1)}, u32[]{:S(2)}) copy-start(bf16[1,232,32]{1,2,0:T(8,128)(2,1)S(1)} %get-tuple-element.937) | copy-start | bytes 44548
  492.4 24.2 %copy-start.24 = (f32[232,32]{0,1:T(8,128)}, f32[232,32]{0,1:T(8,128)S(1)}, u32[]{:S(2)}) copy-start(f32[232,32]{0,1:T(8,128)S(1)} %get-tuple-element.940) | copy-start | bytes 89092
  492.5 24.1 %copy-start.38 = (bf16[1,232,32]{1,2,0:T(8,128)(2,1)}, bf16[1,232,32]{1,2,0:T(8,128)(2,1)S(1)}, u32[]{:S(2)}) copy-start(bf16[1,232,32]{1,2,0:T(8,128)(2,1)S(1)} %get-tuple-element.989) | copy-start | bytes 44548
  493.3 23.4 %copy-start.36 = (bf16[1,232,32]{1,2,0:T(8,128)(2,1)}, bf16[1,232,32]{1,2,0:T(8,128)(2,1)S(1)}, u32[]{:S(2)}) copy-start(bf16[1,232,32]{1,2,0:T(8,128)(2,1)S(1)} %get-tuple-element.965) | copy-start | bytes 44548
  493.3 23.4 %copy-start.39 = (bf16[1,232,32]{1,2,0:T(8,128)(2,1)}, bf16[1,232,32]{1,2,0:T(8,128)(2,1)S(1)}, u32[]{:S(2)}) copy-start(bf16[1,232,32]{1,2,0:T(8,128)(2,1)S(1)} %get-tuple-element.967) | copy-start | bytes 44548
  494.2 360.4 %reduce-scatter.19.cloned.1.call-start = ((), (), s32[]{:S(2)}) async-start(), calls=%async_computation.13 | async-start | bytes 81920 | tf_op jit(solution)/shard_map/reduce_scatter | solution.py:171
  496.5 734.7 %reduce-scatter.11.cloned.1.call-start = ((), (), s32[]{:S(2)}) async-start(), calls=%async_computation.9 | async-start | bytes 81920 | tf_op jit(solution)/shard_map/reduce_scatter | solution.py:171
  497.1 1102.1 %all-reduce.6.cloned.1.call-start = ((), (), s32[]{:S(2)}) async-start(), calls=%async_computation.18 | async-start | bytes 786432
  498.3 1114.0 %reduce-scatter.25.cloned.1.call-start = ((), (), s32[]{:S(2)}) async-start(), calls=%async_computation.17 | async-start | bytes 73728
  517.0 21.5 %copy-start.12 = (bf16[8,16,812]{2,1,0:T(8,128)(2,1)}, bf16[8,16,812]{2,1,0:T(8,128)(2,1)S(1)}, u32[]{:S(2)}) copy-start(bf16[8,16,812]{2,1,0:T(8,128)(2,1)S(1)} %get-tuple-element.1645) | copy-start | bytes 623620 | tf_op jit(solution)/shard_map/while
  558.7 21.5 %copy-start.12 = (bf16[8,16,812]{2,1,0:T(8,128)(2,1)}, bf16[8,16,812]{2,1,0:T(8,128)(2,1)S(1)}, u32[]{:S(2)}) copy-start(bf16[8,16,812]{2,1,0:T(8,128)(2,1)S(1)} %get-tuple-element.1645) | copy-start | bytes 623620 | tf_op jit(solution)/shard_map/while
  601.0 21.5 %copy-start.12 = (bf16[8,16,812]{2,1,0:T(8,128)(2,1)}, bf16[8,16,812]{2,1,0:T(8,128)(2,1)S(1)}, u32[]{:S(2)}) copy-start(bf16[8,16,812]{2,1,0:T(8,128)(2,1)S(1)} %get-tuple-element.1645) | copy-start | bytes 623620 | tf_op jit(solution)/shard_map/while
  643.3 21.5 %copy-start.12 = (bf16[8,16,812]{2,1,0:T(8,128)(2,1)}, bf16[8,16,812]{2,1,0:T(8,128)(2,1)S(1)}, u32[]{:S(2)}) copy-start(bf16[8,16,812]{2,1,0:T(8,128)(2,1)S(1)} %get-tuple-element.1645) | copy-start | bytes 623620 | tf_op jit(solution)/shard_map/while
  685.6 21.5 %copy-start.12 = (bf16[8,16,812]{2,1,0:T(8,128)(2,1)}, bf16[8,16,812]{2,1,0:T(8,128)(2,1)S(1)}, u32[]{:S(2)}) copy-start(bf16[8,16,812]{2,1,0:T(8,128)(2,1)S(1)} %get-tuple-element.1645) | copy-start | bytes 623620 | tf_op jit(solution)/shard_map/while
  727.8 21.5 %copy-start.12 = (bf16[8,16,812]{2,1,0:T(8,128)(2,1)}, bf16[8,16,812]{2,1,0:T(8,128)(2,1)S(1)}, u32[]{:S(2)}) copy-start(bf16[8,16,812]{2,1,0:T(8,128)(2,1)S(1)} %get-tuple-element.1645) | copy-start | bytes 623620 | tf_op jit(solution)/shard_map/while
  770.1 21.5 %copy-start.12 = (bf16[8,16,812]{2,1,0:T(8,128)(2,1)}, bf16[8,16,812]{2,1,0:T(8,128)(2,1)S(1)}, u32[]{:S(2)}) copy-start(bf16[8,16,812]{2,1,0:T(8,128)(2,1)S(1)} %get-tuple-element.1645) | copy-start | bytes 623620 | tf_op jit(solution)/shard_map/while
  812.3 21.5 %copy-start.12 = (bf16[8,16,812]{2,1,0:T(8,128)(2,1)}, bf16[8,16,812]{2,1,0:T(8,128)(2,1)S(1)}, u32[]{:S(2)}) copy-start(bf16[8,16,812]{2,1,0:T(8,128)(2,1)S(1)} %get-tuple-element.1645) | copy-start | bytes 623620 | tf_op jit(solution)/shard_map/while
  857.6 376.6 %copy-start.20 = (f32[16,128]{1,0:T(8,128)S(1)}, f32[16,128]{1,0:T(8,128)}, u32[]{:S(2)}) copy-start(f32[16,128]{1,0:T(8,128)} %custom-call.1) | copy-start | bytes 24580
  1578.2 15.0 copy-start.6
  1580.8 53.4 %reduce-scatter.17.cloned.1.call-start = ((), (), s32[]{:S(2)}) async-start(), calls=%async_computation.12 | async-start | bytes 81920 | tf_op jit(solution)/shard_map/reduce_scatter | solution.py:231
  1584.6 69.7 %reduce-scatter.21.cloned.1.call-start = ((), (), s32[]{:S(2)}) async-start(), calls=%async_computation.14 | async-start | bytes 81920 | tf_op jit(solution)/shard_map/reduce_scatter | solution.py:231
  1586.3 88.1 %reduce-scatter.13.cloned.1.call-start = ((), (), s32[]{:S(2)}) async-start(), calls=%async_computation.10 | async-start | bytes 81920 | tf_op jit(solution)/shard_map/reduce_scatter | solution.py:231
  1588.0 127.7 %all-reduce.4.cloned.1.call-start = ((), (), s32[]{:S(2)}) async-start(), calls=%async_computation.15 | async-start | bytes 1253376 | tf_op jit(solution)/shard_map/psum | solution.py:251
  1591.5 8.5 copy-start.32
  1591.5 8.5 copy-start.52
  1591.5 8.5 copy-start.53
  1591.5 33.2 %copy-start.54 = (f32[16,16]{1,0:T(8,128)S(1)}, f32[16,16]{1,0:T(8,128)}, u32[]{:S(2)}) copy-start(f32[16,16]{1,0:T(8,128)} %param.35) | copy-start | bytes 3076
  1591.5 33.2 %copy-start.61 = (f32[16,16]{1,0:T(8,128)S(1)}, f32[16,16]{1,0:T(8,128)}, u32[]{:S(2)}) copy-start(f32[16,16]{1,0:T(8,128)} %param.39) | copy-start | bytes 3076
  1591.5 33.2 %copy-start.62 = (f32[16,16]{1,0:T(8,128)S(1)}, f32[16,16]{1,0:T(8,128)}, u32[]{:S(2)}) copy-start(f32[16,16]{1,0:T(8,128)} %param.38) | copy-start | bytes 3076
  1591.8 82.6 %copy-start.17 = (f32[696,32]{0,1:T(8,128)S(1)}, f32[696,32]{0,1:T(8,128)}, u32[]{:S(2)}) copy-start(f32[696,32]{0,1:T(8,128)} %param.34) | copy-start | bytes 267268
  1591.8 82.6 %copy-start.25 = (f32[232,32]{0,1:T(8,128)S(1)}, f32[232,32]{0,1:T(8,128)}, u32[]{:S(2)}) copy-start(f32[232,32]{0,1:T(8,128)} %copy-done.24) | copy-start | bytes 89092
  1591.8 82.5 %copy-start.27 = (f32[232,32]{0,1:T(8,128)S(1)}, f32[232,32]{0,1:T(8,128)}, u32[]{:S(2)}) copy-start(f32[232,32]{0,1:T(8,128)} %copy-done.26) | copy-start | bytes 89092
  1591.8 82.5 %copy-start.29 = (f32[232,32]{0,1:T(8,128)S(1)}, f32[232,32]{0,1:T(8,128)}, u32[]{:S(2)}) copy-start(f32[232,32]{0,1:T(8,128)} %copy-done.28) | copy-start | bytes 89092
  1591.8 82.5 %copy-start.56 = (f32[232]{0:T(256)S(1)}, f32[232]{0:T(256)}, u32[]{:S(2)}) copy-start(f32[232]{0:T(256)} %copy-done.55) | copy-start | bytes 2788
  1591.8 82.5 %copy-start.58 = (f32[232]{0:T(256)S(1)}, f32[232]{0:T(256)}, u32[]{:S(2)}) copy-start(f32[232]{0:T(256)} %copy-done.57) | copy-start | bytes 2788
  1591.8 82.5 %copy-start.60 = (f32[232]{0:T(256)S(1)}, f32[232]{0:T(256)}, u32[]{:S(2)}) copy-start(f32[232]{0:T(256)} %copy-done.59) | copy-start | bytes 2788
  1593.1 167.3 %reduce-scatter.23.cloned.1.call-start = ((), (), s32[]{:S(2)}) async-start(), calls=%async_computation.16 | async-start | bytes 2359296 | tf_op jit(solution)/shard_map/reduce_scatter | solution.py:245
  1593.1 167.2 %copy-start.15 = (f32[16,4096]{1,0:T(8,128)S(1)}, f32[16,4096]{1,0:T(8,128)}, u32[]{:S(2)}) copy-start(f32[16,4096]{1,0:T(8,128)} %param.36) | copy-start | bytes 786436
  1593.1 167.2 %copy-start.30 = (f32[16,4096]{1,0:T(8,128)S(1)}, f32[16,4096]{1,0:T(8,128)}, u32[]{:S(2)}) copy-start(f32[16,4096]{1,0:T(8,128)} %param.41) | copy-start | bytes 786436
  1593.1 167.2 %copy-start.31 = (f32[16,4096]{1,0:T(8,128)S(1)}, f32[16,4096]{1,0:T(8,128)}, u32[]{:S(2)}) copy-start(f32[16,4096]{1,0:T(8,128)} %param.40) | copy-start | bytes 786436
  (151 other events, 761.9 us)
Sparse Core Ops, SparseCore 0:
  10.5 26.2 all-gather.1
  494.3 19.2 reduce-scatter.14
  516.5 17.1 reduce-scatter.18
  535.9 17.1 reduce-scatter.10
  556.3 52.2 all-reduce.5
  1580.9 31.3 reduce-scatter.24
  1615.1 19.0 reduce-scatter.16
  1637.1 17.1 reduce-scatter.20
  1657.1 17.1 reduce-scatter.12
  1677.2 38.4 all-reduce.3
  1719.3 40.9 reduce-scatter.22
where the time goes:
time: 1790 us; the launch traced here: 1770 us
  matrix products  741 us (41%)
  local copies, waits for them, and re-layouts  564 us (32%)
  other arithmetic  174 us (10%)
  waiting for transfers between devices  158 us (9%)
  blocking collectives  85.4 us (5%)
  loops' own time  29.5 us (2%)
    while x400, local copies, waits for them, and re-layouts  445 us
    dot_general x48, matrix products, edge_network(): jnp.dot(hidden, w_out, preferred_element_type=jnp.float32)  215 us
    convert_element_type x24, other arithmetic, backward_one(): matrix_grad = (edge_grad.astype(jnp.float32)[:, :, None] * gathered.astyp...  158 us
    dot_general x24, matrix products, backward_one(): lax.dot_general(hidden, matrix_grad, first_dims(), preferred_element_type...  154 us
    dot_general x24, matrix products, forward_one(): jnp.einsum('erk,ek->er', matrices.reshape(MOL_EDGES, rows_out, HID), gath...  84.7 us
    dynamic_slice x96, local copies, waits for them, and re-layouts, body(): lax.scan(forward_one, 0, (features, senders, receivers, edge_live, per_st...  51.3 us
    reduce_scatter x3, waiting for transfers between devices, body(): lax.psum_scatter((state_part + sender_grads.reshape(atoms_mb, HID)).astyp...  48.9 us
    dot_general x24, matrix products, backward_one(): lax.dot_general(matrix_grad, w_out, (((1,), (1,)), ((), ())), preferred_e...  45.6 us
  transfers between devices with their start and end apart: 11, of which 7 were waited for; matrix products, arithmetic and copies ran while one was open for 60% of the time, Pallas kernels for 0%

commit v1 on v0

v1 whole, which is shorter than its diff:
```python
import functools

import jax
import jax.numpy as jnp
from jax import lax
from jax.experimental import pallas as pl
from jax.experimental.pallas import tpu as pltpu
from jax.sharding import PartitionSpec as P

HID = 128
EFEAT = 16
MA = 29
ME = 812
PADA = 32
STEP = 5
DXC = 4
MESH = pl.DeviceIdType.MESH
VMEM_LIMIT = 60 << 20
bf = jnp.bfloat16
f32 = jnp.float32
NT = (((1,), (1,)), ((), ()))
TN = (((0,), (0,)), ((), ()))
NN = (((1,), (0,)), ((), ()))

def dot(a,b,dn): return lax.dot_general(a,b,dn,preferred_element_type=f32)

def lane_take(x, src, dst):
    sh=(dst-src)%128
    y=pltpu.roll(x,sh,1) if sh else x
    return y

def compute_kernel(nm, ndp, nmp, hl, wr, il,
        feat_ref, key_ref, xs_ref, wall_ref,
        grads_ref, outs_ref, ge_ref,
        featp, kron, emat, hid, slope, bmat, cmat, dpre, gin, gacc, gfull, wgs, geacc):
    gr=wr; wi=wr+32
    bases=[(ME*i//128)*128 for i in range(nm)]
    lanes128=lax.broadcasted_iota(jnp.int32,(1,128),1)
    w_in=jnp.zeros((EFEAT,HID),f32)
    for d in range(ndp):
        w_in=w_in+wall_ref[d,0,wi:wi+16,:].astype(f32)
    w_in=w_in.astype(bf)
    delta=(lax.broadcasted_iota(jnp.int32,(PADA,256),0)==lax.broadcasted_iota(jnp.int32,(PADA,256),1)%32)
    @pl.loop(0,16)
    def _(c):
        e=jnp.where(lax.broadcasted_iota(jnp.int32,(HID,256),0)==c*8+lax.broadcasted_iota(jnp.int32,(HID,256),1)//32,1.0,0.0).astype(bf)
        emat[c]=e
        wexp=dot(w_in,e,NN)
        for f in range(EFEAT):
            kron[c,f*32:(f+1)*32,:]=jnp.where(delta,wexp[f:f+1,:],0.0).astype(bf)
    wio=lax.broadcasted_iota(jnp.int32,(PADA,1024),0)
    for m in range(nm):
        b=bases[m]
        sk=key_ref[0:1,b:b+1024]; rk=key_ref[1:2,b:b+1024]
        st=(wio+32*m)==sk
        rt=jnp.where(wio==rk,1.0,0.0).astype(bf)
        ff=feat_ref[:,b:b+1024].astype(f32)
        for q in range(4):
            z=jnp.concatenate([jnp.where(st,ff[f:f+1,:],0.0).astype(bf) for f in range(4*q,4*q+4)],axis=0)
            featp[m*32:(m+1)*32,q*128:(q+1)*128]=dot(rt,z,NT).astype(bf)
    fp=featp[...]
    @pl.loop(0,16)
    def _(c):
        p=dot(fp,kron[c],NN)
        s=0.5+0.5*jnp.tanh(0.5*p)
        h=p*s
        hid[c]=h.astype(bf)
        slope[c]=(s+h-h*s).astype(bf)
    lane=lanes128
    xf=jnp.zeros((nm*32,HID),f32); cf=jnp.zeros((nm*32,HID),f32)
    for j in range(nmp):
        sl=xs_ref[j].astype(f32)
        here=(lane>=32*j)&(lane<32*j+32)
        xf=jnp.where(here,lane_take(sl,0,32*j),xf)
        cf=jnp.where(here,lane_take(sl,32,32*j),cf)
    x=xf.astype(bf)
    @pl.loop(0,ndp)
    def _(d):
        for q in range(hl//2):
            w=jnp.concatenate([wall_ref[d,j,(2*q+t)*32:(2*q+t+1)*32,:] for t in range(2) for j in range(nmp)],axis=0)
            o=dot(x,w,NT).astype(bf)
            bmat[d*hl+2*q]=o[:,:128]
            bmat[d*hl+2*q+1]=o[:,128:]
    sums=[]
    for m in range(nm):
        hm=jnp.concatenate([hid[c,m*32:(m+1)*32,:] for c in range(16)],axis=1)
        sums.append(dot(hm,bmat[:,m*32:(m+1)*32,:].reshape(4096,128),NN))
    summed=jnp.concatenate(sums,axis=0).astype(bf)
    for s in range(2):
        for j in range(nmp):
            for d in range(ndp):
                wgs[s,j,d*il:(d+1)*il,:]=wall_ref[d,j,gr+16*s:gr+16*s+16,:].astype(f32)[:il]
    wg=[[wgs[s,j].astype(bf) for j in range(nmp)] for s in range(2)]
    def gates(a,s):
        outs=[dot(a,wg[s][j],NN) for j in range(nmp)]
        res=[]
        for g in range(3):
            t=None
            for j in range(nmp):
                y=lane_take(outs[j],32*g,32*j)
                here=(lane>=32*j)&(lane<32*j+32)
                t=y if t is None else jnp.where(here,y,t)
            res.append(t)
        return res
    gi=gates(summed,0); gs=gates(x,1)
    def sig(v): return 0.5+0.5*jnp.tanh(0.5*v)
    reset=sig(gi[0]+gs[0]); update=sig(gi[1]+gs[1]); cand=jnp.tanh(gi[2]+reset*gs[2])
    ostate=(1.0-update)*cand+update*xf
    dc=cf*(1.0-update)*(1.0-cand*cand)
    du=cf*(xf-cand)*update*(1.0-update)
    dr=dc*gs[2]*reset*(1.0-reset)
    def pack(gl,j):
        t=jnp.zeros((nm*32,HID),f32)
        for g in range(3):
            here=(lane>=32*g)&(lane<32*g+32)
            t=jnp.where(here,lane_take(gl[g],32*j,32*g),t)
        return t.astype(bf)
    al=[];bl=[]
    for j in range(nmp):
        a=pack([dr,du,dc],j); b=pack([dr,du,dc*reset],j)
        al.append(a);bl.append(b)
        for s,(l,r) in enumerate(((summed,a),(x,b))):
            gg=dot(l,r,TN)
            for d in range(ndp):
                part=gg[d*il:(d+1)*il]
                if il<16:
                    part=jnp.concatenate([part,jnp.zeros((16-il,128),f32)],axis=0)
                grads_ref[d,j,gr+16*s:gr+16*s+16,:]=part.astype(bf)
    dsum=dot(jnp.concatenate(al,axis=1),jnp.concatenate(wg[0],axis=1),NT)
    gfull[:,128:256]=cf*update
    gfull[:,0:128]=dot(jnp.concatenate(bl,axis=1),jnp.concatenate(wg[1],axis=1),NT)
    ds=dsum.astype(bf)
    zero=jnp.zeros((32,128),bf)
    for p in range(nm//2):
        blk=jnp.concatenate([jnp.concatenate([ds[p*64:p*64+32],zero],axis=1),jnp.concatenate([zero,ds[p*64+32:p*64+64]],axis=1)],axis=0)
        @pl.loop(0,16)
        def _(c):
            o=dot(hid[c,p*64:(p+1)*64,:],blk,TN).astype(bf)
            cmat[pl.ds(c*8,8),p*64:p*64+32,:]=o[:,:128].reshape(8,32,128)
            cmat[pl.ds(c*8,8),p*64+32:p*64+64,:]=o[:,128:].reshape(8,32,128)
    @pl.loop(0,ndp)
    def _(d):
        for q in range(hl):
            o=dot(cmat[d*hl+q],x,TN).astype(bf)
            for j in range(nmp):
                grads_ref[d,j,q*32:(q+1)*32,:]=o[32*j:32*j+32]
    gacc[...]=jnp.zeros(gacc.shape,f32)
    @pl.loop(0,ndp)
    def _(d):
        for q4 in range(hl//min(DXC,hl)):
            qs=range(q4*min(DXC,hl),(q4+1)*min(DXC,hl))
            cc=jnp.concatenate([cmat[d*hl+q] for q in qs],axis=1)
            w=jnp.concatenate([wall_ref[d,j,q*32:(q+1)*32,:] for q in qs for j in range(nmp)],axis=0)
            gacc[...]+=dot(cc,w,NN)
    gfin=gacc[...]+gfull[:,0:128]+gfull[:,128:256]
    for j in range(nmp):
        a=lane_take(ostate,32*j,0); b=lane_take(gfin,32*j,32)
        outs_ref[j]=jnp.where(lane<32,a,b).astype(bf)
    for m in range(nm):
        dm=ds[m*32:(m+1)*32]
        for c in range(16):
            o=dot(dm,bmat[c*8:(c+1)*8,m*32:(m+1)*32,:].reshape(256,128),NT)
            dpre[c,m*32:(m+1)*32,:]=(o*slope[c,m*32:(m+1)*32,:].astype(f32)).astype(bf)
    gfull[...]=jnp.zeros(gfull.shape,f32)
    gin[...]=jnp.zeros(gin.shape,f32)
    @pl.loop(0,16)
    def _(c):
        dp_=dpre[c]
        gfull[...]+=dot(dp_,kron[c],NT)
        full=dot(fp,dp_,TN)
        full=jnp.where(delta[None],full.reshape(16,32,256),0.0).sum(axis=1)
        gin[...]+=dot(full.astype(bf),emat[c],NT)
    gin_bf=gin[...].astype(bf)
    for d in range(ndp):
        for j in range(nmp):
            grads_ref[d,j,wi:wi+16,:]=gin_bf
    gb=gfull[...].astype(bf)
    geacc[...]=jnp.zeros(geacc.shape,f32)
    for m in range(nm):
        b=bases[m]
        sk=key_ref[0:1,b:b+1024]; rk=key_ref[1:2,b:b+1024]
        for n in range(4):
            lo=b+n*256
            w2=wio[:,:256]
            st=(w2+32*m)==key_ref[0:1,lo:lo+256]
            rt=jnp.where(w2==key_ref[1:2,lo:lo+256],1.0,0.0).astype(bf)
            u=dot(gb[m*32:(m+1)*32],rt,TN).reshape(16,32,256)
            geacc[:,lo:lo+256]+=jnp.where(st[None],u,0.0).sum(axis=1)
    ge_ref[...]=geacc[...].astype(bf)

def compute(feat,key,xs,wall,nm,ndp,nmp,hl,wr,il):
    rb=wall.shape[2]; win=feat.shape[1]
    return pl.pallas_call(functools.partial(compute_kernel,nm,ndp,nmp,hl,wr,il),
        out_shape=(jax.ShapeDtypeStruct((ndp,nmp,rb,128),bf),jax.ShapeDtypeStruct((nmp,nm*32,128),bf),jax.ShapeDtypeStruct((16,win),bf)),
        in_specs=[pl.BlockSpec(memory_space=pltpu.VMEM)]*4,
        out_specs=(pl.BlockSpec(memory_space=pltpu.VMEM),)*3,
        scratch_shapes=[pltpu.VMEM((nm*32,512),bf),pltpu.VMEM((16,512,256),bf),pltpu.VMEM((16,128,256),bf),
            pltpu.VMEM((16,nm*32,256),bf),pltpu.VMEM((16,nm*32,256),bf),
            pltpu.VMEM((128,nm*32,128),bf),pltpu.VMEM((128,nm*32,128),bf),pltpu.VMEM((16,nm*32,256),bf),
            pltpu.VMEM((16,128),f32),pltpu.VMEM((nm*32,128),f32),pltpu.VMEM((nm*32,512),f32),pltpu.VMEM((2,nmp,128,128),f32),pltpu.VMEM((16,win),f32)],
        compiler_params=pltpu.CompilerParams(vmem_limit_bytes=60<<20))(feat,key,xs,wall)

def places(ndp, nmp):
    d = lax.axis_index("dp")
    m = lax.axis_index("mp")
    half = ndp // 2
    u = d // 2
    c = d % 2
    zp = [(d, (m + i) % nmp) for i in range(1, nmp)]
    pp = [(2 * ((u + t) % half) + c, m) for t in range(1, half)]
    cp = (2 * u + (1 - c), m)
    return d, m, u, c, half, zp, pp, cp


def greet(plist):
    bar = pltpu.get_barrier_semaphore()
    for p in plist:
        pl.semaphore_signal(bar, inc=1, device_id=p, device_id_type=MESH)
    pl.semaphore_wait(bar, len(plist))


def rcopy(src, dst, ssem, rsem, dev):
    return pltpu.make_async_remote_copy(
        src_ref=src, dst_ref=dst, send_sem=ssem, recv_sem=rsem, device_id=dev, device_id_type=MESH
    )


def gather_kernel(ndp, nmp, blk_ref, xs_ref, wall_ref, xo_ref, zsem, psem, csem, rsem, xssem, xrsem, lsem):
    d, m, u, c, half, zp, pp, cp = places(ndp, nmp)
    greet(zp + pp + [cp])
    local = [
        pltpu.make_async_copy(blk_ref, wall_ref.at[d, m], lsem.at[0]),
        pltpu.make_async_copy(xs_ref.at[m], xo_ref.at[m], lsem.at[1]),
    ]
    sends = []
    for i, p in enumerate(zp):
        sends.append(rcopy(xs_ref.at[p[1]], xo_ref.at[m], xssem.at[i], xrsem.at[m], p))
        sends.append(rcopy(blk_ref, wall_ref.at[d, m], zsem.at[i], rsem.at[d, m], p))
    for x in sends + local:
        x.start()

    def push(n, row, col, plane):
        src = wall_ref.at[row, col]
        out = []
        if plane:
            for t, p in enumerate(pp):
                out.append(rcopy(src, src, psem.at[n, t], rsem.at[row, col], p))
        out.append(rcopy(src, src, csem.at[n if plane else nmp + n], rsem.at[row, col], cp))
        for x in out:
            x.start()
        sends.extend(out)

    def arrived(row, col):
        here = wall_ref.at[row, col]
        rcopy(here, here, zsem.at[0], rsem.at[row, col], cp).wait_recv()

    local[0].wait()
    push(0, d, m, True)
    for i in range(1, nmp):
        col = (m - i + nmp) % nmp
        arrived(d, col)
        push(i, d, col, True)
    n = 0
    for i in range(nmp):
        col = (m - i + nmp) % nmp
        for t in range(1, half):
            row = 2 * ((u - t + half) % half) + c
            arrived(row, col)
            push(n, row, col, False)
            n += 1
    for i in range(nmp):
        for t in range(half):
            arrived(2 * ((u - t + half) % half) + (1 - c), (m - i + nmp) % nmp)
    for i in range(1, nmp):
        col = (m - i + nmp) % nmp
        here = xo_ref.at[col]
        rcopy(here, here, xssem.at[0], xrsem.at[col], cp).wait_recv()
    local[1].wait()
    for x in sends:
        x.wait_send()


def gather(blk, xs, ndp, nmp):
    rb = blk.shape[0]
    half = ndp // 2
    dma = pltpu.SemaphoreType.DMA
    return pl.pallas_call(
        functools.partial(gather_kernel, ndp, nmp),
        out_shape=(
            jax.ShapeDtypeStruct((ndp, nmp, rb, 128), bf),
            jax.ShapeDtypeStruct(xs.shape, bf),
        ),
        in_specs=[pl.BlockSpec(memory_space=pltpu.VMEM)] * 2,
        out_specs=(pl.BlockSpec(memory_space=pltpu.VMEM),) * 2,
        scratch_shapes=[
            dma((nmp - 1,)),
            dma((nmp, half - 1)),
            dma((nmp + nmp * (half - 1),)),
            dma((ndp, nmp)),
            dma((nmp - 1,)),
            dma((nmp,)),
            dma((2,)),
        ],
        compiler_params=pltpu.CompilerParams(
            collective_id=0, has_side_effects=True, vmem_limit_bytes=VMEM_LIMIT
        ),
    )(blk, xs)


def scatter_kernel(
    ndp, nmp,
    g_ref, ge_ref, os_ref,
    fin_ref, geo_ref, oso_ref,
    rc, sb, rp, zs, rz,
    cs, cr, ps, pr, zsem, zr, os_s, os_r, ge_s, ge_r, lsem,
):
    d, m, u, c, half, zp, pp, cp = places(ndp, nmp)
    greet(zp + pp + [cp])
    local = [
        pltpu.make_async_copy(ge_ref, geo_ref.at[m], lsem.at[0]),
        pltpu.make_async_copy(os_ref.at[m], oso_ref.at[m], lsem.at[1]),
    ]
    sends = []
    order = list(range(1, half)) + [0]
    cols = [(m + i) % nmp for i in range(1, nmp)] + [m]
    for t in order:
        row = 2 * ((u + t) % half) + (1 - c)
        sends.append(rcopy(g_ref.at[row], rc.at[t], cs.at[t], cr.at[t], cp))
    for i, p in enumerate(zp):
        sends.append(rcopy(os_ref.at[p[1]], oso_ref.at[m], os_s.at[i], os_r.at[m], p))
        sends.append(rcopy(ge_ref, geo_ref.at[m], ge_s.at[i], ge_r.at[m], p))
    for x in sends + local:
        x.start()
    for t in order:
        rcopy(rc.at[t], rc.at[t], cs.at[t], cr.at[t], cp).wait_recv()
        if t == 0:
            continue
        row = 2 * ((u + t) % half) + c
        for i, col in enumerate(cols):
            sb[t - 1, i] = (g_ref[row, col].astype(f32) + rc[t, col].astype(f32)).astype(bf)
            x = rcopy(sb.at[t - 1, i], rp.at[t - 1, col], ps.at[t - 1, i], pr.at[t - 1, col], pp[t - 1])
            x.start()
            sends.append(x)
    for i, col in enumerate(cols):
        q = g_ref[d, col].astype(f32) + rc[0, col].astype(f32)
        for t in range(1, half):
            here = rp.at[t - 1, col]
            rcopy(here, here, ps.at[0, 0], pr.at[t - 1, col], cp).wait_recv()
            q = q + rp[t - 1, col].astype(f32)
        if i < nmp - 1:
            zs[i] = q.astype(bf)
            x = rcopy(zs.at[i], rz.at[m], zsem.at[i], zr.at[m], zp[i])
            x.start()
            sends.append(x)
        else:
            fin_ref[...] = q
    for i in range(1, nmp):
        col = (m - i + nmp) % nmp
        here = rz.at[col]
        rcopy(here, here, zsem.at[0], zr.at[col], cp).wait_recv()
        fin_ref[...] += rz[col].astype(f32)
    for i in range(1, nmp):
        col = (m - i + nmp) % nmp
        rcopy(geo_ref.at[col], geo_ref.at[col], ge_s.at[0], ge_r.at[col], cp).wait_recv()
        rcopy(oso_ref.at[col], oso_ref.at[col], os_s.at[0], os_r.at[col], cp).wait_recv()
    for x in local:
        x.wait()
    for x in sends:
        x.wait_send()


def scatter(grads, ge, os, ndp, nmp):
    rb = grads.shape[2]
    half = ndp // 2
    dma = pltpu.SemaphoreType.DMA
    return pl.pallas_call(
        functools.partial(scatter_kernel, ndp, nmp),
        out_shape=(
            jax.ShapeDtypeStruct((rb, 128), f32),
            jax.ShapeDtypeStruct((nmp,) + ge.shape, bf),
            jax.ShapeDtypeStruct(os.shape, bf),
        ),
        in_specs=[pl.BlockSpec(memory_space=pltpu.VMEM)] * 3,
        out_specs=(pl.BlockSpec(memory_space=pltpu.VMEM),) * 3,
        scratch_shapes=[
            pltpu.VMEM((half, nmp, rb, 128), bf),
            pltpu.VMEM((half - 1, nmp, rb, 128), bf),
            pltpu.VMEM((half - 1, nmp, rb, 128), bf),
            pltpu.VMEM((nmp - 1, rb, 128), bf),
            pltpu.VMEM((nmp, rb, 128), bf),
            dma((half,)), dma((half,)),
            dma((half - 1, nmp)), dma((half - 1, nmp)),
            dma((nmp - 1,)), dma((nmp,)),
            dma((nmp - 1,)), dma((nmp,)),
            dma((nmp - 1,)), dma((nmp,)),
            dma((2,)),
        ],
        compiler_params=pltpu.CompilerParams(
            collective_id=1, has_side_effects=True, vmem_limit_bytes=VMEM_LIMIT
        ),
    )(grads, ge, os)


beta_one = 0.5
beta_two = 0.5
learn_rate = 0.05
decay_rate = 0.01
epsilon = 1e-08


def adam_update(weight, gradient, first_moment, second_moment):
    first_new = beta_one * first_moment + (1.0 - beta_one) * gradient
    second_new = beta_two * second_moment + (1.0 - beta_two) * gradient * gradient
    mean_hat = first_new / (1.0 - beta_one**STEP)
    square_hat = second_new / (1.0 - beta_two**STEP)
    weight_new = weight - learn_rate * (
        mean_hat / (jnp.sqrt(square_hat) + epsilon) + decay_rate * weight
    )
    return (first_new, second_new, weight_new, weight_new.astype(bf))


def body(
    ndp, nmp,
    node_state, edge_feat, sender, receiver, edge_mask, node_mask, out_grad,
    edge_in, edge_out, gru_weight,
    edge_in_m1, edge_in_m2, edge_out_m1, edge_out_m2, gru_m1, gru_m2,
):
    d = lax.axis_index("dp")
    m = lax.axis_index("mp")
    atoms = node_state.shape[0]
    edges = sender.shape[0]
    mols = atoms // MA
    nm = mols // nmp
    uw = node_state.shape[1]
    hl = edge_out.shape[0]
    il = gru_weight.shape[2]
    wr = hl * edge_out.shape[1] // HID
    w_rows = edge_out.astype(bf).reshape(wr, HID)
    g_rows = gru_weight.transpose(0, 2, 1, 3).reshape(2, il, 3 * uw).astype(bf)
    g_rows = jnp.pad(g_rows, ((0, 0), (0, 16 - il), (0, HID - 3 * uw))).reshape(32, HID)
    i_rows = lax.dynamic_update_slice(
        jnp.zeros((EFEAT, HID), bf), edge_in.astype(bf), (0, d * edge_in.shape[1])
    )
    blk = jnp.concatenate([w_rows, g_rows, i_rows], axis=0)
    cot = (out_grad * node_mask.astype(f32)[:, None]).astype(bf)
    xs = jnp.concatenate([node_state, cot], axis=1).reshape(mols, MA, 2 * uw)
    xs = jnp.pad(xs, ((0, 0), (0, PADA - MA), (0, HID - 2 * uw))).reshape(nmp, nm * PADA, HID)
    per = nm * ME
    starts = [per * j // 128 * 128 for j in range(nmp)]
    shift = max(per * j - s for j, s in enumerate(starts))
    win = max(ME * i // 128 * 128 for i in range(nm)) + 1024
    assert all(ME * i + shift + ME <= ME * i // 128 * 128 + 1024 for i in range(nm))
    start = (per * m) // 128 * 128
    total = max(starts[-1] + win, edges)
    mol_id = lax.broadcasted_iota(jnp.int32, (1, edges), 1) // ME
    s_key = jnp.where(edge_mask[None] == 1, sender[None] + PADA * mol_id, -1)
    keys = jnp.concatenate([s_key, receiver[None]], axis=0)
    keys = jnp.pad(keys, ((0, 0), (0, total - edges)), constant_values=-1)
    keys = lax.dynamic_slice(keys, (0, start), (2, win))
    keys = keys - jnp.array([[1], [0]], jnp.int32) * (PADA * nm * m)
    feat = lax.dynamic_slice(jnp.pad(edge_feat, ((0, 0), (0, total - edges))), (0, start), (EFEAT, win))

    wall, xo = gather(blk, xs, ndp, nmp)
    grads, outs, ge = compute(feat, keys, xo, wall, nm, ndp, nmp, hl, wr, il)
    fin, geo, oso = scatter(grads, ge, outs, ndp, nmp)

    oso = oso.reshape(mols, PADA, HID)[:, :MA].reshape(atoms, HID).astype(f32)
    out_state = oso[:, :uw] * node_mask.astype(f32)[:, None]
    grad_state = oso[:, uw : 2 * uw]
    grad_edges = jnp.concatenate(
        [geo[j][:, per * j - starts[j] : per * (j + 1) - starts[j]] for j in range(nmp)], axis=1
    ).astype(f32)
    g_out = fin[:wr].reshape(edge_out.shape)
    g_gru = fin[wr : wr + 32].reshape(2, 16, HID)[:, :il, : 3 * uw].reshape(2, il, 3, uw).transpose(0, 2, 1, 3)
    g_in = lax.dynamic_slice(fin[wr + 32 :], (0, d * edge_in.shape[1]), edge_in.shape)
    return (
        (out_state, grad_state, grad_edges)
        + adam_update(edge_in, g_in, edge_in_m1, edge_in_m2)
        + adam_update(edge_out, g_out, edge_out_m1, edge_out_m2)
        + adam_update(gru_weight, g_gru, gru_m1, gru_m2)
    )


def solution(mesh):
    ndp, nmp = mesh.shape["dp"], mesh.shape["mp"]
    rows, lanes, gru = P("dp", "mp"), P(None, "dp"), P(None, None, "dp", "mp")
    edge = P("dp")
    return jax.shard_map(
        functools.partial(body, ndp, nmp),
        mesh=mesh,
        in_specs=(
            rows, lanes, edge, edge, edge, edge, rows,
            lanes, rows, gru, lanes, lanes, rows, rows, gru, gru,
        ),
        out_specs=(rows, rows, lanes) + (lanes,) * 4 + (rows,) * 4 + (gru,) * 4,
        check_vma=False,
    )
```

time: 1790 us -> 151 us (0.08); the launches traced: 1770 us -> 151 us
  matrix products: 741 us -> 0 us
  local copies, waits for them, and re-layouts: 564 us -> 10.8 us
  other arithmetic: 174 us -> 11.4 us
  waiting for transfers between devices: 158 us -> 0 us
  Pallas kernels: 0 us -> 128 us
  blocking collectives: 85.4 us -> 0 us
  loops' own time: 29.5 us -> 0 us
    dot_general x351 -> x0, matrix products: 741 us -> none  [the longest x48 215 us: edge_network(): jnp.dot(hidden, w_out, preferred_element_type=jnp.float32)]
    while x404 -> x0, local copies, waits for them, and re-layouts: 445 us -> none
    convert_element_type x31 -> x10, other arithmetic: 166 us -> 7.9 us  [the longest x3 2.43 us: adam_update(): return (first_new, second_new, weight_new, weight_new.astype(bf))]
    pallas_call x0 -> x3, Pallas kernels: none -> 128 us  [the longest x1 46.8 us: compute(): pl.pallas_call(functools.partial(compute_kernel, nm, ndp, nmp, hl, wr, il...]
    reduce_scatter x7 -> x0, waiting for transfers between devices: 107 us -> none  [the longest x3 48.9 us: body(): lax.psum_scatter((state_part + sender_grads.reshape(atoms_mb, HID)).astyp...]
    all_gather x6 -> x0, blocking collectives: 73.7 us -> none  [the longest x3 39.7 us: body(): message_full = lax.all_gather(messages, 'mp', axis=1, tiled=True)]
    dynamic_slice x96 -> x1, local copies, waits for them, and re-layouts: 51.3 us -> 1.62 us  [body(): lax.dynamic_slice(jnp.pad(edge_feat, ((0, 0), (0, total - edges))), (0, s...]
    psum x1 -> x0, waiting for transfers between devices: 39.8 us -> none  [body(): lax.psum(jnp.concatenate(feature_parts, axis=1).astype(jnp.bfloat16), 'mp')]
  transfers between devices with their start and end apart: 11 -> 0, of which waited for: 7 -> 0; matrix products, arithmetic and copies ran while one was open for 60% -> 0% of each run, Pallas kernels for 0% -> 0%
where the time goes in v1:
time: 151 us
  Pallas kernels  128 us (85%)
  other arithmetic  11.4 us (8%)
  local copies, waits for them, and re-layouts  10.8 us (7%)
    pallas_call x1, Pallas kernels, compute(): pl.pallas_call(functools.partial(compute_kernel, nm, ndp, nmp, hl, wr, il...  46.8 us
    pallas_call x1, Pallas kernels, scatter(): pl.pallas_call(functools.partial(scatter_kernel, ndp, nmp), out_shape=(ja...  43.4 us
    pallas_call x1, Pallas kernels, gather(): pl.pallas_call(functools.partial(gather_kernel, ndp, nmp), out_shape=(jax...  37.5 us
    unnamed x24, local copies, waits for them, and re-layouts  3.64 us

profile of v1, /device:TPU:0, one launch (start us, length us, event | category | flops | bytes accessed | tf_op | source)
XLA Modules:
  0.0 150.9 jit_solution(419402175990172666)
XLA Ops:
  0.7 0.7 multiply_bitcast_fusion
  1.3 0.7 convert_element_type.51
  2.0 0.7 convert_element_type.50
  2.7 0.1 dynamic_update_slice.3
  2.8 0.8 convert_bitcast_fusion
  3.6 0.1 convert_element_type.49
  3.7 0.9 broadcast_in_dim.6
  4.7 1.0 fusion.3
  5.6 0.1 select_n.30
  5.7 0.1 pad_add_fusion
  5.8 0.7 fusion.6.key_ref
  6.5 1.0 convert_element_type.46
  7.5 0.1 reshape.75
  7.6 0.7 pad_maximum_fusion.1.blk_ref
  8.2 1.6 %pad_dynamic-slice_fusion.feat_ref = bf16[16,4992]{1,0:T(8,128)(2,1)} fusion(s32[]{:T(128)S(6)} %select_n.27, bf16[16,19488]{1,0:T(8,128)(2,1)} %param.18), kind=kLoop, calls=%fused_computation | loop fusion | bytes 783364 | tf_op jit(solution)/shard_map/dynamic_slice | solution.py:461
  9.9 1.0 copy.49
  10.8 1.1 copy.48
  11.9 0.2 multiply_convert_fusion
  12.1 0.1 pad_maximum_fusion
  12.2 0.1 reshape.77
  12.2 0.7 pad.19
  13.0 37.5 %shard_map.280 = (bf16[8,4,560,128]{3,2,1,0:T(8,128)(2,1)}, bf16[4,192,128]{2,1,0:T(8,128)(2,1)}) custom-call(bf16[560,128]{1,0:T(8,128)(2,1)} %pad_maximum_fusion.1.blk_ref, bf16[4,192,128]{2,1,0:T(8,128)(2,1)} %bitcast.23), custom_call_target="tpu_custom_call" | custom-call | tf_op jit(solution)/shard_map/pallas_call | solution.py:287
  50.5 0.0 copy-start.7
  50.5 0.0 copy-start.8
  50.5 0.0 copy-start.9
  50.5 0.0 copy-start.4
  50.5 0.0 copy-start.5
  50.5 0.0 copy-start.6
  50.5 46.8 %shard_map.281 = (bf16[8,4,560,128]{3,2,1,0:T(8,128)(2,1)}, bf16[4,192,128]{2,1,0:T(8,128)(2,1)}, bf16[16,4992]{1,0:T(8,128)(2,1)}) custom-call(bf16[16,4992]{1,0:T(8,128)(2,1)} %pad_dynamic-slice_fusion.feat_ref, s32[2,4992]{1,0:T(2,128)} %fusion.6.key_ref, bf16[4,192,128]{2,1,0:T(8,128)(2,1)} %get-tuple-element.23.xs_ref, ...), custom_call_target="tpu_custom_call" | custom-call | tf_op jit(solution)/shard_map/pallas_call | solution.py:193
  97.4 43.4 %shard_map.282 = (f32[560,128]{1,0:T(8,128)}, bf16[4,16,4992]{2,1,0:T(8,128)(2,1)}, bf16[4,192,128]{2,1,0:T(8,128)(2,1)}) custom-call(bf16[8,4,560,128]{3,2,1,0:T(8,128)(2,1)} %get-tuple-element.25.g_ref, bf16[16,4992]{1,0:T(8,128)(2,1)} %get-tuple-element.26.ge_ref, bf16[4,192,128]{2,1,0:T(8,128)(2,1)} %get-tuple-element.27.os_ref), custom_call_target="tpu_custom_call" | custom-call | tf_op jit(solution)/shard_map/pallas_call | solution.py:376
  140.8 0.0 copy-start.1
  140.8 0.8 slice.56
  141.6 0.7 slice.58
  142.3 1.0 slice.57
  143.3 0.1 reshape.80
  143.3 0.0 copy-done.7
  143.3 0.0 copy-done.8
  143.3 0.0 copy-done.9
  143.4 0.7 fusion.12
  144.1 0.1 reshape.82
  144.2 0.0 copy-done.4
  144.2 0.0 copy-done.5
  144.2 0.0 copy-done.6
  144.2 0.7 fusion.8
  144.9 0.0 copy-start
  144.9 0.0 copy-start.2
  144.9 0.0 copy-start.3
  144.9 1.0 slice_convert_fusion
  145.9 0.2 fusion.14
  146.2 0.8 copy.52
  147.0 0.8 copy.51
  147.8 0.0 copy-done.1
  147.8 0.1 slice.66
  147.9 0.1 slice.65
  148.0 0.1 slice.64
  148.2 0.5 concatenate.15
  148.7 1.1 convert_element_type.55
  149.8 0.0 copy-done
  149.8 0.0 copy-done.2
  149.8 0.0 copy-done.3
  149.8 1.0 fusion.10
  (5 shorter events, 0.1 us)
Async XLA Ops:
  50.5 92.9 %copy-start.7 = (f32[16,16]{1,0:T(8,128)S(1)}, f32[16,16]{1,0:T(8,128)}, u32[]{:S(2)}) copy-start(f32[16,16]{1,0:T(8,128)} %param.24) | copy-start | bytes 3076
  50.5 92.9 %copy-start.8 = (f32[16,16]{1,0:T(8,128)S(1)}, f32[16,16]{1,0:T(8,128)}, u32[]{:S(2)}) copy-start(f32[16,16]{1,0:T(8,128)} %param.28) | copy-start | bytes 3076
  50.5 92.9 %copy-start.9 = (f32[16,16]{1,0:T(8,128)S(1)}, f32[16,16]{1,0:T(8,128)}, u32[]{:S(2)}) copy-start(f32[16,16]{1,0:T(8,128)} %param.27) | copy-start | bytes 3076
  50.5 93.6 %copy-start.4 = (f32[2,3,16,32]{3,2,1,0:T(8,128)S(1)}, f32[2,3,16,32]{3,2,1,0:T(8,128)}, u32[]{:S(2)}) copy-start(f32[2,3,16,32]{3,2,1,0:T(8,128)} %param.26) | copy-start | bytes 36868
  50.5 93.6 %copy-start.5 = (f32[2,3,16,32]{3,2,1,0:T(8,128)S(1)}, f32[2,3,16,32]{3,2,1,0:T(8,128)}, u32[]{:S(2)}) copy-start(f32[2,3,16,32]{3,2,1,0:T(8,128)} %param.32) | copy-start | bytes 36868
  50.5 93.6 %copy-start.6 = (f32[2,3,16,32]{3,2,1,0:T(8,128)S(1)}, f32[2,3,16,32]{3,2,1,0:T(8,128)}, u32[]{:S(2)}) copy-start(f32[2,3,16,32]{3,2,1,0:T(8,128)} %param.31) | copy-start | bytes 36868
  140.8 7.0 %copy-start.1 = (bf16[4,16,4992]{2,1,0:T(8,128)(2,1)S(1)}, bf16[4,16,4992]{2,1,0:T(8,128)(2,1)}, u32[]{:S(2)}) copy-start(bf16[4,16,4992]{2,1,0:T(8,128)(2,1)} %get-tuple-element.29) | copy-start | bytes 1916932
  144.9 4.9 %copy-start = (f32[16,4096]{1,0:T(8,128)S(1)}, f32[16,4096]{1,0:T(8,128)}, u32[]{:S(2)}) copy-start(f32[16,4096]{1,0:T(8,128)} %param.25) | copy-start | bytes 786436
  144.9 4.9 %copy-start.2 = (f32[16,4096]{1,0:T(8,128)S(1)}, f32[16,4096]{1,0:T(8,128)}, u32[]{:S(2)}) copy-start(f32[16,4096]{1,0:T(8,128)} %param.30) | copy-start | bytes 786436
  144.9 4.9 %copy-start.3 = (f32[16,4096]{1,0:T(8,128)S(1)}, f32[16,4096]{1,0:T(8,128)}, u32[]{:S(2)}) copy-start(f32[16,4096]{1,0:T(8,128)} %param.29) | copy-start | bytes 786436

commit v2 on v1

v2 whole, which is shorter than its diff:
```python
import functools

import jax
import jax.numpy as jnp
from jax import lax
from jax.experimental import pallas as pl
from jax.experimental.pallas import tpu as pltpu
from jax.sharding import PartitionSpec as P

HID = 128
EFEAT = 16
MA = 29
ME = 812
PADA = 32
STEP = 5
DXC = 4
MESH = pl.DeviceIdType.MESH
VMEM_LIMIT = 60 << 20
bf = jnp.bfloat16
f32 = jnp.float32
NT = (((1,), (1,)), ((), ()))
TN = (((0,), (0,)), ((), ()))
NN = (((1,), (0,)), ((), ()))


def dot(a, b, dims):
    return lax.dot_general(a, b, dims, preferred_element_type=f32)


def roll(x, src, dst):
    shift = (dst - src) % HID
    return pltpu.roll(x, shift, 1) if shift else x


def sig(v):
    return 0.5 + 0.5 * jnp.tanh(0.5 * v)


def rcopy(src, dst, ssem, rsem, dev):
    return pltpu.make_async_remote_copy(
        src_ref=src, dst_ref=dst, send_sem=ssem, recv_sem=rsem, device_id=dev, device_id_type=MESH
    )


class Shape:
    def __init__(self, ndp, nmp, node_state, edge_feat, edge_in, edge_out, gru):
        self.ndp, self.nmp, self.half = ndp, nmp, ndp // 2
        self.atoms, self.uw = node_state.shape
        self.edges = edge_feat.shape[1]
        self.mols = self.atoms // MA
        self.nm = self.mols // nmp
        self.rows = self.nm * PADA
        self.hl, self.il, self.ew = edge_out.shape[0], gru.shape[2], edge_in.shape[1]
        self.rw = edge_out.shape[1] // HID
        self.wr = self.hl * self.rw
        self.rb = self.wr + 32
        self.per = self.nm * ME
        self.starts = [self.per * j // 128 * 128 for j in range(nmp)]
        self.bases = [ME * i // 128 * 128 for i in range(self.nm)]
        self.win = self.bases[-1] + 1024
        self.full = self.edges // 128 * 128
        shift = max(self.per * j - s for j, s in enumerate(self.starts))
        assert all(ME * i + shift + ME <= b + 1024 for i, b in enumerate(self.bases))
        assert self.starts[-1] + self.win - 128 == self.full
        assert all(b - a == self.win - 128 for a, b in zip(self.starts, self.starts[1:]))


def kernel(
    z,
    eo_ref, ei_ref, gw_ref, xc_ref, feat_ref, snd_ref, rcv_ref, msk_ref,
    go_ref, gg_ref, gi_ref, at_ref, ge_ref,
    wall, xsb, xo, wis, stage, stage2, wtmp, stmp, itmp, featw, keyw,
    featp, kron, emat, hid, slope, bmat, cmat, dpre, gacc, gfull, gin, geacc,
    grads, rc, sb, rp, zs, rz, fin, osb, oso, geo, gis, giz, giz_s,
    zsem, psem, csem, rsem, xs_s, xs_r, wi_s, wi_r, lsem,
    cs, cr, ps, pr, z2, zr, os_s, os_r, ge_s, ge_r, gi_s, gi_r, gz_s, gz_r,
):
    ndp, nmp, half, nm = z.ndp, z.nmp, z.half, z.nm
    hl, il, wr, rb, rw = z.hl, z.il, z.wr, z.rb, z.rw
    d = lax.axis_index("dp")
    m = lax.axis_index("mp")
    u = d // 2
    c = d % 2
    zp = [(d, (m + i) % nmp) for i in range(1, nmp)]
    pp = [(2 * ((u + t) % half) + c, m) for t in range(1, half)]
    cp = (2 * u + (1 - c), m)
    dpp = [((d + i) % ndp, m) for i in range(1, ndp)]
    bar = pltpu.get_barrier_semaphore()
    for p in zp + dpp:
        pl.semaphore_signal(bar, inc=1, device_id=p, device_id_type=MESH)
    lane = lax.broadcasted_iota(jnp.int32, (1, HID), 1)
    for r in range(rw):
        wtmp[:, r, :] = eo_ref[:, r * HID : (r + 1) * HID]
    wall[d, m, 0:wr, :] = wtmp[...].reshape(wr, HID).astype(bf)
    stmp[...] = jnp.zeros(stmp.shape, f32)
    for s in range(2):
        for g in range(3):
            stmp[16 * s : 16 * s + il, g * z.uw : (g + 1) * z.uw] = gw_ref[s, g]
    wall[d, m, wr:rb, :] = stmp[...].astype(bf)
    itmp[...] = jnp.zeros(itmp.shape, f32)
    itmp[:, 0 : z.ew] = ei_ref[...]
    wis[d] = pltpu.roll(itmp[...], d * z.ew, 1).astype(bf)
    stage[...] = xc_ref[...].astype(f32)
    stage2[...] = jnp.zeros(stage2.shape, f32)
    for i in range(z.mols):
        stage2[i * PADA : i * PADA + MA, 0 : 2 * z.uw] = stage[i * MA : (i + 1) * MA, :]
    for j in range(nmp):
        xsb[j] = stage2[j * z.rows : (j + 1) * z.rows, :].astype(bf)
    pl.semaphore_wait(bar, len(zp + dpp))

    sends = []

    def go(*copies):
        for x in copies:
            x.start()
        sends.extend(copies)

    for i, p in enumerate(dpp):
        go(rcopy(wis.at[d], wis.at[d], wi_s.at[i], wi_r.at[d], p))

    def push(n, row, col, plane):
        src = wall.at[row, col]
        if plane:
            for t, p in enumerate(pp):
                go(rcopy(src, src, psem.at[n, t], rsem.at[row, col], p))
        go(rcopy(src, src, csem.at[n if plane else nmp + n], rsem.at[row, col], cp))

    def arrived(row, col):
        here = wall.at[row, col]
        rcopy(here, here, zsem.at[0], rsem.at[row, col], cp).wait_recv()

    for i, p in enumerate(zp):
        go(rcopy(wall.at[d, m], wall.at[d, m], zsem.at[i], rsem.at[d, m], p))
    push(0, d, m, True)
    for i, p in enumerate(zp):
        go(rcopy(xsb.at[p[1]], xo.at[m], xs_s.at[i], xs_r.at[m], p))
    xo[m] = xsb[m]

    start = pl.multiple_of(z.per * m // 128 * 128, 128)
    shift = z.per * m - start
    main = z.win - 128
    featw[:, 0:main] = feat_ref[:, pl.ds(start, main)]
    for n, ref in enumerate((snd_ref, rcv_ref, msk_ref)):
        keyw[n : n + 1, 0:main] = ref[:, pl.ds(start, main)]

    @pl.when(m < nmp - 1)
    def _():
        after = pl.multiple_of(start + main, 128)
        featw[:, main:] = feat_ref[:, pl.ds(after, 128)]
        for n, ref in enumerate((snd_ref, rcv_ref, msk_ref)):
            keyw[n : n + 1, main:] = ref[:, pl.ds(after, 128)]

    @pl.when(m == nmp - 1)
    def _():
        featw[:, main:] = jnp.zeros((EFEAT, 128), bf)
        keyw[:, main:] = jnp.zeros((3, 128), jnp.int32)
        tail = z.edges - z.full
        if tail:
            featw[:, main : main + tail] = feat_ref[:, z.full :]
            for n, ref in enumerate((snd_ref, rcv_ref, msk_ref)):
                keyw[n : n + 1, main : main + tail] = ref[:, z.full :]

    def sender_key(i, lo, count):
        place = lax.broadcasted_iota(jnp.int32, (1, count), 1) + (lo - ME * i) - shift
        ok = (keyw[2:3, lo : lo + count] == 1) & (place >= 0) & (place < ME)
        return jnp.where(ok, keyw[0:1, lo : lo + count], -1)

    wio = lax.broadcasted_iota(jnp.int32, (PADA, 1024), 0)

    def permute(i):
        b = z.bases[i]
        st = wio == sender_key(i, b, 1024)
        rt = jnp.where(wio == keyw[1:2, b : b + 1024], 1.0, 0.0).astype(bf)
        ff = featw[:, b : b + 1024].astype(f32)
        for q in range(4):
            zz = jnp.concatenate(
                [jnp.where(st, ff[f : f + 1, :], 0.0).astype(bf) for f in range(4 * q, 4 * q + 4)], axis=0
            )
            featp[i * PADA : (i + 1) * PADA, q * 128 : (q + 1) * 128] = dot(rt, zz, NT).astype(bf)

    for i in range(nm):
        permute(i)
        if i == nm - 1:
            arrived(d, (m - 1 + nmp) % nmp)
            push(1, d, (m - 1 + nmp) % nmp, True)

    for i in range(1, ndp):
        row = (d - i + ndp) % ndp
        rcopy(wis.at[row], wis.at[row], wi_s.at[0], wi_r.at[row], cp).wait_recv()
    w_in = wis[...].astype(f32).sum(axis=0).astype(bf)
    delta = (
        lax.broadcasted_iota(jnp.int32, (PADA, 256), 0)
        == lax.broadcasted_iota(jnp.int32, (PADA, 256), 1) % PADA
    )

    @pl.loop(0, 16)
    def _(k):
        e = jnp.where(
            lax.broadcasted_iota(jnp.int32, (HID, 256), 0)
            == k * 8 + lax.broadcasted_iota(jnp.int32, (HID, 256), 1) // PADA,
            1.0,
            0.0,
        ).astype(bf)
        emat[k] = e
        wexp = dot(w_in, e, NN)
        for f in range(EFEAT):
            kron[k, f * PADA : (f + 1) * PADA, :] = jnp.where(delta, wexp[f : f + 1, :], 0.0).astype(bf)

    for i in range(2, nmp):
        arrived(d, (m - i + nmp) % nmp)
        push(i, d, (m - i + nmp) % nmp, True)
    fp = featp[...]

    @pl.loop(0, 16)
    def _(k):
        p = dot(fp, kron[k], NN)
        s = sig(p)
        h = p * s
        hid[k] = h.astype(bf)
        slope[k] = (s + h - h * s).astype(bf)

    for i in range(1, nmp):
        col = (m - i + nmp) % nmp
        rcopy(xo.at[col], xo.at[col], xs_s.at[0], xs_r.at[col], cp).wait_recv()
    xf = jnp.zeros((z.rows, HID), f32)
    cf = jnp.zeros((z.rows, HID), f32)
    for j in range(nmp):
        sl = xo[j].astype(f32)
        here = (lane >= z.uw * j) & (lane < z.uw * (j + 1))
        xf = jnp.where(here, roll(sl, 0, z.uw * j), xf)
        cf = jnp.where(here, roll(sl, z.uw, z.uw * j), cf)
    x = xf.astype(bf)

    n = 0
    for i in range(nmp):
        col = (m - i + nmp) % nmp
        for t in range(1, half):
            row = 2 * ((u - t + half) % half) + c
            arrived(row, col)
            push(n, row, col, False)
            n += 1

    def rows_of(row, qs):
        return jnp.concatenate(
            [wall[row, j, q * rw : (q + 1) * rw, :] for q in qs for j in range(nmp)], axis=0
        )

    def make_b(row):
        for q in range(hl // 2):
            o = dot(x, rows_of(row, (2 * q, 2 * q + 1)), NT).astype(bf)
            bmat[row * hl + 2 * q] = o[:, :HID]
            bmat[row * hl + 2 * q + 1] = o[:, HID:]

    @pl.loop(0, half)
    def _(t):
        make_b(2 * t + c)

    for i in range(nmp):
        for t in range(half):
            arrived(2 * ((u - t + half) % half) + (1 - c), (m - i + nmp) % nmp)

    @pl.loop(0, half)
    def _(t):
        make_b(2 * t + (1 - c))

    sums = []
    for i in range(nm):
        hm = jnp.concatenate([hid[k, i * PADA : (i + 1) * PADA, :] for k in range(16)], axis=1)
        sums.append(dot(hm, bmat[:, i * PADA : (i + 1) * PADA, :].reshape(PADA * HID, HID), NN))
    summed = jnp.concatenate(sums, axis=0).astype(bf)

    def gru_rows(s, j):
        for k in range(ndp):
            gfull[k * il : (k + 1) * il, 0:HID] = wall[k, j, wr + 16 * s : wr + 16 * s + 16, :].astype(f32)[:il]
        return gfull[0:HID, 0:HID].astype(bf)

    wg = [[gru_rows(s, j) for j in range(nmp)] for s in range(2)]

    def gates(a, s):
        outs = [dot(a, wg[s][j], NN) for j in range(nmp)]
        res = []
        for g in range(3):
            t = None
            for j in range(nmp):
                y = roll(outs[j], z.uw * g, z.uw * j)
                here = (lane >= z.uw * j) & (lane < z.uw * (j + 1))
                t = y if t is None else jnp.where(here, y, t)
            res.append(t)
        return res

    gi = gates(summed, 0)
    gs = gates(x, 1)
    reset = sig(gi[0] + gs[0])
    update = sig(gi[1] + gs[1])
    cand = jnp.tanh(gi[2] + reset * gs[2])
    ostate = (1.0 - update) * cand + update * xf
    dc = cf * (1.0 - update) * (1.0 - cand * cand)
    du = cf * (xf - cand) * update * (1.0 - update)
    dr = dc * gs[2] * reset * (1.0 - reset)

    def pack(gl, j):
        t = jnp.zeros((z.rows, HID), f32)
        for g in range(3):
            here = (lane >= z.uw * g) & (lane < z.uw * (g + 1))
            t = jnp.where(here, roll(gl[g], z.uw * j, z.uw * g), t)
        return t.astype(bf)

    al = [pack([dr, du, dc], j) for j in range(nmp)]
    bl = [pack([dr, du, dc * reset], j) for j in range(nmp)]
    ds = dot(jnp.concatenate(al, axis=1), jnp.concatenate(wg[0], axis=1), NT).astype(bf)
    gfull[:, HID : 2 * HID] = cf * update
    gfull[:, 0:HID] = dot(jnp.concatenate(bl, axis=1), jnp.concatenate(wg[1], axis=1), NT)
    for j in range(nmp):
        for s, (l, r) in enumerate(((summed, al[j]), (x, bl[j]))):
            gg = dot(l, r, TN)
            for k in range(ndp):
                part = gg[k * il : (k + 1) * il]
                if il < 16:
                    part = jnp.concatenate([part, jnp.zeros((16 - il, HID), f32)], axis=0)
                grads[k, j, wr + 16 * s : wr + 16 * s + 16, :] = part.astype(bf)

    zero = jnp.zeros((PADA, HID), bf)
    for p in range(nm // 2):
        lo = p * 64
        blk = jnp.concatenate(
            [
                jnp.concatenate([ds[lo : lo + 32], zero], axis=1),
                jnp.concatenate([zero, ds[lo + 32 : lo + 64]], axis=1),
            ],
            axis=0,
        )

        @pl.loop(0, 16)
        def _(k):
            o = dot(hid[k, lo : lo + 64, :], blk, TN).astype(bf)
            cmat[pl.ds(k * 8, 8), lo : lo + 32, :] = o[:, :HID].reshape(8, PADA, HID)
            cmat[pl.ds(k * 8, 8), lo + 32 : lo + 64, :] = o[:, HID:].reshape(8, PADA, HID)

    def grad_w(row):
        for q in range(hl):
            o = dot(cmat[row * hl + q], x, TN).astype(bf)
            for j in range(nmp):
                grads[row, j, q * rw : (q + 1) * rw, :] = o[rw * j : rw * (j + 1)]

    order = list(range(1, half)) + [0]
    cols = [(m + i) % nmp for i in range(1, nmp)] + [m]

    def core_arrived(t):
        rcopy(rc.at[t], rc.at[t], cs.at[t], cr.at[t], cp).wait_recv()
        if t == 0:
            return
        row = 2 * ((u + t) % half) + c
        for i, col in enumerate(cols):
            sb[t - 1, i] = (grads[row, col].astype(f32) + rc[t, col].astype(f32)).astype(bf)
            go(rcopy(sb.at[t - 1, i], rp.at[t - 1, col], ps.at[t - 1, i], pr.at[t - 1, col], pp[t - 1]))

    for n, t in enumerate(order):
        row = 2 * ((u + t) % half) + (1 - c)
        grad_w(row)
        go(rcopy(grads.at[row], rc.at[t], cs.at[t], cr.at[t], cp))
        grad_w(2 * ((u + t) % half) + c)
        if n > 0:
            core_arrived(order[n - 1])
    core_arrived(0)

    gacc[...] = jnp.zeros(gacc.shape, f32)
    step = min(DXC, hl)

    @pl.loop(0, ndp)
    def _(row):
        for q in range(0, hl, step):
            qs = range(q, q + step)
            cc = jnp.concatenate([cmat[row * hl + k] for k in qs], axis=1)
            gacc[...] += dot(cc, rows_of(row, qs), NN)

    gfin = gacc[...] + gfull[:, 0:HID] + gfull[:, HID : 2 * HID]
    for j in range(nmp):
        a = roll(ostate, z.uw * j, 0)
        b = roll(gfin, z.uw * j, z.uw)
        osb[j] = jnp.where(lane < z.uw, a, b).astype(bf)
    for i, p in enumerate(zp):
        go(rcopy(osb.at[p[1]], oso.at[m], os_s.at[i], os_r.at[m], p))
    oso[m] = osb[m]

    for i in range(nm):
        dm = ds[i * PADA : (i + 1) * PADA]
        for k in range(16):
            o = dot(dm, bmat[k * 8 : (k + 1) * 8, i * PADA : (i + 1) * PADA, :].reshape(256, HID), NT)
            dpre[k, i * PADA : (i + 1) * PADA, :] = (
                o * slope[k, i * PADA : (i + 1) * PADA, :].astype(f32)
            ).astype(bf)
    gfull[...] = jnp.zeros(gfull.shape, f32)
    gin[...] = jnp.zeros(gin.shape, f32)

    @pl.loop(0, 16)
    def _(k):
        dp_ = dpre[k]
        gfull[...] += dot(dp_, kron[k], NT)
        full = dot(fp, dp_, TN)
        full = jnp.where(delta[None], full.reshape(EFEAT, PADA, 256), 0.0).sum(axis=1)
        gin[...] += dot(full.astype(bf), emat[k], NT)

    gis[d] = gin[...].astype(bf)
    for i, p in enumerate(dpp):
        go(rcopy(gis.at[d], gis.at[d], gi_s.at[i], gi_r.at[d], p))

    def to_z(i):
        col = cols[i]
        q = grads[d, col].astype(f32) + rc[0, col].astype(f32)
        for t in range(1, half):
            here = rp.at[t - 1, col]
            rcopy(here, here, ps.at[0, 0], pr.at[t - 1, col], cp).wait_recv()
            q = q + rp[t - 1, col].astype(f32)
        if i < nmp - 1:
            zs[i] = q.astype(bf)
            go(rcopy(zs.at[i], rz.at[m], z2.at[i], zr.at[m], zp[i]))
        else:
            fin[...] = q

    gb = gfull[...].astype(bf)
    geacc[...] = jnp.zeros(geacc.shape, f32)
    w2 = wio[:, :256]
    for i in range(nm):
        for n in range(4):
            lo = z.bases[i] + n * 256
            st = w2 == sender_key(i, lo, 256)
            rt = jnp.where(w2 == keyw[1:2, lo : lo + 256], 1.0, 0.0).astype(bf)
            o = dot(gb[i * PADA : (i + 1) * PADA], rt, TN).reshape(EFEAT, PADA, 256)
            geacc[:, lo : lo + 256] += jnp.where(st[None], o, 0.0).sum(axis=1)
    geo[m] = geacc[...].astype(bf)
    for i, p in enumerate(zp):
        go(rcopy(geo.at[m], geo.at[m], ge_s.at[i], ge_r.at[m], p))

    gi_sum = gis[d].astype(f32)
    for i in range(1, ndp):
        row = (d - i + ndp) % ndp
        rcopy(gis.at[row], gis.at[row], gi_s.at[0], gi_r.at[row], cp).wait_recv()
        gi_sum = gi_sum + gis[row].astype(f32)
    giz_s[...] = gi_sum.astype(bf)
    for i, p in enumerate(zp):
        go(rcopy(giz_s, giz.at[m], gz_s.at[i], gz_r.at[m], p))
    for i in range(nmp):
        to_z(i)

    for i in range(1, nmp):
        col = (m - i + nmp) % nmp
        rcopy(oso.at[col], oso.at[col], os_s.at[0], os_r.at[col], cp).wait_recv()
    for j in range(nmp):
        stage2[j * z.rows : (j + 1) * z.rows, :] = oso[j].astype(f32)
    for i in range(z.mols):
        at_ref[i * MA : (i + 1) * MA, :] = stage2[i * PADA : i * PADA + MA, :]

    for i in range(1, nmp):
        col = (m - i + nmp) % nmp
        rcopy(giz.at[col], giz.at[col], gz_s.at[0], gz_r.at[col], cp).wait_recv()
        gi_sum = gi_sum + giz[col].astype(f32)
    gi_ref[...] = pltpu.roll(gi_sum, HID - d * z.ew, 1)[:, 0 : z.ew]
    for i in range(1, nmp):
        col = (m - i + nmp) % nmp
        rcopy(rz.at[col], rz.at[col], z2.at[0], zr.at[col], cp).wait_recv()
        fin[...] += rz[col].astype(f32)
    for s in range(2):
        for g in range(3):
            gg_ref[s, g] = fin[wr + 16 * s : wr + 16 * s + il, g * z.uw : (g + 1) * z.uw]
    wtmp[...] = fin[0:wr, :].reshape(hl, rw, HID)
    for r in range(rw):
        go_ref[:, r * HID : (r + 1) * HID] = wtmp[:, r, :]

    for i in range(1, nmp):
        col = (m - i + nmp) % nmp
        rcopy(geo.at[col], geo.at[col], ge_s.at[0], ge_r.at[col], cp).wait_recv()
    for j, lo in enumerate(z.starts):
        first = geo[j, :, 0:128]
        if j:
            first = (first.astype(f32) + geo[j - 1, :, main:].astype(f32)).astype(bf)
        ge_ref[:, lo : lo + 128] = first
        ge_ref[:, lo + 128 : lo + main] = geo[j, :, 128:main]
    if z.edges > z.full:
        ge_ref[:, z.full :] = geo[nmp - 1, :, main : main + z.edges - z.full]
    for y in sends:
        y.wait_send()


def whole_step(z, eo, ei, gw, xc, feat, snd, rcv, msk):
    dma = pltpu.SemaphoreType.DMA
    ndp, nmp, half = z.ndp, z.nmp, z.half
    rows, rb, win = z.rows, z.rb, z.win
    vm = pltpu.VMEM
    return pl.pallas_call(
        functools.partial(kernel, z),
        out_shape=(
            jax.ShapeDtypeStruct(eo.shape, f32),
            jax.ShapeDtypeStruct(gw.shape, f32),
            jax.ShapeDtypeStruct(ei.shape, f32),
            jax.ShapeDtypeStruct((z.atoms, HID), f32),
            jax.ShapeDtypeStruct(feat.shape, bf),
        ),
        in_specs=[pl.BlockSpec(memory_space=vm)] * 8,
        out_specs=(pl.BlockSpec(memory_space=vm),) * 5,
        scratch_shapes=[
            vm((ndp, nmp, rb, HID), bf),
            vm((nmp, rows, HID), bf),
            vm((nmp, rows, HID), bf),
            vm((ndp, EFEAT, HID), bf),
            vm(xc.shape, f32),
            vm((nmp * rows, HID), f32),
            vm((z.hl, z.rw, HID), f32),
            vm((32, HID), f32),
            vm((EFEAT, HID), f32),
            vm((EFEAT, win), bf),
            vm((3, win), jnp.int32),
            vm((rows, 512), bf),
            vm((16, 512, 256), bf),
            vm((16, HID, 256), bf),
            vm((16, rows, 256), bf),
            vm((16, rows, 256), bf),
            vm((HID, rows, HID), bf),
            vm((HID, rows, HID), bf),
            vm((16, rows, 256), bf),
            vm((rows, HID), f32),
            vm((rows, 512), f32),
            vm((EFEAT, HID), f32),
            vm((EFEAT, win), f32),
            vm((ndp, nmp, rb, HID), bf),
            vm((half, nmp, rb, HID), bf),
            vm((half - 1, nmp, rb, HID), bf),
            vm((half - 1, nmp, rb, HID), bf),
            vm((nmp - 1, rb, HID), bf),
            vm((nmp, rb, HID), bf),
            vm((rb, HID), f32),
            vm((nmp, rows, HID), bf),
            vm((nmp, rows, HID), bf),
            vm((nmp, EFEAT, win), bf),
            vm((ndp, EFEAT, HID), bf),
            vm((nmp, EFEAT, HID), bf),
            vm((EFEAT, HID), bf),
            dma((nmp - 1,)),
            dma((nmp, half - 1)),
            dma((nmp + nmp * (half - 1),)),
            dma((ndp, nmp)),
            dma((nmp - 1,)), dma((nmp,)),
            dma((ndp - 1,)), dma((ndp,)),
            dma((2,)),
            dma((half,)), dma((half,)),
            dma((half - 1, nmp)), dma((half - 1, nmp)),
            dma((nmp - 1,)), dma((nmp,)),
            dma((nmp - 1,)), dma((nmp,)),
            dma((nmp - 1,)), dma((nmp,)),
            dma((ndp - 1,)), dma((ndp,)),
            dma((nmp - 1,)), dma((nmp,)),
        ],
        compiler_params=pltpu.CompilerParams(
            collective_id=0, has_side_effects=True, vmem_limit_bytes=VMEM_LIMIT
        ),
    )(eo, ei, gw, xc, feat, snd, rcv, msk)


beta_one = 0.5
beta_two = 0.5
learn_rate = 0.05
decay_rate = 0.01
epsilon = 1e-08


def adam_update(weight, gradient, first_moment, second_moment):
    first_new = beta_one * first_moment + (1.0 - beta_one) * gradient
    second_new = beta_two * second_moment + (1.0 - beta_two) * gradient * gradient
    mean_hat = first_new / (1.0 - beta_one**STEP)
    square_hat = second_new / (1.0 - beta_two**STEP)
    weight_new = weight - learn_rate * (
        mean_hat / (jnp.sqrt(square_hat) + epsilon) + decay_rate * weight
    )
    return (first_new, second_new, weight_new, weight_new.astype(bf))


def body(
    ndp, nmp,
    node_state, edge_feat, sender, receiver, edge_mask, node_mask, out_grad,
    edge_in, edge_out, gru_weight,
    edge_in_m1, edge_in_m2, edge_out_m1, edge_out_m2, gru_m1, gru_m2,
):
    z = Shape(ndp, nmp, node_state, edge_feat, edge_in, edge_out, gru_weight)
    live = node_mask.astype(f32)[:, None]
    xc = jnp.concatenate([node_state, (out_grad * live).astype(bf)], axis=1)
    g_out, g_gru, g_in, at, ge = whole_step(
        z, edge_out, edge_in, gru_weight, xc, edge_feat,
        sender[None], receiver[None], edge_mask[None],
    )
    return (
        (at[:, : z.uw] * live, at[:, z.uw : 2 * z.uw], ge.astype(f32))
        + adam_update(edge_in, g_in, edge_in_m1, edge_in_m2)
        + adam_update(edge_out, g_out, edge_out_m1, edge_out_m2)
        + adam_update(gru_weight, g_gru, gru_m1, gru_m2)
    )


def solution(mesh):
    ndp, nmp = mesh.shape["dp"], mesh.shape["mp"]
    rows, lanes, gru = P("dp", "mp"), P(None, "dp"), P(None, None, "dp", "mp")
    edge = P("dp")
    return jax.shard_map(
        functools.partial(body, ndp, nmp),
        mesh=mesh,
        in_specs=(
            rows, lanes, edge, edge, edge, edge, rows,
            lanes, rows, gru, lanes, lanes, rows, rows, gru, gru,
        ),
        out_specs=(rows, rows, lanes) + (lanes,) * 4 + (rows,) * 4 + (gru,) * 4,
        check_vma=False,
    )
```

time: 151 us -> 110 us (0.73)
  Pallas kernels: 128 us -> 97 us
  local copies, waits for them, and re-layouts: 10.8 us -> 5.76 us
  other arithmetic: 11.4 us -> 6.53 us
    pallas_call x3 -> x1, Pallas kernels: 128 us -> 97 us  [whole_step(): pl.pallas_call(functools.partial(kernel, z), out_shape=(jax.ShapeDtypeStr...]
    convert_element_type x7 -> x3, other arithmetic: 5.47 us -> 1.97 us  [the longest x1 1.12 us: body(): ge.astype(f32)]
    slice x6 -> x0, local copies, waits for them, and re-layouts: 2.78 us -> none  [the longest x1 0.97 us: body(): g_out = fin[:wr].reshape(edge_out.shape)]
    dynamic_slice x1 -> x0, local copies, waits for them, and re-layouts: 1.62 us -> none  [body(): lax.dynamic_slice(jnp.pad(edge_feat, ((0, 0), (0, total - edges))), (0, s...]
    unnamed x24 -> x36, local copies, waits for them, and re-layouts: 3.64 us -> 3.69 us
where the time goes in v2:
time: 110 us
  Pallas kernels  97 us (88%)
  other arithmetic  6.53 us (6%)
  local copies, waits for them, and re-layouts  5.76 us (5%)
    pallas_call x1, Pallas kernels, whole_step(): pl.pallas_call(functools.partial(kernel, z), out_shape=(jax.ShapeDtypeStr...  97 us
    unnamed x36, local copies, waits for them, and re-layouts  3.69 us
    convert_element_type x3, other arithmetic, adam_update(): return (first_new, second_new, weight_new, weight_new.astype(bf))  2.35 us

profile of v2, /device:TPU:0, one launch (start us, length us, event | category | flops | bytes accessed | tf_op | source)
XLA Modules:
  0.0 110.1 jit_solution(11297003369360198169)
XLA Ops:
  0.6 0.0 copy-start.6
  0.7 0.0 copy-start.7
  0.7 0.0 copy-start.8
  0.7 1.1 copy.31
  1.8 0.7 convert_element_type.18
  2.5 0.2 multiply_convert_fusion
  2.6 1.0 copy.32
  3.6 0.8 pad_maximum_fusion.xc_ref
  4.4 0.0 copy-done.6
  4.4 0.7 broadcast_in_dim.10.snd_ref
  5.1 0.0 copy-done.7
  5.1 0.7 broadcast_in_dim.11.rcv_ref
  5.8 0.0 copy-done.8
  5.8 0.7 broadcast_in_dim.12.msk_ref
  6.5 97.0 %shard_map.271 = (f32[16,4096]{1,0:T(8,128)}, f32[2,3,16,32]{3,2,1,0:T(8,128)}, f32[16,16]{1,0:T(8,128)}, f32[696,128]{1,0:T(8,128)}, bf16[16,19488]{1,0:T(8,128)(2,1)}) custom-call(f32[16,4096]{1,0:T(8,128)} %eo_ref.1, f32[16,16]{1,0:T(8,128)} %ei_ref.1, f32[2,3,16,32]{3,2,1,0:T(8,128)} %gw_ref.1, bf16[696,64]{1,0:T(8,128)(2,1)} %pad_maximum_fusion.xc_ref, ...), custom_call_target="tpu_custom_call" | custom-call | tf_op jit(solution)/shard_map/pallas_call | solution.py:489
  103.4 0.0 copy-start.1
  103.5 1.4 %fusion.9 = (f32[696,32]{1,0:T(8,128)S(1)}, f32[696,32]{1,0:T(8,128)S(1)}) fusion(f32[696,128]{1,0:T(8,128)} %get-tuple-element.20, f32[696]{0:T(1024)S(1)} %convert_element_type.18), kind=kLoop, calls=%fused_computation.18 | loop fusion | flops 22272 | bytes 359136 | tf_op jit(solution)/shard_map/slice | solution.py:590
  104.9 0.8 copy.33
  105.6 0.0 copy-start.12
  105.6 0.0 copy-start.13
  105.7 0.0 copy-start.14
  105.7 0.0 copy-start.15
  105.7 0.0 copy-start
  105.7 0.0 copy-start.2
  105.7 0.0 copy-start.3
  105.7 0.0 copy-start.4
  105.7 0.8 copy.34
  106.5 0.0 copy-done.1
  106.5 1.1 %convert_element_type.20 = f32[16,19488]{1,0:T(8,128)} convert(bf16[16,19488]{1,0:T(8,128)(2,1)S(1)} %copy-done.1) | non-fusion elementwise | flops 311808 | bytes 1870848 | tf_op jit(solution)/shard_map/convert_element_type | solution.py:590
  107.6 0.0 copy-start.5
  107.6 0.0 copy-start.9
  107.6 0.0 copy-start.10
  107.6 0.0 copy-start.11
  107.6 0.0 copy-done.12
  107.6 0.0 copy-done.13
  107.6 0.0 copy-done.14
  107.7 0.0 copy-done.15
  107.7 0.6 fusion.7
  108.3 0.0 copy-done
  108.3 0.0 copy-done.2
  108.3 0.0 copy-done.3
  108.3 0.0 copy-done.4
  108.3 1.0 fusion.5
  109.4 0.0 copy-done.5
  109.4 0.0 copy-done.9
  109.4 0.0 copy-done.10
  109.4 0.0 copy-done.11
  109.4 0.7 fusion.3
Async XLA Ops:
  0.6 3.8 %copy-start.6 = (s32[19488]{0:T(1024)S(1)}, s32[19488]{0:T(1024)}, u32[]{:S(2)}) copy-start(s32[19488]{0:T(1024)} %param.18) | copy-start | bytes 233860
  0.7 4.4 %copy-start.7 = (s32[19488]{0:T(1024)S(1)}, s32[19488]{0:T(1024)}, u32[]{:S(2)}) copy-start(s32[19488]{0:T(1024)} %param.19) | copy-start | bytes 233860
  0.7 5.1 %copy-start.8 = (s32[19488]{0:T(1024)S(1)}, s32[19488]{0:T(1024)}, u32[]{:S(2)}) copy-start(s32[19488]{0:T(1024)} %param.20) | copy-start | bytes 233860
  103.4 3.0 %copy-start.1 = (bf16[16,19488]{1,0:T(8,128)(2,1)S(1)}, bf16[16,19488]{1,0:T(8,128)(2,1)}, u32[]{:S(2)}) copy-start(bf16[16,19488]{1,0:T(8,128)(2,1)} %get-tuple-element.21) | copy-start | bytes 1870852
  105.6 2.0 %copy-start.12 = (f32[16,16]{1,0:T(8,128)S(1)}, f32[16,16]{1,0:T(8,128)}, u32[]{:S(2)}) copy-start(f32[16,16]{1,0:T(8,128)} %ei_ref.1) | copy-start | bytes 3076
  105.6 2.0 %copy-start.13 = (f32[16,16]{1,0:T(8,128)S(1)}, f32[16,16]{1,0:T(8,128)}, u32[]{:S(2)}) copy-start(f32[16,16]{1,0:T(8,128)} %param.27) | copy-start | bytes 3076
  105.7 2.0 %copy-start.14 = (f32[16,16]{1,0:T(8,128)S(1)}, f32[16,16]{1,0:T(8,128)}, u32[]{:S(2)}) copy-start(f32[16,16]{1,0:T(8,128)} %param.26) | copy-start | bytes 3076
  105.7 2.0 %copy-start.15 = (f32[16,16]{1,0:T(8,128)S(1)}, f32[16,16]{1,0:T(8,128)}, u32[]{:S(2)}) copy-start(f32[16,16]{1,0:T(8,128)} %get-tuple-element.22) | copy-start | bytes 3076
  105.7 2.6 %copy-start = (f32[16,4096]{1,0:T(8,128)S(1)}, f32[16,4096]{1,0:T(8,128)}, u32[]{:S(2)}) copy-start(f32[16,4096]{1,0:T(8,128)} %eo_ref.1) | copy-start | bytes 786436
  105.7 2.6 %copy-start.2 = (f32[16,4096]{1,0:T(8,128)S(1)}, f32[16,4096]{1,0:T(8,128)}, u32[]{:S(2)}) copy-start(f32[16,4096]{1,0:T(8,128)} %param.29) | copy-start | bytes 786436
  105.7 2.6 %copy-start.3 = (f32[16,4096]{1,0:T(8,128)S(1)}, f32[16,4096]{1,0:T(8,128)}, u32[]{:S(2)}) copy-start(f32[16,4096]{1,0:T(8,128)} %param.28) | copy-start | bytes 786436
  105.7 2.6 %copy-start.4 = (f32[16,4096]{1,0:T(8,128)S(1)}, f32[16,4096]{1,0:T(8,128)}, u32[]{:S(2)}) copy-start(f32[16,4096]{1,0:T(8,128)} %get-tuple-element.23) | copy-start | bytes 786436
  107.6 1.8 %copy-start.5 = (f32[2,3,16,32]{3,2,1,0:T(8,128)S(1)}, f32[2,3,16,32]{3,2,1,0:T(8,128)}, u32[]{:S(2)}) copy-start(f32[2,3,16,32]{3,2,1,0:T(8,128)} %gw_ref.1) | copy-start | bytes 36868
  107.6 1.8 %copy-start.9 = (f32[2,3,16,32]{3,2,1,0:T(8,128)S(1)}, f32[2,3,16,32]{3,2,1,0:T(8,128)}, u32[]{:S(2)}) copy-start(f32[2,3,16,32]{3,2,1,0:T(8,128)} %param.31) | copy-start | bytes 36868
  107.6 1.8 %copy-start.10 = (f32[2,3,16,32]{3,2,1,0:T(8,128)S(1)}, f32[2,3,16,32]{3,2,1,0:T(8,128)}, u32[]{:S(2)}) copy-start(f32[2,3,16,32]{3,2,1,0:T(8,128)} %param.30) | copy-start | bytes 36868
  107.6 1.8 %copy-start.11 = (f32[2,3,16,32]{3,2,1,0:T(8,128)S(1)}, f32[2,3,16,32]{3,2,1,0:T(8,128)}, u32[]{:S(2)}) copy-start(f32[2,3,16,32]{3,2,1,0:T(8,128)} %get-tuple-element.24) | copy-start | bytes 36868

commit v3 on v2

v3 whole, which is shorter than its diff:
```python
import functools

import jax
import jax.numpy as jnp
from jax import lax
from jax.experimental import pallas as pl
from jax.experimental.pallas import tpu as pltpu
from jax.sharding import PartitionSpec as P

HID = 128
EFEAT = 16
MA = 29
ME = 812
PADA = 32
STEP = 5
DXC = 4
GEU = 19
MESH = pl.DeviceIdType.MESH
VMEM_LIMIT = 60 << 20
bf = jnp.bfloat16
f32 = jnp.float32
NT = (((1,), (1,)), ((), ()))
TN = (((0,), (0,)), ((), ()))
NN = (((1,), (0,)), ((), ()))


def dot(a, b, dims):
    return lax.dot_general(a, b, dims, preferred_element_type=f32)


def roll(x, src, dst):
    shift = (dst - src) % HID
    return pltpu.roll(x, shift, 1) if shift else x


def sig(v):
    return 0.5 + 0.5 * jnp.tanh(0.5 * v)


def rcopy(src, dst, ssem, rsem, dev):
    return pltpu.make_async_remote_copy(
        src_ref=src, dst_ref=dst, send_sem=ssem, recv_sem=rsem, device_id=dev, device_id_type=MESH
    )


class Shape:
    def __init__(self, ndp, nmp, node_state, edge_feat, edge_in, edge_out, gru):
        self.ndp, self.nmp, self.half = ndp, nmp, ndp // 2
        self.atoms, self.uw = node_state.shape
        self.edges = edge_feat.shape[1]
        self.mols = self.atoms // MA
        self.nm = self.mols // nmp
        self.rows = self.nm * PADA
        self.hl, self.il, self.ew = edge_out.shape[0], gru.shape[2], edge_in.shape[1]
        self.rw = edge_out.shape[1] // HID
        self.wr = self.hl * self.rw
        self.rb = self.wr + 32
        self.per = self.nm * ME
        self.starts = [self.per * j // 128 * 128 for j in range(nmp)]
        self.bases = [ME * i // 128 * 128 for i in range(self.nm)]
        self.win = self.bases[-1] + 1024
        self.full = self.edges // 128 * 128
        shift = max(self.per * j - s for j, s in enumerate(self.starts))
        assert all(ME * i + shift + ME <= b + 1024 for i, b in enumerate(self.bases))
        assert self.starts[-1] + self.win - 128 == self.full
        assert all(b - a == self.win - 128 for a, b in zip(self.starts, self.starts[1:]))


def kernel(
    z,
    eo_ref, ei_ref, gw_ref, ns_ref, og_ref, nm_ref, feat_ref, code_ref,
    go_ref, gg_ref, gi_ref, at_ref, ge_ref,
    wall, xsb, xo, wis, stage, stage1, stage2, wtmp, stmp, itmp, featw, keyw,
    featp, featt, kron, emat, hid, hidt, slope, bmat, cmat, dsb, dpre, gacc, gfull, eights,
    grads, rc, sb, rp, ta, tb, r2a, r2b, zs, rz, fin, osb, oso, geo, gis, giz, giz_s,
    zsem, zfsem, psem, csem, rsem, hsem, xs_s, xs_r, wi_s, wi_r,
    cs, cr, ps, pr, p2s, p2r, z2, zr, os_s, os_r, ge_s, ge_r, gi_s, gi_r, gz_s, gz_r,
):
    ndp, nmp, half, nm = z.ndp, z.nmp, z.half, z.nm
    hl, il, wr, rb, rw = z.hl, z.il, z.wr, z.rb, z.rw
    d = lax.axis_index("dp")
    m = lax.axis_index("mp")
    u = d // 2
    c = d % 2
    relay = half == 4
    low = jnp.where(2 * m < nmp, 1, 0)
    side = low * m + (1 - low) * (nmp - 1 - m)
    near = [jnp.where(i <= side, i - 1, i) for i in range(1, nmp)]
    zcols = [low * i + (1 - low) * (nmp - 1 - i) for i in near]
    zp = [(d, col) for col in zcols]
    if relay:
        ux = u + 1 - 2 * (u % 2)
        uy = (u + 2) % half
        ud = (ux + 2) % half
        chips = [ud, ux, uy, u]
        px, py = (2 * ux + c, m), (2 * uy + c, m)
        pp = [px, py]
    else:
        chips = [(u + t) % half for t in range(1, half)] + [u]
        pp = [(2 * v + c, m) for v in chips[:-1]]
    ra = rb // 2
    cp = (2 * u + (1 - c), m)
    dpp = [((d + i) % ndp, m) for i in range(1, ndp)]
    bar = pltpu.get_barrier_semaphore()
    for p in zp + dpp:
        pl.semaphore_signal(bar, inc=1, device_id=p, device_id_type=MESH)
    lane = lax.broadcasted_iota(jnp.int32, (1, HID), 1)

    def two_up(v):
        return jnp.where(lane < 64, v[: z.rows // 2], pltpu.roll(v[z.rows // 2 :], 64, 1))

    def one_up(v):
        return jnp.concatenate([v, pltpu.roll(v, 64, 1)], axis=0)

    for r in range(rw):
        wtmp[:, r, :] = eo_ref[:, r * HID : (r + 1) * HID]
    wall[d, m, 0:wr, :] = wtmp[...].reshape(wr, HID).astype(bf)
    stmp[...] = jnp.zeros(stmp.shape, f32)
    for s in range(2):
        for g in range(3):
            stmp[16 * s : 16 * s + il, g * z.uw : (g + 1) * z.uw] = gw_ref[s, g]
    wall[d, m, wr:rb, :] = stmp[...].astype(bf)
    itmp[...] = jnp.zeros(itmp.shape, f32)
    itmp[:, 0 : z.ew] = ei_ref[...]
    wis[d] = pltpu.roll(itmp[...], d * z.ew, 1).astype(bf)
    stage[...] = jnp.zeros(stage.shape, f32)
    stage[0 : z.uw, 0 : z.atoms] = ns_ref[...].astype(f32)
    stage[z.uw : 2 * z.uw, 0 : z.atoms] = og_ref[...] * nm_ref[...]
    stage1[...] = stage[...].T
    stage2[...] = jnp.zeros(stage2.shape, f32)
    for i in range(z.mols):
        stage2[i * PADA : i * PADA + MA, :] = stage1[i * MA : (i + 1) * MA, :]
    for j in range(nmp):
        xsb[j] = two_up(stage2[j * z.rows : (j + 1) * z.rows, :]).astype(bf)
    pl.semaphore_wait(bar, len(zp + dpp))

    sends = []
    maybe = []

    def go(*copies):
        for x in copies:
            x.start()
        sends.extend(copies)

    def go_if(ok, x):
        pl.when(ok)(x.start)
        maybe.append((ok, x))

    def inside(col):
        return (col >= 0) & (col < nmp)

    def apart(col, n):
        return (col - m == n) | (col - m == -n)

    for i, p in enumerate(dpp):
        go(rcopy(wis.at[d], wis.at[d], wi_s.at[i], wi_r.at[d], p))

    def push(n, row, col, plane):
        src = wall.at[row, col]
        if plane:
            for t, p in enumerate(pp):
                go(rcopy(src, src, psem.at[n, t], rsem.at[row, col], p))
        go(rcopy(src, src, csem.at[n if plane else nmp + n], rsem.at[row, col], cp))

    def arrived(row, col):
        here = wall.at[row, col]
        rcopy(here, here, zsem.at[0], rsem.at[row, col], cp).wait_recv()

    def along_z(i):
        col = zcols[i - 1]
        arrived(d, col)
        if i < 3:
            beyond = 2 * m - col
            src = wall.at[d, col]
            go_if(inside(beyond) & apart(col, 1), rcopy(src, src, zfsem.at[i - 1], rsem.at[d, col], (d, beyond)))
        push(i, d, col, True)

    def in_plane(n):
        col = ([m] + zcols)[n]
        if not relay:
            for t in range(1, half):
                row = 2 * ((u - t + half) % half) + c
                arrived(row, col)
                push(n * (half - 1) + t - 1, row, col, False)
            return
        for t, (row, dev, lo) in enumerate(((2 * ux + c, py, ra), (2 * uy + c, px, 0))):
            arrived(row, col)
            part = wall.at[row, col, pl.ds(lo, ra), :]
            go(rcopy(part, part, psem.at[n, 2 + t], hsem.at[t, col], dev))
            push(3 * n + t, row, col, False)

    def from_diagonal(n):
        if relay:
            col = ([m] + zcols)[n]
            row = 2 * ud + c
            for t, lo in enumerate((ra, 0)):
                part = wall.at[row, col, pl.ds(lo, ra), :]
                rcopy(part, part, zsem.at[0], hsem.at[t, col], cp).wait_recv()
            push(3 * n + 2, row, col, False)

    for i, col in enumerate(zcols):
        go_if(
            (col - m != 2) & (col - m != -2),
            rcopy(wall.at[d, m], wall.at[d, m], zsem.at[i], rsem.at[d, m], (d, col)),
        )
    push(0, d, m, True)
    xo[m] = xsb[m]

    start = pl.multiple_of(z.per * m // 128 * 128, 128)
    main = z.win - 128
    featw[:, 0:main] = feat_ref[:, pl.ds(start, main)]
    keyw[0:1, 0:main] = code_ref[:, pl.ds(start, main)]

    @pl.when(m < nmp - 1)
    def _():
        after = pl.multiple_of(start + main, 128)
        featw[:, main:] = feat_ref[:, pl.ds(after, 128)]
        keyw[0:1, main:] = code_ref[:, pl.ds(after, 128)]

    @pl.when(m == nmp - 1)
    def _():
        featw[:, main:] = jnp.zeros((EFEAT, 128), bf)
        keyw[0:1, main:] = jnp.zeros((1, 128), jnp.int32)
        tail = z.edges - z.full
        if tail:
            featw[:, main : main + tail] = feat_ref[:, z.full :]
            keyw[0:1, main : main + tail] = code_ref[:, z.full :]

    code = keyw[0:1, :]
    place = lax.broadcasted_iota(jnp.int32, (1, z.win), 1) + (start - z.per * m)
    valid = (place >= 0) & (place < z.per)
    mol = jnp.zeros((1, z.win), jnp.int32)
    for i in range(1, nm):
        mol = mol + jnp.where(place >= ME * i, PADA, 0)
    live = lax.shift_right_logical(code, 10)
    code = code - live * 1024
    from_ = lax.shift_right_logical(code, 5)
    keyw[0:1, :] = jnp.where(valid & (live == 1), from_, -1)
    keyw[1:2, :] = jnp.where(valid, code - from_ * 32 + mol, -1)

    wio = lax.broadcasted_iota(jnp.int32, (PADA, 1024), 0)

    def permute(i):
        b = z.bases[i]
        st = wio == keyw[0:1, b : b + 1024]
        rt = jnp.where(wio + PADA * i == keyw[1:2, b : b + 1024], 1.0, 0.0).astype(bf)
        ff = featw[:, b : b + 1024].astype(f32)
        for q in range(4):
            zz = jnp.concatenate(
                [jnp.where(st, ff[f : f + 1, :], 0.0).astype(bf) for f in range(4 * q, 4 * q + 4)], axis=0
            )
            featp[i * PADA : (i + 1) * PADA, q * 128 : (q + 1) * 128] = dot(rt, zz, NT).astype(bf)

    for i in range(nm):
        permute(i)

    for i in range(1, ndp):
        row = (d - i + ndp) % ndp
        rcopy(wis.at[row], wis.at[row], wi_s.at[0], wi_r.at[row], cp).wait_recv()
    w_in = wis[...].astype(f32).sum(axis=0).astype(bf)
    delta = (
        lax.broadcasted_iota(jnp.int32, (PADA, 256), 0)
        == lax.broadcasted_iota(jnp.int32, (PADA, 256), 1) % PADA
    )

    @pl.loop(0, 16, unroll=4)
    def _(k):
        e = jnp.where(
            lax.broadcasted_iota(jnp.int32, (HID, 256), 0)
            == k * 8 + lax.broadcasted_iota(jnp.int32, (HID, 256), 1) // PADA,
            1.0,
            0.0,
        ).astype(bf)
        emat[k] = e
        wexp = dot(w_in, e, NN)
        for f in range(EFEAT):
            kron[k, f * PADA : (f + 1) * PADA, :] = jnp.where(delta, wexp[f : f + 1, :], 0.0).astype(bf)

    along_z(1)
    for i, p in enumerate(zp):
        go(rcopy(xsb.at[p[1]], xo.at[m], xs_s.at[i], xs_r.at[m], p))
    fp = featp[...]
    featt[...] = fp.T

    def hidden(lo):
        @pl.loop(lo, lo + 8, unroll=4)
        def _(k):
            p = dot(fp, kron[k], NN)
            s = sig(p)
            h = p * s
            hid[k] = h.astype(bf)
            hidt[k] = h.T.astype(bf)
            slope[k] = (s + h - h * s).astype(bf)

    hidden(0)
    in_plane(0)
    along_z(2)
    hidden(8)

    in_plane(1)
    from_diagonal(0)
    for i in range(3, nmp):
        along_z(i)
    for n in range(2, nmp):
        in_plane(n)
        from_diagonal(n - 1)
    from_diagonal(nmp - 1)

    for col in zcols:
        rcopy(xo.at[col], xo.at[col], xs_s.at[0], xs_r.at[col], cp).wait_recv()
    xf = jnp.zeros((z.rows, HID), f32)
    cf = jnp.zeros((z.rows, HID), f32)
    for j in range(nmp):
        sl = one_up(xo[j].astype(f32))
        here = (lane >= z.uw * j) & (lane < z.uw * (j + 1))
        xf = jnp.where(here, roll(sl, 0, z.uw * j), xf)
        cf = jnp.where(here, roll(sl, z.uw, z.uw * j), cf)
    x = xf.astype(bf)

    def rows_of(row, qs):
        return jnp.concatenate(
            [wall[row, j, q * rw : (q + 1) * rw, :] for q in qs for j in range(nmp)], axis=0
        )

    def make_b(row):
        for q in range(hl // 2):
            o = dot(x, rows_of(row, (2 * q, 2 * q + 1)), NT).astype(bf)
            bmat[row * hl + 2 * q] = o[:, :HID]
            bmat[row * hl + 2 * q + 1] = o[:, HID:]

    @pl.loop(0, half, unroll=2)
    def _(t):
        make_b(2 * t + c)

    for col in [m] + zcols:
        for t in range(half):
            arrived(2 * t + (1 - c), col)

    @pl.loop(0, half, unroll=2)
    def _(t):
        make_b(2 * t + (1 - c))

    sums = []
    for i in range(nm):
        hm = jnp.concatenate([hid[k, i * PADA : (i + 1) * PADA, :] for k in range(16)], axis=1)
        sums.append(dot(hm, bmat[:, i * PADA : (i + 1) * PADA, :].reshape(PADA * HID, HID), NN))
    summed = jnp.concatenate(sums, axis=0).astype(bf)

    def gru_rows(s, j):
        if il == 16:
            return jnp.concatenate([wall[k, j, wr + 16 * s : wr + 16 * s + 16, :] for k in range(ndp)], axis=0)
        for k in range(ndp):
            gfull[k * il : (k + 1) * il, 0:HID] = wall[k, j, wr + 16 * s : wr + 16 * s + 16, :].astype(f32)[:il]
        return gfull[0:HID, 0:HID].astype(bf)

    wg = [[gru_rows(s, j) for j in range(nmp)] for s in range(2)]

    def gates(a, s):
        outs = [dot(a, wg[s][j], NN) for j in range(nmp)]
        res = []
        for g in range(3):
            t = None
            for j in range(nmp):
                y = roll(outs[j], z.uw * g, z.uw * j)
                here = (lane >= z.uw * j) & (lane < z.uw * (j + 1))
                t = y if t is None else jnp.where(here, y, t)
            res.append(t)
        return res

    gi = gates(summed, 0)
    gs = gates(x, 1)
    reset = sig(gi[0] + gs[0])
    update = sig(gi[1] + gs[1])
    cand = jnp.tanh(gi[2] + reset * gs[2])
    ostate = (1.0 - update) * cand + update * xf
    dc = cf * (1.0 - update) * (1.0 - cand * cand)
    du = cf * (xf - cand) * update * (1.0 - update)
    dr = dc * gs[2] * reset * (1.0 - reset)

    def pack(gl, j):
        t = jnp.zeros((z.rows, HID), f32)
        for g in range(3):
            here = (lane >= z.uw * g) & (lane < z.uw * (g + 1))
            t = jnp.where(here, roll(gl[g], z.uw * j, z.uw * g), t)
        return t.astype(bf)

    al = [pack([dr, du, dc], j) for j in range(nmp)]
    bl = [pack([dr, du, dc * reset], j) for j in range(nmp)]
    ds = dot(jnp.concatenate(al, axis=1), jnp.concatenate(wg[0], axis=1), NT).astype(bf)
    gfull[:, HID : 2 * HID] = cf * update
    gfull[:, 0:HID] = dot(jnp.concatenate(bl, axis=1), jnp.concatenate(wg[1], axis=1), NT)
    for j in range(nmp):
        for s, (l, r) in enumerate(((summed, al[j]), (x, bl[j]))):
            gg = dot(l, r, TN)
            for k in range(ndp):
                part = gg[k * il : (k + 1) * il]
                if il < 16:
                    part = jnp.concatenate([part, jnp.zeros((16 - il, HID), f32)], axis=0)
                grads[k, j, wr + 16 * s : wr + 16 * s + 16, :] = part.astype(bf)

    dsb[...] = jnp.zeros(dsb.shape, bf)
    for i in range(nm):
        dsb[i * PADA : (i + 1) * PADA, i * HID : (i + 1) * HID] = ds[i * PADA : (i + 1) * PADA]

    @pl.loop(0, 16, unroll=8)
    def _(k):
        for p in range(nm // 2):
            o = dot(hidt[k], dsb[:, p * 256 : (p + 1) * 256], NN).astype(bf)
            for i in range(2):
                at = (2 * p + i) * PADA
                cmat[pl.ds(k * 8, 8), at : at + PADA, :] = o[:, i * HID : (i + 1) * HID].reshape(8, PADA, HID)

    def grad_w(row):
        for q in range(hl):
            o = dot(cmat[row * hl + q], x, TN).astype(bf)
            for j in range(nmp):
                grads[row, j, q * rw : (q + 1) * rw, :] = o[rw * j : rw * (j + 1)]

    cols = zcols[::-1] + [m]

    def core_arrived(t):
        rcopy(rc.at[t], rc.at[t], cs.at[t], cr.at[t], cp).wait_recv()
        if t == half - 1:
            return
        row = 2 * chips[t] + c
        for i, col in enumerate(cols):
            sb[t, i] = (grads[row, col].astype(f32) + rc[t, col].astype(f32)).astype(bf)
            if not relay:
                go(rcopy(sb.at[t, i], rp.at[t, col], ps.at[t, i], pr.at[t, col], pp[t]))
                continue
            if t < 2:
                go(rcopy(sb.at[t, i, pl.ds(0, ra), :], rp.at[t, col, pl.ds(0, ra), :], ps.at[t, i], pr.at[t, col], px))
            if t != 1:
                k = t // 2 + 2
                go(rcopy(sb.at[t, i, pl.ds(ra, ra), :], rp.at[k % 3, col, pl.ds(ra, ra), :], ps.at[k, i], pr.at[k, col], py))

    for t in range(half):
        grad_w(2 * chips[t] + (1 - c))
        go(rcopy(grads.at[2 * chips[t] + (1 - c)], rc.at[t], cs.at[t], cr.at[t], cp))
        grad_w(2 * chips[t] + c)
        if t > 0:
            core_arrived(t - 1)
    core_arrived(half - 1)

    def part_arrived(slot, lo, col, k):
        here = rp.at[slot, col, pl.ds(lo, ra), :]
        rcopy(here, here, zsem.at[0], pr.at[k, col], cp).wait_recv()
        return rp[slot, col, lo : lo + ra, :].astype(f32)

    def turn(i):
        if not relay:
            return
        col = cols[i]
        ta[i] = (sb[2, i, 0:ra, :].astype(f32) + part_arrived(0, 0, col, 0)).astype(bf)
        go(rcopy(ta.at[i], r2a.at[col], p2s.at[0, i], p2r.at[0, col], py))
        tb[i] = (sb[1, i, ra:, :].astype(f32) + part_arrived(2, ra, col, 2)).astype(bf)
        go(rcopy(tb.at[i], r2b.at[col], p2s.at[1, i], p2r.at[1, col], px))

    def to_z(i):
        col = cols[i]
        q = grads[d, col].astype(f32) + rc[half - 1, col].astype(f32)
        if relay:
            rcopy(r2a.at[col], r2a.at[col], zsem.at[0], p2r.at[0, col], cp).wait_recv()
            rcopy(r2b.at[col], r2b.at[col], zsem.at[0], p2r.at[1, col], cp).wait_recv()
            qa = q[:ra] + part_arrived(1, 0, col, 1) + r2a[col].astype(f32)
            qb = q[ra:] + part_arrived(0, ra, col, 3) + r2b[col].astype(f32)
            q = jnp.concatenate([qa, qb], axis=0)
        else:
            for t in range(half - 1):
                here = rp.at[t, col]
                rcopy(here, here, zsem.at[0], pr.at[t, col], cp).wait_recv()
                q = q + rp[t, col].astype(f32)
        if i < nmp - 1:
            zs[i] = q.astype(bf)
            go(rcopy(zs.at[i], rz.at[m], z2.at[i], zr.at[m], (d, col)))
        else:
            fin[...] = q

    for i in range(nm):
        dm = ds[i * PADA : (i + 1) * PADA]
        for k in range(16):
            o = dot(dm, bmat[k * 8 : (k + 1) * 8, i * PADA : (i + 1) * PADA, :].reshape(256, HID), NT)
            dpre[k, i * PADA : (i + 1) * PADA, :] = (
                o * slope[k, i * PADA : (i + 1) * PADA, :].astype(f32)
            ).astype(bf)
    turn(0)
    gb = dot(
        jnp.concatenate([dpre[k] for k in range(16)], axis=1),
        jnp.concatenate([kron[k] for k in range(16)], axis=1),
        NT,
    ).astype(bf)

    def by_eight(v, mask):
        v = jnp.where(mask[None], v.reshape(EFEAT, PADA, -1), 0.0)
        return (v[:, 0:8] + v[:, 8:16] + v[:, 16:24] + v[:, 24:32]).reshape(EFEAT * 8, -1).astype(bf)

    @pl.loop(0, 16, unroll=16)
    def _(k):
        eights[k] = by_eight(dot(featt[...], dpre[k], NN), delta)

    gin = dot(
        jnp.concatenate([eights[k] for k in range(16)], axis=1),
        jnp.concatenate([emat[k] for k in range(16)], axis=1),
        NT,
    )
    gis[d] = gin.reshape(EFEAT, 8, HID).sum(axis=1).astype(bf)
    for i, p in enumerate(dpp):
        go(rcopy(gis.at[d], gis.at[d], gi_s.at[i], gi_r.at[d], p))

    turn(1)
    eight = jnp.where(
        lax.broadcasted_iota(jnp.int32, (EFEAT, EFEAT * 8), 0)
        == lax.broadcasted_iota(jnp.int32, (EFEAT, EFEAT * 8), 1) // 8,
        1.0,
        0.0,
    ).astype(bf)

    featt[...] = gb.T

    def edges_back(n, count):
        at = pl.ds(pl.multiple_of(n * 256, 256), count)
        all_rows = lax.broadcasted_iota(jnp.int32, (z.rows, count), 0)
        rt = jnp.where(all_rows == keyw[1:2, at], 1.0, 0.0).astype(bf)
        eights[n, :, 0:count] = by_eight(dot(featt[...], rt, NN), wio[:, :count] == keyw[0:1, at])

    pairs = z.win // 256
    pl.loop(0, pairs, unroll=GEU)(lambda n: edges_back(n, 256))
    if z.win % 256:
        edges_back(pairs, 128)
    for n in range(pairs):
        geo[m, :, n * 256 : (n + 1) * 256] = dot(eight, eights[n], NN).astype(bf)
    if z.win % 256:
        geo[m, :, pairs * 256 :] = dot(eight, eights[pairs, :, 0:128], NN).astype(bf)

    def edges_on(s):
        for way in (0, 1):
            col = m - s if way == 0 else m + s
            nxt = m + 1 if way == 0 else m - 1
            src = geo.at[col]
            if s:
                pl.when(inside(col))(rcopy(src, src, zsem.at[0], ge_r.at[col], cp).wait_recv)
            if s < nmp - 1:
                go_if(inside(col) & inside(nxt), rcopy(src, src, ge_s.at[s, way], ge_r.at[col], (d, nxt)))

    edges_on(0)
    turn(2)
    to_z(0)

    gacc[...] = jnp.zeros(gacc.shape, f32)
    step = min(DXC, hl)

    @pl.loop(0, ndp, unroll=2)
    def _(row):
        for q in range(0, hl, step):
            qs = range(q, q + step)
            cc = jnp.concatenate([cmat[row * hl + k] for k in qs], axis=1)
            gacc[...] += dot(cc, rows_of(row, qs), NN)

    gfin = gacc[...] + gfull[:, 0:HID] + gfull[:, HID : 2 * HID]
    for j in range(nmp):
        a = roll(ostate, z.uw * j, 0)
        b = roll(gfin, z.uw * j, z.uw)
        osb[j] = two_up(jnp.where(lane < z.uw, a, b)).astype(bf)
    for i, p in enumerate(zp):
        go(rcopy(osb.at[p[1]], oso.at[m], os_s.at[i], os_r.at[m], p))
    oso[m] = osb[m]
    turn(3)
    to_z(1)
    edges_on(1)

    gi_sum = gis[d].astype(f32)
    for i in range(1, ndp):
        row = (d - i + ndp) % ndp
        rcopy(gis.at[row], gis.at[row], gi_s.at[0], gi_r.at[row], cp).wait_recv()
        gi_sum = gi_sum + gis[row].astype(f32)
    giz_s[...] = gi_sum.astype(bf)
    for i, p in enumerate(zp):
        go(rcopy(giz_s, giz.at[m], gz_s.at[i], gz_r.at[m], p))
    to_z(2)
    edges_on(2)
    to_z(3)

    for col in zcols:
        rcopy(oso.at[col], oso.at[col], os_s.at[0], os_r.at[col], cp).wait_recv()
    for j in range(nmp):
        stage2[j * z.rows : (j + 1) * z.rows, :] = one_up(oso[j].astype(f32))
    for i in range(z.mols):
        stage1[i * MA : (i + 1) * MA, :] = stage2[i * PADA : i * PADA + MA, :]
    stage[...] = stage1[...].T
    at_ref[0 : z.uw, :] = stage[0 : z.uw, 0 : z.atoms] * nm_ref[...]
    at_ref[z.uw : 2 * z.uw, :] = stage[z.uw : 2 * z.uw, 0 : z.atoms]

    for col in zcols:
        rcopy(giz.at[col], giz.at[col], gz_s.at[0], gz_r.at[col], cp).wait_recv()
        gi_sum = gi_sum + giz[col].astype(f32)
    gi_ref[...] = pltpu.roll(gi_sum, HID - d * z.ew, 1)[:, 0 : z.ew]
    for col in zcols:
        rcopy(rz.at[col], rz.at[col], z2.at[0], zr.at[col], cp).wait_recv()
        fin[...] += rz[col].astype(f32)
    for s in range(2):
        for g in range(3):
            gg_ref[s, g] = fin[wr + 16 * s : wr + 16 * s + il, g * z.uw : (g + 1) * z.uw]
    wtmp[...] = fin[0:wr, :].reshape(hl, rw, HID)
    for r in range(rw):
        go_ref[:, r * HID : (r + 1) * HID] = wtmp[:, r, :]

    edges_on(3)
    for j, lo in enumerate(z.starts):
        first = geo[j, :, 0:128]
        if j:
            first = (first.astype(f32) + geo[j - 1, :, main:].astype(f32)).astype(bf)
        ge_ref[:, lo : lo + 128] = first
        ge_ref[:, lo + 128 : lo + main] = geo[j, :, 128:main]
    if z.edges > z.full:
        ge_ref[:, z.full :] = geo[nmp - 1, :, main : main + z.edges - z.full]
    for y in sends:
        y.wait_send()
    for ok, y in maybe:
        pl.when(ok)(y.wait_send)


def whole_step(z, eo, ei, gw, ns, og, live, feat, code):
    dma = pltpu.SemaphoreType.DMA
    ndp, nmp, half = z.ndp, z.nmp, z.half
    rows, rb, win = z.rows, z.rb, z.win
    vm = pltpu.VMEM
    ra = rb // 2
    relay = half == 4
    return pl.pallas_call(
        functools.partial(kernel, z),
        out_shape=(
            jax.ShapeDtypeStruct(eo.shape, f32),
            jax.ShapeDtypeStruct(gw.shape, f32),
            jax.ShapeDtypeStruct(ei.shape, f32),
            jax.ShapeDtypeStruct((2 * z.uw, z.atoms), f32),
            jax.ShapeDtypeStruct(feat.shape, bf),
        ),
        in_specs=[pl.BlockSpec(memory_space=vm)] * 8,
        out_specs=(pl.BlockSpec(memory_space=vm),) * 5,
        scratch_shapes=[
            vm((ndp, nmp, rb, HID), bf),
            vm((nmp, rows // 2, HID), bf),
            vm((nmp, rows // 2, HID), bf),
            vm((ndp, EFEAT, HID), bf),
            vm((HID, -(-z.atoms // 128) * 128), f32),
            vm((-(-z.atoms // 128) * 128, HID), f32),
            vm((nmp * rows, HID), f32),
            vm((z.hl, z.rw, HID), f32),
            vm((32, HID), f32),
            vm((EFEAT, HID), f32),
            vm((EFEAT, win), bf),
            vm((2, win), jnp.int32),
            vm((rows, 512), bf),
            vm((512, rows), bf),
            vm((16, 512, 256), bf),
            vm((16, HID, 256), bf),
            vm((16, rows, 256), bf),
            vm((16, 256, rows), bf),
            vm((16, rows, 256), bf),
            vm((HID, rows, HID), bf),
            vm((HID, rows, HID), bf),
            vm((rows, z.nm * HID), bf),
            vm((16, rows, 256), bf),
            vm((rows, HID), f32),
            vm((rows, 512), f32),
            vm((max(16, -(-win // 256)), EFEAT * 8, 256), bf),
            vm((ndp, nmp, rb, HID), bf),
            vm((half, nmp, rb, HID), bf),
            vm((half - 1, nmp, rb, HID), bf),
            vm((half - 1, nmp, rb, HID), bf),
            vm((nmp, ra, HID), bf),
            vm((nmp, ra, HID), bf),
            vm((nmp, ra, HID), bf),
            vm((nmp, ra, HID), bf),
            vm((nmp - 1, rb, HID), bf),
            vm((nmp, rb, HID), bf),
            vm((rb, HID), f32),
            vm((nmp, rows // 2, HID), bf),
            vm((nmp, rows // 2, HID), bf),
            vm((nmp, EFEAT, win), bf),
            vm((ndp, EFEAT, HID), bf),
            vm((nmp, EFEAT, HID), bf),
            vm((EFEAT, HID), bf),
            dma((nmp - 1,)),
            dma((2,)),
            dma((nmp, max(half - 1, 4))),
            dma((nmp + nmp * (half - 1),)),
            dma((ndp, nmp)),
            dma((2, nmp)),
            dma((nmp - 1,)), dma((nmp,)),
            dma((ndp - 1,)), dma((ndp,)),
            dma((half,)), dma((half,)),
            dma((max(half - 1, 4), nmp)), dma((max(half - 1, 4), nmp)),
            dma((2, nmp)), dma((2, nmp)),
            dma((nmp - 1,)), dma((nmp,)),
            dma((nmp - 1,)), dma((nmp,)),
            dma((nmp - 1, 2)), dma((nmp,)),
            dma((ndp - 1,)), dma((ndp,)),
            dma((nmp - 1,)), dma((nmp,)),
        ],
        compiler_params=pltpu.CompilerParams(
            collective_id=0, has_side_effects=True, vmem_limit_bytes=VMEM_LIMIT
        ),
    )(eo, ei, gw, ns, og, live, feat, code)


beta_one = 0.5
beta_two = 0.5
learn_rate = 0.05
decay_rate = 0.01
epsilon = 1e-08


def adam_update(weight, gradient, first_moment, second_moment):
    first_new = beta_one * first_moment + (1.0 - beta_one) * gradient
    second_new = beta_two * second_moment + (1.0 - beta_two) * gradient * gradient
    mean_hat = first_new / (1.0 - beta_one**STEP)
    square_hat = second_new / (1.0 - beta_two**STEP)
    weight_new = weight - learn_rate * (
        mean_hat / (jnp.sqrt(square_hat) + epsilon) + decay_rate * weight
    )
    return (first_new, second_new, weight_new, weight_new.astype(bf))


def body(
    ndp, nmp,
    node_state, edge_feat, sender, receiver, edge_mask, node_mask, out_grad,
    edge_in, edge_out, gru_weight,
    edge_in_m1, edge_in_m2, edge_out_m1, edge_out_m2, gru_m1, gru_m2,
):
    z = Shape(ndp, nmp, node_state, edge_feat, edge_in, edge_out, gru_weight)
    code = (edge_mask * 1024 + sender * 32 + receiver)[None]
    g_out, g_gru, g_in, at, ge = whole_step(
        z, edge_out, edge_in, gru_weight, node_state.T, out_grad.T,
        node_mask.astype(f32)[None], edge_feat, code,
    )
    return (
        (at[: z.uw].T, at[z.uw :].T, ge.astype(f32))
        + adam_update(edge_in, g_in, edge_in_m1, edge_in_m2)
        + adam_update(edge_out, g_out, edge_out_m1, edge_out_m2)
        + adam_update(gru_weight, g_gru, gru_m1, gru_m2)
    )


def solution(mesh):
    ndp, nmp = mesh.shape["dp"], mesh.shape["mp"]
    rows, lanes, gru = P("dp", "mp"), P(None, "dp"), P(None, None, "dp", "mp")
    edge = P("dp")
    return jax.shard_map(
        functools.partial(body, ndp, nmp),
        mesh=mesh,
        in_specs=(
            rows, lanes, edge, edge, edge, edge, rows,
            lanes, rows, gru, lanes, lanes, rows, rows, gru, gru,
        ),
        out_specs=(rows, rows, lanes) + (lanes,) * 4 + (rows,) * 4 + (gru,) * 4,
        check_vma=False,
    )
```

time: 110 us -> 91.8 us (0.83)
  Pallas kernels: 97 us -> 81.5 us
  local copies, waits for them, and re-layouts: 5.76 us -> 3.04 us
    pallas_call x1, Pallas kernels: 97 us -> 81.5 us  [whole_step(): pl.pallas_call(functools.partial(kernel, z), out_shape=(jax.ShapeDtypeStr...]
    unnamed x36 -> x24, local copies, waits for them, and re-layouts: 3.69 us -> 0.06 us
    transpose x0 -> x1, local copies, waits for them, and re-layouts: none -> 1.71 us  [body(): at[z.uw:]]
    slice x1 -> x0, other arithmetic: 1.4 us -> none  [body(): at[:, z.uw:2 * z.uw]]
where the time goes in v3:
time: 91.8 us; the launch traced here: 91.5 us
  Pallas kernels  81.5 us (89%)
  other arithmetic  6.21 us (7%)
  local copies, waits for them, and re-layouts  3.04 us (3%)
    pallas_call x1, Pallas kernels, whole_step(): pl.pallas_call(functools.partial(kernel, z), out_shape=(jax.ShapeDtypeStr...  81.5 us
    convert_element_type x3, other arithmetic, adam_update(): return (first_new, second_new, weight_new, weight_new.astype(bf))  2.35 us
    convert_element_type x1, other arithmetic, body(): ge.astype(f32)  2.2 us

profile of v3, /device:TPU:0, one launch (start us, length us, event | category | flops | bytes accessed | tf_op | source)
XLA Modules:
  0.0 91.5 jit_solution(6624756793179106322)
XLA Ops:
  0.6 0.7 convert_element_type.15
  1.3 0.6 broadcast_in_dim.6.nm_ref
  1.9 1.0 %add_add_fusion = s32[19488]{0:T(1024)S(1)} fusion(s32[19488]{0:T(1024)} %param.19, s32[19488]{0:T(1024)} %param.18, s32[19488]{0:T(1024)} %param.20), kind=kLoop, calls=%fused_computation.6 | loop fusion | flops 77952 | bytes 311808 | tf_op jit(solution)/shard_map/add | solution.py:732
  2.9 0.7 broadcast_in_dim.7.code_ref
  3.6 81.5 %shard_map.271 = (f32[16,4096]{1,0:T(8,128)}, f32[2,3,16,32]{3,2,1,0:T(8,128)}, f32[16,16]{1,0:T(8,128)}, f32[64,696]{1,0:T(8,128)}, bf16[16,19488]{1,0:T(8,128)(2,1)}) custom-call(f32[16,4096]{1,0:T(8,128)} %eo_ref.1, f32[16,16]{1,0:T(8,128)} %ei_ref.1, f32[2,3,16,32]{3,2,1,0:T(8,128)} %gw_ref.1, bf16[32,696]{1,0:T(8,128)(2,1)} %bitcast.7, ...), custom_call_target="tpu_custom_call" | custom-call | tf_op jit(solution)/shard_map/pallas_call | solution.py:629
  85.1 0.0 copy-start.8
  85.1 0.0 copy-start.9
  85.1 0.0 copy-start.10
  85.1 0.0 copy-start.11
  85.1 0.0 copy-start
  85.1 0.0 copy-start.1
  85.1 0.0 copy-start.2
  85.1 0.0 copy-start.3
  85.2 1.7 %slice_bitcast_fusion = (f32[696,32]{0,1:T(8,128)}, f32[696,32]{0,1:T(8,128)}) fusion(f32[64,696]{1,0:T(8,128)} %get-tuple-element.20), kind=kLoop, calls=%fused_computation.4 | loop fusion | bytes 356352 | tf_op jit(solution)/shard_map/transpose | solution.py:738
  86.9 2.2 %convert_element_type.16 = f32[16,19488]{1,0:T(8,128)} convert(bf16[16,19488]{1,0:T(8,128)(2,1)} %get-tuple-element.21) | non-fusion elementwise | flops 311808 | bytes 1870848 | tf_op jit(solution)/shard_map/convert_element_type | solution.py:738
  89.1 0.0 copy-start.4
  89.1 0.0 copy-start.5
  89.1 0.0 copy-start.6
  89.1 0.0 copy-start.7
  89.1 0.0 copy-done.8
  89.1 0.0 copy-done.9
  89.1 0.0 copy-done.10
  89.1 0.0 copy-done.11
  89.1 0.6 fusion.7
  89.7 0.0 copy-done
  89.7 0.0 copy-done.1
  89.7 0.0 copy-done.2
  89.8 0.0 copy-done.3
  89.8 1.0 %fusion.5 = (bf16[16,4096]{1,0:T(8,128)(2,1)}, f32[16,4096]{1,0:T(8,128)}, f32[16,4096]{1,0:T(8,128)}, f32[16,4096]{1,0:T(8,128)}) fusion(f32[16,4096]{1,0:T(8,128)S(1)} %copy-done, f32[16,4096]{1,0:T(8,128)S(1)} %copy-done.3, f32[16,4096]{1,0:T(8,128)S(1)} %copy-done.1, f32[16,4096]{1,0:T(8,128)S(1)} %copy-done.2), kind=kLoop, calls=%fused_computation.16 | loop fusion | flops 983040 | bytes 1966080 | tf_op jit(solution)/shard_map/convert_element_type | solution.py:722
  90.8 0.0 copy-done.4
  90.8 0.0 copy-done.5
  90.8 0.0 copy-done.6
  90.8 0.0 copy-done.7
  90.8 0.7 fusion.3
Async XLA Ops:
  85.1 4.0 %copy-start.8 = (f32[16,16]{1,0:T(8,128)S(1)}, f32[16,16]{1,0:T(8,128)}, u32[]{:S(2)}) copy-start(f32[16,16]{1,0:T(8,128)} %ei_ref.1) | copy-start | bytes 3076
  85.1 4.0 %copy-start.9 = (f32[16,16]{1,0:T(8,128)S(1)}, f32[16,16]{1,0:T(8,128)}, u32[]{:S(2)}) copy-start(f32[16,16]{1,0:T(8,128)} %param.27) | copy-start | bytes 3076
  85.1 4.0 %copy-start.10 = (f32[16,16]{1,0:T(8,128)S(1)}, f32[16,16]{1,0:T(8,128)}, u32[]{:S(2)}) copy-start(f32[16,16]{1,0:T(8,128)} %param.26) | copy-start | bytes 3076
  85.1 4.0 %copy-start.11 = (f32[16,16]{1,0:T(8,128)S(1)}, f32[16,16]{1,0:T(8,128)}, u32[]{:S(2)}) copy-start(f32[16,16]{1,0:T(8,128)} %get-tuple-element.22) | copy-start | bytes 3076
  85.1 4.6 %copy-start = (f32[16,4096]{1,0:T(8,128)S(1)}, f32[16,4096]{1,0:T(8,128)}, u32[]{:S(2)}) copy-start(f32[16,4096]{1,0:T(8,128)} %eo_ref.1) | copy-start | bytes 786436
  85.1 4.6 %copy-start.1 = (f32[16,4096]{1,0:T(8,128)S(1)}, f32[16,4096]{1,0:T(8,128)}, u32[]{:S(2)}) copy-start(f32[16,4096]{1,0:T(8,128)} %param.29) | copy-start | bytes 786436
  85.1 4.6 %copy-start.2 = (f32[16,4096]{1,0:T(8,128)S(1)}, f32[16,4096]{1,0:T(8,128)}, u32[]{:S(2)}) copy-start(f32[16,4096]{1,0:T(8,128)} %param.28) | copy-start | bytes 786436
  85.1 4.6 %copy-start.3 = (f32[16,4096]{1,0:T(8,128)S(1)}, f32[16,4096]{1,0:T(8,128)}, u32[]{:S(2)}) copy-start(f32[16,4096]{1,0:T(8,128)} %get-tuple-element.23) | copy-start | bytes 786436
  89.1 1.7 %copy-start.4 = (f32[2,3,16,32]{3,2,1,0:T(8,128)S(1)}, f32[2,3,16,32]{3,2,1,0:T(8,128)}, u32[]{:S(2)}) copy-start(f32[2,3,16,32]{3,2,1,0:T(8,128)} %gw_ref.1) | copy-start | bytes 36868
  89.1 1.7 %copy-start.5 = (f32[2,3,16,32]{3,2,1,0:T(8,128)S(1)}, f32[2,3,16,32]{3,2,1,0:T(8,128)}, u32[]{:S(2)}) copy-start(f32[2,3,16,32]{3,2,1,0:T(8,128)} %param.31) | copy-start | bytes 36868
  89.1 1.8 %copy-start.6 = (f32[2,3,16,32]{3,2,1,0:T(8,128)S(1)}, f32[2,3,16,32]{3,2,1,0:T(8,128)}, u32[]{:S(2)}) copy-start(f32[2,3,16,32]{3,2,1,0:T(8,128)} %param.30) | copy-start | bytes 36868
  89.1 1.8 %copy-start.7 = (f32[2,3,16,32]{3,2,1,0:T(8,128)S(1)}, f32[2,3,16,32]{3,2,1,0:T(8,128)}, u32[]{:S(2)}) copy-start(f32[2,3,16,32]{3,2,1,0:T(8,128)} %get-tuple-element.24) | copy-start | bytes 36868

commit v4 on v3

--- a/solution.py
+++ b/solution.py
@@ -14,7 +14,6 @@
 PADA = 32
 STEP = 5
 DXC = 4
-GEU = 19
 MESH = pl.DeviceIdType.MESH
 VMEM_LIMIT = 60 << 20
 bf = jnp.bfloat16
@@ -68,12 +67,12 @@
 
 def kernel(
     z,
-    eo_ref, ei_ref, gw_ref, ns_ref, og_ref, nm_ref, feat_ref, code_ref,
+    eo_ref, ei_ref, gw_ref, ns_ref, og_ref, nm_ref, feat_hbm, snd_ref, rcv_ref, msk_ref,
     go_ref, gg_ref, gi_ref, at_ref, ge_ref,
-    wall, xsb, xo, wis, stage, stage1, stage2, wtmp, stmp, itmp, featw, keyw,
-    featp, featt, kron, emat, hid, hidt, slope, bmat, cmat, dsb, dpre, gacc, gfull, eights,
+    wall, xsb, xo, wis, stage, stage1, stage2, wtmp, stmp, itmp, nmrow, feat_ref, featw, keyw,
+    featp, featt, gbt, kron, emat, hid, hidt, slope, bmat, cmat, dsb, dpre, gacc, gfull, eights,
     grads, rc, sb, rp, ta, tb, r2a, r2b, zs, rz, fin, osb, oso, geo, gis, giz, giz_s,
-    zsem, zfsem, psem, csem, rsem, hsem, xs_s, xs_r, wi_s, wi_r,
+    fsem, zsem, zfsem, psem, csem, rsem, hsem, xs_s, xs_r, wi_s, wi_r,
     cs, cr, ps, pr, p2s, p2r, z2, zr, os_s, os_r, ge_s, ge_r, gi_s, gi_r, gz_s, gz_r,
 ):
     ndp, nmp, half, nm = z.ndp, z.nmp, z.half, z.nm
@@ -102,6 +101,8 @@
     cp = (2 * u + (1 - c), m)
     dpp = [((d + i) % ndp, m) for i in range(1, ndp)]
     bar = pltpu.get_barrier_semaphore()
+    feat_in = pltpu.make_async_copy(feat_hbm, feat_ref, fsem)
+    feat_in.start()
     for p in zp + dpp:
         pl.semaphore_signal(bar, inc=1, device_id=p, device_id_type=MESH)
     lane = lax.broadcasted_iota(jnp.int32, (1, HID), 1)
@@ -125,7 +126,8 @@
     wis[d] = pltpu.roll(itmp[...], d * z.ew, 1).astype(bf)
     stage[...] = jnp.zeros(stage.shape, f32)
     stage[0 : z.uw, 0 : z.atoms] = ns_ref[...].astype(f32)
-    stage[z.uw : 2 * z.uw, 0 : z.atoms] = og_ref[...] * nm_ref[...]
+    nmrow[0, :] = nm_ref[...].astype(f32)
+    stage[z.uw : 2 * z.uw, 0 : z.atoms] = og_ref[...] * nmrow[...]
     stage1[...] = stage[...].T
     stage2[...] = jnp.zeros(stage2.shape, f32)
     for i in range(z.mols):
@@ -208,35 +210,36 @@
 
     start = pl.multiple_of(z.per * m // 128 * 128, 128)
     main = z.win - 128
+    feat_in.wait()
     featw[:, 0:main] = feat_ref[:, pl.ds(start, main)]
-    keyw[0:1, 0:main] = code_ref[:, pl.ds(start, main)]
+    keys = (snd_ref, rcv_ref, msk_ref)
+    for n, ref in enumerate(keys):
+        keyw[n, 0:main] = ref[pl.ds(start, main)]
 
     @pl.when(m < nmp - 1)
     def _():
         after = pl.multiple_of(start + main, 128)
         featw[:, main:] = feat_ref[:, pl.ds(after, 128)]
-        keyw[0:1, main:] = code_ref[:, pl.ds(after, 128)]
+        for n, ref in enumerate(keys):
+            keyw[n, main:] = ref[pl.ds(after, 128)]
 
     @pl.when(m == nmp - 1)
     def _():
         featw[:, main:] = jnp.zeros((EFEAT, 128), bf)
-        keyw[0:1, main:] = jnp.zeros((1, 128), jnp.int32)
+        keyw[:, main:] = jnp.zeros((3, 128), jnp.int32)
         tail = z.edges - z.full
         if tail:
             featw[:, main : main + tail] = feat_ref[:, z.full :]
-            keyw[0:1, main : main + tail] = code_ref[:, z.full :]
-
-    code = keyw[0:1, :]
+            for n, ref in enumerate(keys):
+                keyw[n, main : main + tail] = ref[z.full :]
+
     place = lax.broadcasted_iota(jnp.int32, (1, z.win), 1) + (start - z.per * m)
     valid = (place >= 0) & (place < z.per)
     mol = jnp.zeros((1, z.win), jnp.int32)
     for i in range(1, nm):
         mol = mol + jnp.where(place >= ME * i, PADA, 0)
-    live = lax.shift_right_logical(code, 10)
-    code = code - live * 1024
-    from_ = lax.shift_right_logical(code, 5)
-    keyw[0:1, :] = jnp.where(valid & (live == 1), from_, -1)
-    keyw[1:2, :] = jnp.where(valid, code - from_ * 32 + mol, -1)
+    keyw[0:1, :] = jnp.where(valid & (keyw[2:3, :] == 1), keyw[0:1, :], -1)
+    keyw[1:2, :] = jnp.where(valid, keyw[1:2, :] + mol, -1)
 
     wio = lax.broadcasted_iota(jnp.int32, (PADA, 1024), 0)
 
@@ -402,15 +405,19 @@
     for i in range(nm):
         dsb[i * PADA : (i + 1) * PADA, i * HID : (i + 1) * HID] = ds[i * PADA : (i + 1) * PADA]
 
-    @pl.loop(0, 16, unroll=8)
-    def _(k):
+    def c_block(k):
         for p in range(nm // 2):
             o = dot(hidt[k], dsb[:, p * 256 : (p + 1) * 256], NN).astype(bf)
             for i in range(2):
                 at = (2 * p + i) * PADA
                 cmat[pl.ds(k * 8, 8), at : at + PADA, :] = o[:, i * HID : (i + 1) * HID].reshape(8, PADA, HID)
 
+    if hl % 8:
+        pl.loop(0, 16, unroll=8)(c_block)
+
     def grad_w(row):
+        for k in range(hl // 8):
+            c_block(row * (hl // 8) + k)
         for q in range(hl):
             o = dot(cmat[row * hl + q], x, TN).astype(bf)
             for j in range(nmp):
@@ -434,13 +441,10 @@
                 k = t // 2 + 2
                 go(rcopy(sb.at[t, i, pl.ds(ra, ra), :], rp.at[k % 3, col, pl.ds(ra, ra), :], ps.at[k, i], pr.at[k, col], py))
 
-    for t in range(half):
+    def rows_out(t):
         grad_w(2 * chips[t] + (1 - c))
         go(rcopy(grads.at[2 * chips[t] + (1 - c)], rc.at[t], cs.at[t], cr.at[t], cp))
         grad_w(2 * chips[t] + c)
-        if t > 0:
-            core_arrived(t - 1)
-    core_arrived(half - 1)
 
     def part_arrived(slot, lo, col, k):
         here = rp.at[slot, col, pl.ds(lo, ra), :]
@@ -476,6 +480,59 @@
         else:
             fin[...] = q
 
+    def by_eight(v, mask):
+        v = jnp.where(mask[None], v.reshape(EFEAT, PADA, -1), 0.0)
+        return (v[:, 0:8] + v[:, 8:16] + v[:, 16:24] + v[:, 24:32]).reshape(EFEAT * 8, -1).astype(bf)
+
+    eight = jnp.where(
+        lax.broadcasted_iota(jnp.int32, (EFEAT, EFEAT * 8), 0)
+        == lax.broadcasted_iota(jnp.int32, (EFEAT, EFEAT * 8), 1) // 8,
+        1.0,
+        0.0,
+    ).astype(bf)
+    tiles = -(-z.win // 256)
+    cuts = (0, tiles // 2, tiles)
+
+    def edges_back(part):
+        for n in range(cuts[part], cuts[part + 1]):
+            count = min(256, z.win - n * 256)
+            at = pl.ds(n * 256, count)
+            all_rows = lax.broadcasted_iota(jnp.int32, (z.rows, count), 0)
+            rt = jnp.where(all_rows == keyw[1:2, at], 1.0, 0.0).astype(bf)
+            eights[n, :, 0:count] = by_eight(dot(gbt[...], rt, NN), wio[:, :count] == keyw[0:1, at])
+        for n in range(cuts[part], cuts[part + 1]):
+            count = min(256, z.win - n * 256)
+            geo[m, :, n * 256 : n * 256 + count] = dot(eight, eights[n, :, 0:count], NN).astype(bf)
+
+    def edges_on(s):
+        for part in (0, 1):
+            edges_on_part(s, part)
+
+    def edges_on_part(s, part):
+        lo, hi = 256 * cuts[part], min(256 * cuts[part + 1], z.win)
+        for way in (0, 1):
+            col = m - s if way == 0 else m + s
+            nxt = m + 1 if way == 0 else m - 1
+            src = geo.at[col, :, pl.ds(lo, hi - lo)]
+            if s:
+                pl.when(inside(col))(rcopy(src, src, zsem.at[0], ge_r.at[part, col], cp).wait_recv)
+            if s < nmp - 1:
+                go_if(
+                    inside(col) & inside(nxt),
+                    rcopy(src, src, ge_s.at[part, s, way], ge_r.at[part, col], (d, nxt)),
+                )
+
+    step = min(DXC, hl)
+
+    def state_grad(lo, hi):
+        @pl.loop(lo, hi, unroll=2)
+        def _(row):
+            for q in range(0, hl, step):
+                qs = range(q, q + step)
+                cc = jnp.concatenate([cmat[row * hl + k] for k in qs], axis=1)
+                gacc[...] += dot(cc, rows_of(row, qs), NN)
+
+    rows_out(0)
     for i in range(nm):
         dm = ds[i * PADA : (i + 1) * PADA]
         for k in range(16):
@@ -483,16 +540,23 @@
             dpre[k, i * PADA : (i + 1) * PADA, :] = (
                 o * slope[k, i * PADA : (i + 1) * PADA, :].astype(f32)
             ).astype(bf)
-    turn(0)
+    core_arrived(0)
+    for t in range(1, half - 1):
+        rows_out(t)
     gb = dot(
         jnp.concatenate([dpre[k] for k in range(16)], axis=1),
         jnp.concatenate([kron[k] for k in range(16)], axis=1),
         NT,
     ).astype(bf)
-
-    def by_eight(v, mask):
-        v = jnp.where(mask[None], v.reshape(EFEAT, PADA, -1), 0.0)
-        return (v[:, 0:8] + v[:, 8:16] + v[:, 16:24] + v[:, 24:32]).reshape(EFEAT * 8, -1).astype(bf)
+    gbt[...] = gb.T
+    edges_back(0)
+    edges_on_part(0, 0)
+    for t in range(1, half - 1):
+        core_arrived(t)
+    edges_back(1)
+    edges_on_part(0, 1)
+    rows_out(half - 1)
+    turn(0)
 
     @pl.loop(0, 16, unroll=16)
     def _(k):
@@ -506,56 +570,15 @@
     gis[d] = gin.reshape(EFEAT, 8, HID).sum(axis=1).astype(bf)
     for i, p in enumerate(dpp):
         go(rcopy(gis.at[d], gis.at[d], gi_s.at[i], gi_r.at[d], p))
-
     turn(1)
-    eight = jnp.where(
-        lax.broadcasted_iota(jnp.int32, (EFEAT, EFEAT * 8), 0)
-        == lax.broadcasted_iota(jnp.int32, (EFEAT, EFEAT * 8), 1) // 8,
-        1.0,
-        0.0,
-    ).astype(bf)
-
-    featt[...] = gb.T
-
-    def edges_back(n, count):
-        at = pl.ds(pl.multiple_of(n * 256, 256), count)
-        all_rows = lax.broadcasted_iota(jnp.int32, (z.rows, count), 0)
-        rt = jnp.where(all_rows == keyw[1:2, at], 1.0, 0.0).astype(bf)
-        eights[n, :, 0:count] = by_eight(dot(featt[...], rt, NN), wio[:, :count] == keyw[0:1, at])
-
-    pairs = z.win // 256
-    pl.loop(0, pairs, unroll=GEU)(lambda n: edges_back(n, 256))
-    if z.win % 256:
-        edges_back(pairs, 128)
-    for n in range(pairs):
-        geo[m, :, n * 256 : (n + 1) * 256] = dot(eight, eights[n], NN).astype(bf)
-    if z.win % 256:
-        geo[m, :, pairs * 256 :] = dot(eight, eights[pairs, :, 0:128], NN).astype(bf)
-
-    def edges_on(s):
-        for way in (0, 1):
-            col = m - s if way == 0 else m + s
-            nxt = m + 1 if way == 0 else m - 1
-            src = geo.at[col]
-            if s:
-                pl.when(inside(col))(rcopy(src, src, zsem.at[0], ge_r.at[col], cp).wait_recv)
-            if s < nmp - 1:
-                go_if(inside(col) & inside(nxt), rcopy(src, src, ge_s.at[s, way], ge_r.at[col], (d, nxt)))
-
-    edges_on(0)
+    edges_on(1)
+
+    gacc[...] = jnp.zeros(gacc.shape, f32)
+    state_grad(0, ndp // 2)
     turn(2)
+    core_arrived(half - 1)
     to_z(0)
-
-    gacc[...] = jnp.zeros(gacc.shape, f32)
-    step = min(DXC, hl)
-
-    @pl.loop(0, ndp, unroll=2)
-    def _(row):
-        for q in range(0, hl, step):
-            qs = range(q, q + step)
-            cc = jnp.concatenate([cmat[row * hl + k] for k in qs], axis=1)
-            gacc[...] += dot(cc, rows_of(row, qs), NN)
-
+    state_grad(ndp // 2, ndp)
     gfin = gacc[...] + gfull[:, 0:HID] + gfull[:, HID : 2 * HID]
     for j in range(nmp):
         a = roll(ostate, z.uw * j, 0)
@@ -565,8 +588,8 @@
         go(rcopy(osb.at[p[1]], oso.at[m], os_s.at[i], os_r.at[m], p))
     oso[m] = osb[m]
     turn(3)
+    edges_on(2)
     to_z(1)
-    edges_on(1)
 
     gi_sum = gis[d].astype(f32)
     for i in range(1, ndp):
@@ -577,7 +600,6 @@
     for i, p in enumerate(zp):
         go(rcopy(giz_s, giz.at[m], gz_s.at[i], gz_r.at[m], p))
     to_z(2)
-    edges_on(2)
     to_z(3)
 
     for col in zcols:
@@ -587,7 +609,7 @@
     for i in range(z.mols):
         stage1[i * MA : (i + 1) * MA, :] = stage2[i * PADA : i * PADA + MA, :]
     stage[...] = stage1[...].T
-    at_ref[0 : z.uw, :] = stage[0 : z.uw, 0 : z.atoms] * nm_ref[...]
+    at_ref[0 : z.uw, :] = stage[0 : z.uw, 0 : z.atoms] * nmrow[...]
     at_ref[z.uw : 2 * z.uw, :] = stage[z.uw : 2 * z.uw, 0 : z.atoms]
 
     for col in zcols:
@@ -619,7 +641,7 @@
         pl.when(ok)(y.wait_send)
 
 
-def whole_step(z, eo, ei, gw, ns, og, live, feat, code):
+def whole_step(z, eo, ei, gw, ns, og, live, feat, snd, rcv, msk):
     dma = pltpu.SemaphoreType.DMA
     ndp, nmp, half = z.ndp, z.nmp, z.half
     rows, rb, win = z.rows, z.rb, z.win
@@ -635,7 +657,7 @@
             jax.ShapeDtypeStruct((2 * z.uw, z.atoms), f32),
             jax.ShapeDtypeStruct(feat.shape, bf),
         ),
-        in_specs=[pl.BlockSpec(memory_space=vm)] * 8,
+        in_specs=[pl.BlockSpec(memory_space=vm)] * 6 + [pl.BlockSpec(memory_space=pl.ANY)] + [pl.BlockSpec(memory_space=vm)] * 3,
         out_specs=(pl.BlockSpec(memory_space=vm),) * 5,
         scratch_shapes=[
             vm((ndp, nmp, rb, HID), bf),
@@ -648,9 +670,12 @@
             vm((z.hl, z.rw, HID), f32),
             vm((32, HID), f32),
             vm((EFEAT, HID), f32),
+            vm((1, z.atoms), f32),
+            vm(feat.shape, bf),
             vm((EFEAT, win), bf),
-            vm((2, win), jnp.int32),
+            vm((3, win), jnp.int32),
             vm((rows, 512), bf),
+            vm((512, rows), bf),
             vm((512, rows), bf),
             vm((16, 512, 256), bf),
             vm((16, HID, 256), bf),
@@ -681,6 +706,7 @@
             vm((ndp, EFEAT, HID), bf),
             vm((nmp, EFEAT, HID), bf),
             vm((EFEAT, HID), bf),
+            dma(()),
             dma((nmp - 1,)),
             dma((2,)),
             dma((nmp, max(half - 1, 4))),
@@ -694,14 +720,14 @@
             dma((2, nmp)), dma((2, nmp)),
             dma((nmp - 1,)), dma((nmp,)),
             dma((nmp - 1,)), dma((nmp,)),
-            dma((nmp - 1, 2)), dma((nmp,)),
+            dma((2, nmp - 1, 2)), dma((2, nmp)),
             dma((ndp - 1,)), dma((ndp,)),
             dma((nmp - 1,)), dma((nmp,)),
         ],
         compiler_params=pltpu.CompilerParams(
             collective_id=0, has_side_effects=True, vmem_limit_bytes=VMEM_LIMIT
         ),
-    )(eo, ei, gw, ns, og, live, feat, code)
+    )(eo, ei, gw, ns, og, live, feat, snd, rcv, msk)
 
 
 beta_one = 0.5
@@ -722,6 +748,32 @@
     return (first_new, second_new, weight_new, weight_new.astype(bf))
 
 
+def finish_kernel(at_ref, ge_ref, *refs):
+    gs_uw = at_ref.shape[0] // 2
+    ins, outs = refs[:12], refs[12:]
+    outs[0][...] = at_ref[0:gs_uw, :]
+    outs[1][...] = at_ref[gs_uw:, :]
+    outs[2][...] = ge_ref[...].astype(f32)
+    for n in range(3):
+        new = adam_update(*[r[...] for r in ins[4 * n : 4 * n + 4]])
+        for ref, v in zip(outs[3 + 4 * n : 7 + 4 * n], new):
+            ref[...] = v
+
+
+def finish(at, ge, *layers):
+    half = jax.ShapeDtypeStruct((at.shape[0] // 2, at.shape[1]), f32)
+    results = [half, half, jax.ShapeDtypeStruct(ge.shape, f32)]
+    for n in range(3):
+        results += [jax.ShapeDtypeStruct(layers[4 * n].shape, t) for t in (f32, f32, f32, bf)]
+    return pl.pallas_call(
+        finish_kernel,
+        out_shape=tuple(results),
+        in_specs=[pl.BlockSpec(memory_space=pltpu.VMEM)] * 14,
+        out_specs=(pl.BlockSpec(memory_space=pltpu.VMEM),) * 15,
+        compiler_params=pltpu.CompilerParams(vmem_limit_bytes=VMEM_LIMIT),
+    )(at, ge, *layers)
+
+
 def body(
     ndp, nmp,
     node_state, edge_feat, sender, receiver, edge_mask, node_mask, out_grad,
@@ -729,17 +781,17 @@
     edge_in_m1, edge_in_m2, edge_out_m1, edge_out_m2, gru_m1, gru_m2,
 ):
     z = Shape(ndp, nmp, node_state, edge_feat, edge_in, edge_out, gru_weight)
-    code = (edge_mask * 1024 + sender * 32 + receiver)[None]
     g_out, g_gru, g_in, at, ge = whole_step(
-        z, edge_out, edge_in, gru_weight, node_state.T, out_grad.T,
-        node_mask.astype(f32)[None], edge_feat, code,
+        z, edge_out, edge_in, gru_weight, node_state.T, out_grad.T, node_mask,
+        edge_feat, sender, receiver, edge_mask,
     )
-    return (
-        (at[: z.uw].T, at[z.uw :].T, ge.astype(f32))
-        + adam_update(edge_in, g_in, edge_in_m1, edge_in_m2)
-        + adam_update(edge_out, g_out, edge_out_m1, edge_out_m2)
-        + adam_update(gru_weight, g_gru, gru_m1, gru_m2)
+    out_state, grad_state, *rest = finish(
+        at, ge,
+        edge_in, g_in, edge_in_m1, edge_in_m2,
+        edge_out, g_out, edge_out_m1, edge_out_m2,
+        gru_weight, g_gru, gru_m1, gru_m2,
     )
+    return (out_state.T, grad_state.T, *rest)
 
 
 def solution(mesh):

time: 91.8 us -> 78 us (0.85)
  other arithmetic: 6.21 us -> 0 us
  Pallas kernels: 81.5 us -> 77 us
  local copies, waits for them, and re-layouts: 3.04 us -> 0 us
    pallas_call x1, Pallas kernels: 81.5 us -> 73.8 us  [whole_step(): pl.pallas_call(functools.partial(kernel, z), out_shape=(jax.ShapeDtypeStr...]
    convert_element_type x5 -> x0, other arithmetic: 5.23 us -> none  [the longest x3 2.35 us: adam_update(): return (first_new, second_new, weight_new, weight_new.astype(bf))]
    pallas_call x0 -> x1, Pallas kernels: none -> 3.13 us  [finish(): pl.pallas_call(finish_kernel, out_shape=tuple(results), in_specs=[pl.Bloc...]
    transpose x1 -> x0, local copies, waits for them, and re-layouts: 1.71 us -> none  [body(): at[z.uw:]]
    broadcast_in_dim x2 -> x0, local copies, waits for them, and re-layouts: 1.27 us -> none  [the longest x1 0.69 us: body(): code = (edge_mask * 1024 + sender * 32 + receiver)[None]]
    add x1 -> x0, other arithmetic: 0.98 us -> none  [body(): code = (edge_mask * 1024 + sender * 32 + receiver)[None]]
where the time goes in v4:
time: 78 us; the launch traced here: 77.8 us
  Pallas kernels  77 us (99%)
  between operations  0.83 us (1%)
    pallas_call x1, Pallas kernels, whole_step(): pl.pallas_call(functools.partial(kernel, z), out_shape=(jax.ShapeDtypeStr...  73.8 us
    pallas_call x1, Pallas kernels, finish(): pl.pallas_call(finish_kernel, out_shape=tuple(results), in_specs=[pl.Bloc...  3.13 us

profile of v4, /device:TPU:0, one launch (start us, length us, event | category | flops | bytes accessed | tf_op | source)
XLA Modules:
  0.0 77.8 jit_solution(7179406935365801584)
XLA Ops:
  0.6 73.8 %shard_map.271 = (f32[16,4096]{1,0:T(8,128)}, f32[2,3,16,32]{3,2,1,0:T(8,128)}, f32[16,16]{1,0:T(8,128)}, f32[64,696]{1,0:T(8,128)}, bf16[16,19488]{1,0:T(8,128)(2,1)}) custom-call(f32[16,4096]{1,0:T(8,128)} %refs_4_.1, f32[16,16]{1,0:T(8,128)} %refs_0_.1, f32[2,3,16,32]{3,2,1,0:T(8,128)} %refs_8_.1, bf16[32,696]{1,0:T(8,128)(2,1)} %bitcast.5, ...), custom_call_target="tpu_custom_call" | custom-call | tf_op jit(solution)/shard_map/pallas_call | solution.py:651
  74.5 3.1 %shard_map.272 = (f32[32,696]{1,0:T(8,128)}, f32[32,696]{1,0:T(8,128)}, f32[16,19488]{1,0:T(8,128)}, f32[16,16]{1,0:T(8,128)}, f32[16,16]{1,0:T(8,128)}, /*index...) custom-call(f32[64,696]{1,0:T(8,128)} %get-tuple-element.35.at_ref, ...), custom_call_target="tpu_custom_call" | custom-call | tf_op jit(solution)/shard_map/pallas_call | solution.py:768

commit v5 on v4

--- a/solution.py
+++ b/solution.py
@@ -70,9 +70,9 @@
     eo_ref, ei_ref, gw_ref, ns_ref, og_ref, nm_ref, feat_hbm, snd_ref, rcv_ref, msk_ref,
     go_ref, gg_ref, gi_ref, at_ref, ge_ref,
     wall, xsb, xo, wis, stage, stage1, stage2, wtmp, stmp, itmp, nmrow, feat_ref, featw, keyw,
-    featp, featt, gbt, kron, emat, hid, hidt, slope, bmat, cmat, dsb, dpre, gacc, gfull, eights,
+    featp, featt, gbt, kron, emat, hid, hidt, slope, bmat, cmat, dsb, dpre, gacc, sacc, gfull, eights,
     grads, rc, sb, rp, ta, tb, r2a, r2b, zs, rz, fin, osb, oso, geo, gis, giz, giz_s,
-    fsem, zsem, zfsem, psem, csem, rsem, hsem, xs_s, xs_r, wi_s, wi_r,
+    fsem, zsem, zfsem, psem, csem, rsem, xs_s, xs_r, wi_s, wi_r,
     cs, cr, ps, pr, p2s, p2r, z2, zr, os_s, os_r, ge_s, ge_r, gi_s, gi_r, gz_s, gz_r,
 ):
     ndp, nmp, half, nm = z.ndp, z.nmp, z.half, z.nm
@@ -157,55 +157,80 @@
     for i, p in enumerate(dpp):
         go(rcopy(wis.at[d], wis.at[d], wi_s.at[i], wi_r.at[d], p))
 
-    def push(n, row, col, plane):
-        src = wall.at[row, col]
-        if plane:
-            for t, p in enumerate(pp):
-                go(rcopy(src, src, psem.at[n, t], rsem.at[row, col], p))
-        go(rcopy(src, src, csem.at[n if plane else nmp + n], rsem.at[row, col], cp))
-
-    def arrived(row, col):
-        here = wall.at[row, col]
-        rcopy(here, here, zsem.at[0], rsem.at[row, col], cp).wait_recv()
-
-    def along_z(i):
-        col = zcols[i - 1]
-        arrived(d, col)
-        if i < 3:
-            beyond = 2 * m - col
-            src = wall.at[d, col]
-            go_if(inside(beyond) & apart(col, 1), rcopy(src, src, zfsem.at[i - 1], rsem.at[d, col], (d, beyond)))
-        push(i, d, col, True)
+    rows_x = [2 * ux + c, 2 * uy + c] if relay else [2 * v + c for v in chips[:-1]]
+    here_cols = [m] + zcols
+    turns = [0]
+
+    def piece(row, col, k):
+        return wall.at[row, col, pl.ds(k * ra, ra), :]
+
+    def arrived(row, col, k):
+        src = piece(row, col, k)
+        rcopy(src, src, fsem, rsem.at[row, col, k], cp).wait_recv()
+
+    def give(row, col, k, sem, dev):
+        src = piece(row, col, k)
+        go(rcopy(src, src, sem, rsem.at[row, col, k], dev))
+
+    def to_core(row, col, k):
+        give(row, col, k, csem.at[turns[0]], cp)
+        turns[0] += 1
+
+    def push(n, k):
+        col = here_cols[n]
+        for t in range(len(pp)):
+            t = t if k == 0 else len(pp) - 1 - t
+            give(d, col, k, psem.at[n, k, t], pp[len(pp) - 1 - t])
+        if relay and last_direct(n, k):
+            give(d, col, k, psem.at[n, k, 2], (2 * ud + c, m))
+        to_core(d, col, k)
+
+    def last_direct(n, k):
+        return n == nmp - 1 and k == 1
+
+    def along_z(n):
+        col = here_cols[n]
+        for k in (0, 1):
+            arrived(d, col, k)
+            if n < 3:
+                beyond = 2 * m - col
+                src = piece(d, col, k)
+                go_if(
+                    inside(beyond) & apart(col, 1),
+                    rcopy(src, src, zfsem.at[n - 1, k], rsem.at[d, col, k], (d, beyond)),
+                )
+            push(n, k)
 
     def in_plane(n):
-        col = ([m] + zcols)[n]
+        col = here_cols[n]
         if not relay:
-            for t in range(1, half):
-                row = 2 * ((u - t + half) % half) + c
-                arrived(row, col)
-                push(n * (half - 1) + t - 1, row, col, False)
+            for row in rows_x:
+                for k in (0, 1):
+                    arrived(row, col, k)
+                    to_core(row, col, k)
             return
-        for t, (row, dev, lo) in enumerate(((2 * ux + c, py, ra), (2 * uy + c, px, 0))):
-            arrived(row, col)
-            part = wall.at[row, col, pl.ds(lo, ra), :]
-            go(rcopy(part, part, psem.at[n, 2 + t], hsem.at[t, col], dev))
-            push(3 * n + t, row, col, False)
+        for k in (0, 1):
+            for t in (k, 1 - k):
+                row = rows_x[1 - t]
+                arrived(row, col, k)
+                if t == k and not last_direct(n, k):
+                    give(row, col, k, psem.at[n, k, 3], (px, py)[k])
+                to_core(row, col, k)
 
     def from_diagonal(n):
         if relay:
-            col = ([m] + zcols)[n]
-            row = 2 * ud + c
-            for t, lo in enumerate((ra, 0)):
-                part = wall.at[row, col, pl.ds(lo, ra), :]
-                rcopy(part, part, zsem.at[0], hsem.at[t, col], cp).wait_recv()
-            push(3 * n + 2, row, col, False)
-
-    for i, col in enumerate(zcols):
-        go_if(
-            (col - m != 2) & (col - m != -2),
-            rcopy(wall.at[d, m], wall.at[d, m], zsem.at[i], rsem.at[d, m], (d, col)),
-        )
-    push(0, d, m, True)
+            for k in (0, 1):
+                arrived(2 * ud + c, here_cols[n], k)
+                to_core(2 * ud + c, here_cols[n], k)
+
+    for k in (0, 1):
+        for i, col in enumerate(zcols):
+            src = piece(d, m, k)
+            go_if(
+                (col - m != 2) & (col - m != -2),
+                rcopy(src, src, zsem.at[i, k], rsem.at[d, m, k], (d, col)),
+            )
+        push(0, k)
     xo[m] = xsb[m]
 
     start = pl.multiple_of(z.per * m // 128 * 128, 128)
@@ -280,8 +305,7 @@
             kron[k, f * PADA : (f + 1) * PADA, :] = jnp.where(delta, wexp[f : f + 1, :], 0.0).astype(bf)
 
     along_z(1)
-    for i, p in enumerate(zp):
-        go(rcopy(xsb.at[p[1]], xo.at[m], xs_s.at[i], xs_r.at[m], p))
+    in_plane(0)
     fp = featp[...]
     featt[...] = fp.T
 
@@ -296,18 +320,16 @@
             slope[k] = (s + h - h * s).astype(bf)
 
     hidden(0)
-    in_plane(0)
     along_z(2)
+    in_plane(1)
+    for i, p in enumerate(zp):
+        go(rcopy(xsb.at[p[1]], xo.at[m], xs_s.at[i], xs_r.at[m], p))
     hidden(8)
 
-    in_plane(1)
     from_diagonal(0)
-    for i in range(3, nmp):
-        along_z(i)
-    for n in range(2, nmp):
-        in_plane(n)
-        from_diagonal(n - 1)
-    from_diagonal(nmp - 1)
+    along_z(3)
+    in_plane(2)
+    from_diagonal(1)
 
     for col in zcols:
         rcopy(xo.at[col], xo.at[col], xs_s.at[0], xs_r.at[col], cp).wait_recv()
@@ -331,23 +353,41 @@
             bmat[row * hl + 2 * q] = o[:, :HID]
             bmat[row * hl + 2 * q + 1] = o[:, HID:]
 
-    @pl.loop(0, half, unroll=2)
-    def _(t):
-        make_b(2 * t + c)
-
-    for col in [m] + zcols:
-        for t in range(half):
-            arrived(2 * t + (1 - c), col)
-
-    @pl.loop(0, half, unroll=2)
-    def _(t):
-        make_b(2 * t + (1 - c))
-
-    sums = []
-    for i in range(nm):
-        hm = jnp.concatenate([hid[k, i * PADA : (i + 1) * PADA, :] for k in range(16)], axis=1)
-        sums.append(dot(hm, bmat[:, i * PADA : (i + 1) * PADA, :].reshape(PADA * HID, HID), NN))
-    summed = jnp.concatenate(sums, axis=0).astype(bf)
+    sacc[...] = jnp.zeros(sacc.shape, f32)
+
+    def use_row(row):
+        make_b(row)
+        if hl % 8 == 0:
+            parts = [row * (hl // 8) + k for k in range(hl // 8)]
+            for i in range(nm):
+                at = pl.ds(i * PADA, PADA)
+                hm = jnp.concatenate([hid[k, at, :] for k in parts], axis=1)
+                sacc[at, :] += dot(hm, bmat[pl.ds(row * hl, hl), at, :].reshape(PADA * hl, HID), NN)
+
+    def from_core(row):
+        for col in here_cols:
+            for k in (0, 1):
+                arrived(row, col, k)
+        use_row(row)
+
+    use_row(d)
+    in_plane(3)
+    for row in rows_x:
+        use_row(row)
+    from_core(cp[0])
+    from_diagonal(2)
+    from_diagonal(3)
+    if relay:
+        use_row(2 * ud + c)
+    for row in rows_x + ([2 * ud + c] if relay else []):
+        from_core(row + 1 - 2 * c)
+    if hl % 8:
+        for i in range(nm):
+            hm = jnp.concatenate([hid[k, i * PADA : (i + 1) * PADA, :] for k in range(16)], axis=1)
+            sacc[i * PADA : (i + 1) * PADA, :] = dot(
+                hm, bmat[:, i * PADA : (i + 1) * PADA, :].reshape(PADA * HID, HID), NN
+            )
+    summed = sacc[...].astype(bf)
 
     def gru_rows(s, j):
         if il == 16:
@@ -425,12 +465,14 @@
 
     cols = zcols[::-1] + [m]
 
-    def core_arrived(t):
-        rcopy(rc.at[t], rc.at[t], cs.at[t], cr.at[t], cp).wait_recv()
-        if t == half - 1:
-            return
+    def core_arrived(t, col):
+        rcopy(rc.at[t, col], rc.at[t, col], fsem, cr.at[t, col], cp).wait_recv()
+
+    def plane_out(t, *which):
         row = 2 * chips[t] + c
-        for i, col in enumerate(cols):
+        for i in which:
+            col = cols[i]
+            core_arrived(t, col)
             sb[t, i] = (grads[row, col].astype(f32) + rc[t, col].astype(f32)).astype(bf)
             if not relay:
                 go(rcopy(sb.at[t, i], rp.at[t, col], ps.at[t, i], pr.at[t, col], pp[t]))
@@ -441,14 +483,18 @@
                 k = t // 2 + 2
                 go(rcopy(sb.at[t, i, pl.ds(ra, ra), :], rp.at[k % 3, col, pl.ds(ra, ra), :], ps.at[k, i], pr.at[k, col], py))
 
-    def rows_out(t):
-        grad_w(2 * chips[t] + (1 - c))
-        go(rcopy(grads.at[2 * chips[t] + (1 - c)], rc.at[t], cs.at[t], cr.at[t], cp))
+    def row_out(t):
+        row = 2 * chips[t] + (1 - c)
+        grad_w(row)
+        for i, col in enumerate(cols):
+            go(rcopy(grads.at[row, col], rc.at[t, col], cs.at[t, i], cr.at[t, col], cp))
+
+    def row_own(t):
         grad_w(2 * chips[t] + c)
 
     def part_arrived(slot, lo, col, k):
         here = rp.at[slot, col, pl.ds(lo, ra), :]
-        rcopy(here, here, zsem.at[0], pr.at[k, col], cp).wait_recv()
+        rcopy(here, here, fsem, pr.at[k, col], cp).wait_recv()
         return rp[slot, col, lo : lo + ra, :].astype(f32)
 
     def turn(i):
@@ -460,25 +506,53 @@
         tb[i] = (sb[1, i, ra:, :].astype(f32) + part_arrived(2, ra, col, 2)).astype(bf)
         go(rcopy(tb.at[i], r2b.at[col], p2s.at[1, i], p2r.at[1, col], px))
 
-    def to_z(i):
+    def column(i):
         col = cols[i]
+        core_arrived(half - 1, col)
         q = grads[d, col].astype(f32) + rc[half - 1, col].astype(f32)
-        if relay:
-            rcopy(r2a.at[col], r2a.at[col], zsem.at[0], p2r.at[0, col], cp).wait_recv()
-            rcopy(r2b.at[col], r2b.at[col], zsem.at[0], p2r.at[1, col], cp).wait_recv()
-            qa = q[:ra] + part_arrived(1, 0, col, 1) + r2a[col].astype(f32)
-            qb = q[ra:] + part_arrived(0, ra, col, 3) + r2b[col].astype(f32)
-            q = jnp.concatenate([qa, qb], axis=0)
-        else:
+        if not relay:
             for t in range(half - 1):
                 here = rp.at[t, col]
-                rcopy(here, here, zsem.at[0], pr.at[t, col], cp).wait_recv()
+                rcopy(here, here, fsem, pr.at[t, col], cp).wait_recv()
                 q = q + rp[t, col].astype(f32)
-        if i < nmp - 1:
+            return q
+        rcopy(r2a.at[col], r2a.at[col], fsem, p2r.at[0, col], cp).wait_recv()
+        rcopy(r2b.at[col], r2b.at[col], fsem, p2r.at[1, col], cp).wait_recv()
+        qa = q[:ra] + part_arrived(1, 0, col, 1) + r2a[col].astype(f32)
+        qb = q[ra:] + part_arrived(0, ra, col, 3) + r2b[col].astype(f32)
+        return jnp.concatenate([qa, qb], axis=0)
+
+    at_end = (m == 0) | (m == nmp - 1)
+    between = (m > 0) & (m < nmp - 1)
+
+    def z_piece(ref, k):
+        return ref.at[pl.ds(k * ra, ra), :]
+
+    def z_arrived(way, col):
+        for k in (0, 1):
+            here = z_piece(rz.at[way, col], k)
+            rcopy(here, here, fsem, zr.at[way, col, k], cp).wait_recv()
+        return rz[way, col].astype(f32)
+
+    def z_copies(i):
+        col = cols[i]
+        up = jnp.where(col > m, 1, 0)
+        way = 1 - up
+        return way, [
+            rcopy(z_piece(zs.at[i], k), z_piece(rz.at[way, col], k), z2.at[i, k], zr.at[way, col, k], (d, m + 2 * up - 1))
+            for k in (0, 1)
+        ]
+
+    def to_z(i, when, chained):
+        @pl.when(when)
+        def _():
+            q = column(i)
+            way, copies = z_copies(i)
+            if chained:
+                q = q + z_arrived(way, cols[i])
             zs[i] = q.astype(bf)
-            go(rcopy(zs.at[i], rz.at[m], z2.at[i], zr.at[m], (d, col)))
-        else:
-            fin[...] = q
+            for x in copies:
+                x.start()
 
     def by_eight(v, mask):
         v = jnp.where(mask[None], v.reshape(EFEAT, PADA, -1), 0.0)
@@ -515,7 +589,7 @@
             nxt = m + 1 if way == 0 else m - 1
             src = geo.at[col, :, pl.ds(lo, hi - lo)]
             if s:
-                pl.when(inside(col))(rcopy(src, src, zsem.at[0], ge_r.at[part, col], cp).wait_recv)
+                pl.when(inside(col))(rcopy(src, src, fsem, ge_r.at[part, col], cp).wait_recv)
             if s < nmp - 1:
                 go_if(
                     inside(col) & inside(nxt),
@@ -532,31 +606,49 @@
                 cc = jnp.concatenate([cmat[row * hl + k] for k in qs], axis=1)
                 gacc[...] += dot(cc, rows_of(row, qs), NN)
 
-    rows_out(0)
-    for i in range(nm):
-        dm = ds[i * PADA : (i + 1) * PADA]
-        for k in range(16):
-            o = dot(dm, bmat[k * 8 : (k + 1) * 8, i * PADA : (i + 1) * PADA, :].reshape(256, HID), NT)
-            dpre[k, i * PADA : (i + 1) * PADA, :] = (
-                o * slope[k, i * PADA : (i + 1) * PADA, :].astype(f32)
-            ).astype(bf)
-    core_arrived(0)
-    for t in range(1, half - 1):
-        rows_out(t)
+    def hidden_grad(lo, hi):
+        for i in range(nm):
+            dm = ds[i * PADA : (i + 1) * PADA]
+            for k in range(lo, hi):
+                o = dot(dm, bmat[k * 8 : (k + 1) * 8, i * PADA : (i + 1) * PADA, :].reshape(256, HID), NT)
+                dpre[k, i * PADA : (i + 1) * PADA, :] = (
+                    o * slope[k, i * PADA : (i + 1) * PADA, :].astype(f32)
+                ).astype(bf)
+
+    others = range(half - 1)
+    row_out(0)
+    row_own(0)
+    row_out(1)
+    plane_out(0, 0)
+    row_own(1)
+    for t in others[2:]:
+        row_out(t)
+        plane_out(t - 1, 0)
+        row_own(t)
+    plane_out(0, 1)
+    hidden_grad(0, 8)
+    plane_out(half - 2, 0)
+    hidden_grad(8, 16)
     gb = dot(
         jnp.concatenate([dpre[k] for k in range(16)], axis=1),
         jnp.concatenate([kron[k] for k in range(16)], axis=1),
         NT,
     ).astype(bf)
     gbt[...] = gb.T
+    turn(0)
+    for t in others[1:]:
+        plane_out(t, 1)
+    plane_out(0, 2)
     edges_back(0)
     edges_on_part(0, 0)
-    for t in range(1, half - 1):
-        core_arrived(t)
     edges_back(1)
     edges_on_part(0, 1)
-    rows_out(half - 1)
-    turn(0)
+    turn(1)
+    for t in others[1:]:
+        plane_out(t, 2)
+    plane_out(0, 3)
+    row_out(half - 1)
+    row_own(half - 1)
 
     @pl.loop(0, 16, unroll=16)
     def _(k):
@@ -570,15 +662,17 @@
     gis[d] = gin.reshape(EFEAT, 8, HID).sum(axis=1).astype(bf)
     for i, p in enumerate(dpp):
         go(rcopy(gis.at[d], gis.at[d], gi_s.at[i], gi_r.at[d], p))
-    turn(1)
-    edges_on(1)
+    to_z(0, at_end, False)
 
     gacc[...] = jnp.zeros(gacc.shape, f32)
     state_grad(0, ndp // 2)
     turn(2)
-    core_arrived(half - 1)
-    to_z(0)
+    for t in others[1:]:
+        plane_out(t, 3)
+    edges_on(1)
     state_grad(ndp // 2, ndp)
+    to_z(1, at_end, False)
+    to_z(0, between, True)
     gfin = gacc[...] + gfull[:, 0:HID] + gfull[:, HID : 2 * HID]
     for j in range(nmp):
         a = roll(ostate, z.uw * j, 0)
@@ -587,9 +681,6 @@
     for i, p in enumerate(zp):
         go(rcopy(osb.at[p[1]], oso.at[m], os_s.at[i], os_r.at[m], p))
     oso[m] = osb[m]
-    turn(3)
-    edges_on(2)
-    to_z(1)
 
     gi_sum = gis[d].astype(f32)
     for i in range(1, ndp):
@@ -599,8 +690,11 @@
     giz_s[...] = gi_sum.astype(bf)
     for i, p in enumerate(zp):
         go(rcopy(giz_s, giz.at[m], gz_s.at[i], gz_r.at[m], p))
-    to_z(2)
-    to_z(3)
+    turn(3)
+    edges_on(2)
+    to_z(2, at_end, False)
+    to_z(1, between, True)
+    to_z(2, between, True)
 
     for col in zcols:
         rcopy(oso.at[col], oso.at[col], os_s.at[0], os_r.at[col], cp).wait_recv()
@@ -612,13 +706,21 @@
     at_ref[0 : z.uw, :] = stage[0 : z.uw, 0 : z.atoms] * nmrow[...]
     at_ref[z.uw : 2 * z.uw, :] = stage[z.uw : 2 * z.uw, 0 : z.atoms]
 
+    fin[...] = column(nmp - 1)
+
     for col in zcols:
         rcopy(giz.at[col], giz.at[col], gz_s.at[0], gz_r.at[col], cp).wait_recv()
         gi_sum = gi_sum + giz[col].astype(f32)
     gi_ref[...] = pltpu.roll(gi_sum, HID - d * z.ew, 1)[:, 0 : z.ew]
-    for col in zcols:
-        rcopy(rz.at[col], rz.at[col], z2.at[0], zr.at[col], cp).wait_recv()
-        fin[...] += rz[col].astype(f32)
+
+    @pl.when(m > 0)
+    def _():
+        fin[...] += z_arrived(0, m)
+
+    @pl.when(m < nmp - 1)
+    def _():
+        fin[...] += z_arrived(1, m)
+
     for s in range(2):
         for g in range(3):
             gg_ref[s, g] = fin[wr + 16 * s : wr + 16 * s + il, g * z.uw : (g + 1) * z.uw]
@@ -635,6 +737,8 @@
         ge_ref[:, lo + 128 : lo + main] = geo[j, :, 128:main]
     if z.edges > z.full:
         ge_ref[:, z.full :] = geo[nmp - 1, :, main : main + z.edges - z.full]
+    for i in range(nmp - 1):
+        sends.extend(z_copies(i)[1])
     for y in sends:
         y.wait_send()
     for ok, y in maybe:
@@ -687,6 +791,7 @@
             vm((rows, z.nm * HID), bf),
             vm((16, rows, 256), bf),
             vm((rows, HID), f32),
+            vm((rows, HID), f32),
             vm((rows, 512), f32),
             vm((max(16, -(-win // 256)), EFEAT * 8, 256), bf),
             vm((ndp, nmp, rb, HID), bf),
@@ -698,7 +803,7 @@
             vm((nmp, ra, HID), bf),
             vm((nmp, ra, HID), bf),
             vm((nmp - 1, rb, HID), bf),
-            vm((nmp, rb, HID), bf),
+            vm((2, nmp, rb, HID), bf),
             vm((rb, HID), f32),
             vm((nmp, rows // 2, HID), bf),
             vm((nmp, rows // 2, HID), bf),
@@ -707,18 +812,17 @@
             vm((nmp, EFEAT, HID), bf),
             vm((EFEAT, HID), bf),
             dma(()),
-            dma((nmp - 1,)),
-            dma((2,)),
-            dma((nmp, max(half - 1, 4))),
-            dma((nmp + nmp * (half - 1),)),
-            dma((ndp, nmp)),
-            dma((2, nmp)),
+            dma((nmp - 1, 2)),
+            dma((2, 2)),
+            dma((nmp, 2, max(half - 1, 4))),
+            dma((2 * nmp * half,)),
+            dma((ndp, nmp, 2)),
             dma((nmp - 1,)), dma((nmp,)),
             dma((ndp - 1,)), dma((ndp,)),
-            dma((half,)), dma((half,)),
+            dma((half, nmp)), dma((half, nmp)),
             dma((max(half - 1, 4), nmp)), dma((max(half - 1, 4), nmp)),
             dma((2, nmp)), dma((2, nmp)),
-            dma((nmp - 1,)), dma((nmp,)),
+            dma((nmp - 1, 2)), dma((2, nmp, 2)),
             dma((nmp - 1,)), dma((nmp,)),
             dma((2, nmp - 1, 2)), dma((2, nmp)),
             dma((ndp - 1,)), dma((ndp,)),

time: 78 us -> 72.4 us (0.928)
  Pallas kernels: 77 us -> 71.4 us
    pallas_call x1, Pallas kernels: 73.8 us -> 68.3 us  [whole_step(): pl.pallas_call(functools.partial(kernel, z), out_shape=(jax.ShapeDtypeStr...]
where the time goes in v5:
time: 72.4 us; the launch traced here: 72.2 us
  Pallas kernels  71.4 us (99%)
  between operations  0.83 us (1%)
    pallas_call x1, Pallas kernels, whole_step(): pl.pallas_call(functools.partial(kernel, z), out_shape=(jax.ShapeDtypeStr...  68.3 us
    pallas_call x1, Pallas kernels, finish(): pl.pallas_call(finish_kernel, out_shape=tuple(results), in_specs=[pl.Bloc...  3.13 us

profile of v5, /device:TPU:0, one launch (start us, length us, event | category | flops | bytes accessed | tf_op | source)
XLA Modules:
  0.0 72.2 jit_solution(1212549692882382098)
XLA Ops:
  0.6 68.3 %shard_map.271 = (f32[16,4096]{1,0:T(8,128)}, f32[2,3,16,32]{3,2,1,0:T(8,128)}, f32[16,16]{1,0:T(8,128)}, f32[64,696]{1,0:T(8,128)}, bf16[16,19488]{1,0:T(8,128)(2,1)}) custom-call(f32[16,4096]{1,0:T(8,128)} %refs_4_.1, f32[16,16]{1,0:T(8,128)} %refs_0_.1, f32[2,3,16,32]{3,2,1,0:T(8,128)} %refs_8_.1, bf16[32,696]{1,0:T(8,128)(2,1)} %bitcast.5, ...), custom_call_target="tpu_custom_call" | custom-call | tf_op jit(solution)/shard_map/pallas_call | solution.py:755
  68.9 3.1 %shard_map.272 = (f32[32,696]{1,0:T(8,128)}, f32[32,696]{1,0:T(8,128)}, f32[16,19488]{1,0:T(8,128)}, f32[16,16]{1,0:T(8,128)}, f32[16,16]{1,0:T(8,128)}, /*index...) custom-call(f32[64,696]{1,0:T(8,128)} %get-tuple-element.35.at_ref, ...), custom_call_target="tpu_custom_call" | custom-call | tf_op jit(solution)/shard_map/pallas_call | solution.py:872

commit v6 on v5

--- a/solution.py
+++ b/solution.py
@@ -67,12 +67,13 @@
 
 def kernel(
     z,
-    eo_ref, ei_ref, gw_ref, ns_ref, og_ref, nm_ref, feat_hbm, snd_ref, rcv_ref, msk_ref,
+    eo_hbm, ei_hbm, gw_hbm, ns_hbm, og_hbm, nm_hbm, feat_hbm, snd_hbm, rcv_hbm, msk_hbm,
     go_ref, gg_ref, gi_ref, at_ref, ge_ref,
-    wall, xsb, xo, wis, stage, stage1, stage2, wtmp, stmp, itmp, nmrow, feat_ref, featw, keyw,
+    eo_ref, ei_ref, gw_ref, ns_ref, og_ref, nm_ref, feat_ref, snd_ref, rcv_ref, msk_ref,
+    wall, xsb, xo, wis, stage, stage1, stage2, wtmp, stmp, itmp, nmrow, featw, keyw,
     featp, featt, gbt, kron, emat, hid, hidt, slope, bmat, cmat, dsb, dpre, gacc, sacc, gfull, eights,
     grads, rc, sb, rp, ta, tb, r2a, r2b, zs, rz, fin, osb, oso, geo, gis, giz, giz_s,
-    fsem, zsem, zfsem, psem, csem, rsem, xs_s, xs_r, wi_s, wi_r,
+    lsem, fsem, zsem, zfsem, psem, csem, rsem, xs_s, xs_r, wi_s, wi_r,
     cs, cr, ps, pr, p2s, p2r, z2, zr, os_s, os_r, ge_s, ge_r, gi_s, gi_r, gz_s, gz_r,
 ):
     ndp, nmp, half, nm = z.ndp, z.nmp, z.half, z.nm
@@ -100,11 +101,23 @@
     ra = rb // 2
     cp = (2 * u + (1 - c), m)
     dpp = [((d + i) % ndp, m) for i in range(1, ndp)]
+    pairs = (
+        (eo_hbm, eo_ref), (gw_hbm, gw_ref), (ei_hbm, ei_ref), (ns_hbm, ns_ref), (og_hbm, og_ref), (nm_hbm, nm_ref),
+        (feat_hbm, feat_ref), (snd_hbm, snd_ref), (rcv_hbm, rcv_ref), (msk_hbm, msk_ref),
+    )
+    loads = [pltpu.make_async_copy(a, b, lsem.at[i]) for i, (a, b) in enumerate(pairs)]
+    for x in loads:
+        x.start()
     bar = pltpu.get_barrier_semaphore()
-    feat_in = pltpu.make_async_copy(feat_hbm, feat_ref, fsem)
-    feat_in.start()
-    for p in zp + dpp:
+    near_by = [cp] + pp if relay else dpp
+    for p in near_by:
         pl.semaphore_signal(bar, inc=1, device_id=p, device_id_type=MESH)
+    for col in (m - 1, m + 1):
+
+        @pl.when((col >= 0) & (col < nmp))
+        def _():
+            pl.semaphore_signal(bar, inc=1, device_id=(d, col), device_id_type=MESH)
+
     lane = lax.broadcasted_iota(jnp.int32, (1, HID), 1)
 
     def two_up(v):
@@ -113,6 +126,8 @@
     def one_up(v):
         return jnp.concatenate([v, pltpu.roll(v, 64, 1)], axis=0)
 
+    for x in loads[:3]:
+        x.wait()
     for r in range(rw):
         wtmp[:, r, :] = eo_ref[:, r * HID : (r + 1) * HID]
     wall[d, m, 0:wr, :] = wtmp[...].reshape(wr, HID).astype(bf)
@@ -124,6 +139,8 @@
     itmp[...] = jnp.zeros(itmp.shape, f32)
     itmp[:, 0 : z.ew] = ei_ref[...]
     wis[d] = pltpu.roll(itmp[...], d * z.ew, 1).astype(bf)
+    for x in loads[3:6]:
+        x.wait()
     stage[...] = jnp.zeros(stage.shape, f32)
     stage[0 : z.uw, 0 : z.atoms] = ns_ref[...].astype(f32)
     nmrow[0, :] = nm_ref[...].astype(f32)
@@ -134,7 +151,7 @@
         stage2[i * PADA : i * PADA + MA, :] = stage1[i * MA : (i + 1) * MA, :]
     for j in range(nmp):
         xsb[j] = two_up(stage2[j * z.rows : (j + 1) * z.rows, :]).astype(bf)
-    pl.semaphore_wait(bar, len(zp + dpp))
+    pl.semaphore_wait(bar, len(near_by) + jnp.where(m > 0, 1, 0) + jnp.where(m < nmp - 1, 1, 0))
 
     sends = []
     maybe = []
@@ -151,11 +168,14 @@
     def inside(col):
         return (col >= 0) & (col < nmp)
 
-    def apart(col, n):
-        return (col - m == n) | (col - m == -n)
-
-    for i, p in enumerate(dpp):
-        go(rcopy(wis.at[d], wis.at[d], wi_s.at[i], wi_r.at[d], p))
+    def w_in_to(n, row, *devs):
+        for i, p in enumerate(devs):
+            go(rcopy(wis.at[row], wis.at[row], wi_s.at[n + i], wi_r.at[row], p))
+
+    def w_in_from(row):
+        rcopy(wis.at[row], wis.at[row], fsem, wi_r.at[row], cp).wait_recv()
+
+    w_in_to(0, d, *(near_by if relay else dpp))
 
     rows_x = [2 * ux + c, 2 * uy + c] if relay else [2 * v + c for v in chips[:-1]]
     here_cols = [m] + zcols
@@ -181,24 +201,15 @@
         for t in range(len(pp)):
             t = t if k == 0 else len(pp) - 1 - t
             give(d, col, k, psem.at[n, k, t], pp[len(pp) - 1 - t])
-        if relay and last_direct(n, k):
-            give(d, col, k, psem.at[n, k, 2], (2 * ud + c, m))
         to_core(d, col, k)
-
-    def last_direct(n, k):
-        return n == nmp - 1 and k == 1
 
     def along_z(n):
         col = here_cols[n]
         for k in (0, 1):
             arrived(d, col, k)
-            if n < 3:
-                beyond = 2 * m - col
-                src = piece(d, col, k)
-                go_if(
-                    inside(beyond) & apart(col, 1),
-                    rcopy(src, src, zfsem.at[n - 1, k], rsem.at[d, col, k], (d, beyond)),
-                )
+            beyond = m + 1 - 2 * jnp.where(col > m, 1, 0)
+            src = piece(d, col, k)
+            go_if(inside(beyond), rcopy(src, src, zfsem.at[n - 1, k], rsem.at[d, col, k], (d, beyond)))
             push(n, k)
 
     def in_plane(n):
@@ -213,7 +224,7 @@
             for t in (k, 1 - k):
                 row = rows_x[1 - t]
                 arrived(row, col, k)
-                if t == k and not last_direct(n, k):
+                if t == k:
                     give(row, col, k, psem.at[n, k, 3], (px, py)[k])
                 to_core(row, col, k)
 
@@ -224,18 +235,16 @@
                 to_core(2 * ud + c, here_cols[n], k)
 
     for k in (0, 1):
-        for i, col in enumerate(zcols):
+        for i, col in enumerate((m - 1, m + 1)):
             src = piece(d, m, k)
-            go_if(
-                (col - m != 2) & (col - m != -2),
-                rcopy(src, src, zsem.at[i, k], rsem.at[d, m, k], (d, col)),
-            )
+            go_if(inside(col), rcopy(src, src, zsem.at[i, k], rsem.at[d, m, k], (d, col)))
         push(0, k)
     xo[m] = xsb[m]
 
     start = pl.multiple_of(z.per * m // 128 * 128, 128)
     main = z.win - 128
-    feat_in.wait()
+    for x in loads[6:]:
+        x.wait()
     featw[:, 0:main] = feat_ref[:, pl.ds(start, main)]
     keys = (snd_ref, rcv_ref, msk_ref)
     for n, ref in enumerate(keys):
@@ -282,9 +291,22 @@
     for i in range(nm):
         permute(i)
 
-    for i in range(1, ndp):
-        row = (d - i + ndp) % ndp
-        rcopy(wis.at[row], wis.at[row], wi_s.at[0], wi_r.at[row], cp).wait_recv()
+    if relay:
+        for n, (v, devs) in enumerate(((ux, (py, cp)), (uy, (cp,)))):
+            w_in_from(2 * v + c)
+            w_in_to(3 + 2 * n, 2 * v + c, *devs)
+    along_z(1)
+    in_plane(0)
+    fp = featp[...]
+    featt[...] = fp.T
+    if relay:
+        w_in_from(2 * ud + c)
+        w_in_to(7, 2 * ud + c, cp)
+        for v in (u, ux, uy, ud):
+            w_in_from(2 * v + 1 - c)
+    else:
+        for i in range(1, ndp):
+            w_in_from((d - i + ndp) % ndp)
     w_in = wis[...].astype(f32).sum(axis=0).astype(bf)
     delta = (
         lax.broadcasted_iota(jnp.int32, (PADA, 256), 0)
@@ -304,10 +326,6 @@
         for f in range(EFEAT):
             kron[k, f * PADA : (f + 1) * PADA, :] = jnp.where(delta, wexp[f : f + 1, :], 0.0).astype(bf)
 
-    along_z(1)
-    in_plane(0)
-    fp = featp[...]
-    featt[...] = fp.T
 
     def hidden(lo):
         @pl.loop(lo, lo + 8, unroll=4)
@@ -319,15 +337,15 @@
             hidt[k] = h.T.astype(bf)
             slope[k] = (s + h - h * s).astype(bf)
 
+    along_z(2)
     hidden(0)
-    along_z(2)
     in_plane(1)
     for i, p in enumerate(zp):
         go(rcopy(xsb.at[p[1]], xo.at[m], xs_s.at[i], xs_r.at[m], p))
+
+    along_z(3)
     hidden(8)
-
     from_diagonal(0)
-    along_z(3)
     in_plane(2)
     from_diagonal(1)
 
@@ -671,8 +689,6 @@
         plane_out(t, 3)
     edges_on(1)
     state_grad(ndp // 2, ndp)
-    to_z(1, at_end, False)
-    to_z(0, between, True)
     gfin = gacc[...] + gfull[:, 0:HID] + gfull[:, HID : 2 * HID]
     for j in range(nmp):
         a = roll(ostate, z.uw * j, 0)
@@ -682,6 +698,8 @@
         go(rcopy(osb.at[p[1]], oso.at[m], os_s.at[i], os_r.at[m], p))
     oso[m] = osb[m]
 
+    to_z(1, at_end, False)
+    to_z(0, between, True)
     gi_sum = gis[d].astype(f32)
     for i in range(1, ndp):
         row = (d - i + ndp) % ndp
@@ -761,9 +779,10 @@
             jax.ShapeDtypeStruct((2 * z.uw, z.atoms), f32),
             jax.ShapeDtypeStruct(feat.shape, bf),
         ),
-        in_specs=[pl.BlockSpec(memory_space=vm)] * 6 + [pl.BlockSpec(memory_space=pl.ANY)] + [pl.BlockSpec(memory_space=vm)] * 3,
+        in_specs=[pl.BlockSpec(memory_space=pl.ANY)] * 10,
         out_specs=(pl.BlockSpec(memory_space=vm),) * 5,
         scratch_shapes=[
+            *(vm(a.shape, a.dtype) for a in (eo, ei, gw, ns, og, live, feat, snd, rcv, msk)),
             vm((ndp, nmp, rb, HID), bf),
             vm((nmp, rows // 2, HID), bf),
             vm((nmp, rows // 2, HID), bf),
@@ -775,7 +794,6 @@
             vm((32, HID), f32),
             vm((EFEAT, HID), f32),
             vm((1, z.atoms), f32),
-            vm(feat.shape, bf),
             vm((EFEAT, win), bf),
             vm((3, win), jnp.int32),
             vm((rows, 512), bf),
@@ -811,14 +829,15 @@
             vm((ndp, EFEAT, HID), bf),
             vm((nmp, EFEAT, HID), bf),
             vm((EFEAT, HID), bf),
+            dma((10,)),
             dma(()),
             dma((nmp - 1, 2)),
-            dma((2, 2)),
+            dma((nmp - 1, 2)),
             dma((nmp, 2, max(half - 1, 4))),
             dma((2 * nmp * half,)),
             dma((ndp, nmp, 2)),
             dma((nmp - 1,)), dma((nmp,)),
-            dma((ndp - 1,)), dma((ndp,)),
+            dma((max(ndp - 1, 8),)), dma((ndp,)),
             dma((half, nmp)), dma((half, nmp)),
             dma((max(half - 1, 4), nmp)), dma((max(half - 1, 4), nmp)),
             dma((2, nmp)), dma((2, nmp)),

time: 72.4 us -> 69.9 us (0.965)
  Pallas kernels: 71.4 us -> 68.9 us
    pallas_call x1, Pallas kernels: 68.3 us -> 65.8 us  [whole_step(): pl.pallas_call(functools.partial(kernel, z), out_shape=(jax.ShapeDtypeStr...]
where the time goes in v6:
time: 69.9 us; the launch traced here: 69.7 us
  Pallas kernels  68.9 us (99%)
  between operations  0.83 us (1%)
    pallas_call x1, Pallas kernels, whole_step(): pl.pallas_call(functools.partial(kernel, z), out_shape=(jax.ShapeDtypeStr...  65.8 us
    pallas_call x1, Pallas kernels, finish(): pl.pallas_call(finish_kernel, out_shape=tuple(results), in_specs=[pl.Bloc...  3.13 us

profile of v6, /device:TPU:0, one launch (start us, length us, event | category | flops | bytes accessed | tf_op | source)
XLA Modules:
  0.0 69.7 jit_solution(9417628923516410123)
XLA Ops:
  0.6 65.8 %shard_map.271 = (f32[16,4096]{1,0:T(8,128)}, f32[2,3,16,32]{3,2,1,0:T(8,128)}, f32[16,16]{1,0:T(8,128)}, f32[64,696]{1,0:T(8,128)}, bf16[16,19488]{1,0:T(8,128)(2,1)}) custom-call(f32[16,4096]{1,0:T(8,128)} %refs_4_.1, f32[16,16]{1,0:T(8,128)} %refs_0_.1, f32[2,3,16,32]{3,2,1,0:T(8,128)} %refs_8_.1, bf16[32,696]{1,0:T(8,128)(2,1)} %bitcast.5, ...), custom_call_target="tpu_custom_call" | custom-call | tf_op jit(solution)/shard_map/pallas_call | solution.py:773
  66.4 3.1 %shard_map.272 = (f32[32,696]{1,0:T(8,128)}, f32[32,696]{1,0:T(8,128)}, f32[16,19488]{1,0:T(8,128)}, f32[16,16]{1,0:T(8,128)}, f32[16,16]{1,0:T(8,128)}, /*index...) custom-call(f32[64,696]{1,0:T(8,128)} %get-tuple-element.35.at_ref, ...), custom_call_target="tpu_custom_call" | custom-call | tf_op jit(solution)/shard_map/pallas_call | solution.py:891

commit v7 on v6

--- a/solution.py
+++ b/solution.py
@@ -68,7 +68,8 @@
 def kernel(
     z,
     eo_hbm, ei_hbm, gw_hbm, ns_hbm, og_hbm, nm_hbm, feat_hbm, snd_hbm, rcv_hbm, msk_hbm,
-    go_ref, gg_ref, gi_ref, at_ref, ge_ref,
+    go_ref, gg_ref, gi_ref, at_hbm, ge_hbm,
+    at_ref, ge_ref,
     eo_ref, ei_ref, gw_ref, ns_ref, og_ref, nm_ref, feat_ref, snd_ref, rcv_ref, msk_ref,
     wall, xsb, xo, wis, stage, stage1, stage2, wtmp, stmp, itmp, nmrow, featw, keyw,
     featp, featt, gbt, kron, emat, hid, hidt, slope, bmat, cmat, dsb, dpre, gacc, sacc, gfull, eights,
@@ -639,11 +640,11 @@
     row_out(1)
     plane_out(0, 0)
     row_own(1)
+    plane_out(0, 1)
     for t in others[2:]:
         row_out(t)
         plane_out(t - 1, 0)
         row_own(t)
-    plane_out(0, 1)
     hidden_grad(0, 8)
     plane_out(half - 2, 0)
     hidden_grad(8, 16)
@@ -723,29 +724,10 @@
     stage[...] = stage1[...].T
     at_ref[0 : z.uw, :] = stage[0 : z.uw, 0 : z.atoms] * nmrow[...]
     at_ref[z.uw : 2 * z.uw, :] = stage[z.uw : 2 * z.uw, 0 : z.atoms]
+    at_out = pltpu.make_async_copy(at_ref, at_hbm, lsem.at[0])
+    at_out.start()
 
     fin[...] = column(nmp - 1)
-
-    for col in zcols:
-        rcopy(giz.at[col], giz.at[col], gz_s.at[0], gz_r.at[col], cp).wait_recv()
-        gi_sum = gi_sum + giz[col].astype(f32)
-    gi_ref[...] = pltpu.roll(gi_sum, HID - d * z.ew, 1)[:, 0 : z.ew]
-
-    @pl.when(m > 0)
-    def _():
-        fin[...] += z_arrived(0, m)
-
-    @pl.when(m < nmp - 1)
-    def _():
-        fin[...] += z_arrived(1, m)
-
-    for s in range(2):
-        for g in range(3):
-            gg_ref[s, g] = fin[wr + 16 * s : wr + 16 * s + il, g * z.uw : (g + 1) * z.uw]
-    wtmp[...] = fin[0:wr, :].reshape(hl, rw, HID)
-    for r in range(rw):
-        go_ref[:, r * HID : (r + 1) * HID] = wtmp[:, r, :]
-
     edges_on(3)
     for j, lo in enumerate(z.starts):
         first = geo[j, :, 0:128]
@@ -755,6 +737,31 @@
         ge_ref[:, lo + 128 : lo + main] = geo[j, :, 128:main]
     if z.edges > z.full:
         ge_ref[:, z.full :] = geo[nmp - 1, :, main : main + z.edges - z.full]
+    ge_out = pltpu.make_async_copy(ge_ref, ge_hbm, lsem.at[1])
+    ge_out.start()
+
+    for col in zcols:
+        rcopy(giz.at[col], giz.at[col], gz_s.at[0], gz_r.at[col], cp).wait_recv()
+        gi_sum = gi_sum + giz[col].astype(f32)
+    gi_ref[...] = pltpu.roll(gi_sum, HID - d * z.ew, 1)[:, 0 : z.ew]
+
+    @pl.when(m > 0)
+    def _():
+        fin[...] += z_arrived(0, m)
+
+    @pl.when(m < nmp - 1)
+    def _():
+        fin[...] += z_arrived(1, m)
+
+    for s in range(2):
+        for g in range(3):
+            gg_ref[s, g] = fin[wr + 16 * s : wr + 16 * s + il, g * z.uw : (g + 1) * z.uw]
+    wtmp[...] = fin[0:wr, :].reshape(hl, rw, HID)
+    for r in range(rw):
+        go_ref[:, r * HID : (r + 1) * HID] = wtmp[:, r, :]
+
+    at_out.wait()
+    ge_out.wait()
     for i in range(nmp - 1):
         sends.extend(z_copies(i)[1])
     for y in sends:
@@ -780,8 +787,10 @@
             jax.ShapeDtypeStruct(feat.shape, bf),
         ),
         in_specs=[pl.BlockSpec(memory_space=pl.ANY)] * 10,
-        out_specs=(pl.BlockSpec(memory_space=vm),) * 5,
+        out_specs=(pl.BlockSpec(memory_space=vm),) * 3 + (pl.BlockSpec(memory_space=pl.ANY),) * 2,
         scratch_shapes=[
+            vm((2 * z.uw, z.atoms), f32),
+            vm(feat.shape, bf),
             *(vm(a.shape, a.dtype) for a in (eo, ei, gw, ns, og, live, feat, snd, rcv, msk)),
             vm((ndp, nmp, rb, HID), bf),
             vm((nmp, rows // 2, HID), bf),
@@ -871,16 +880,38 @@
     return (first_new, second_new, weight_new, weight_new.astype(bf))
 
 
-def finish_kernel(at_ref, ge_ref, *refs):
-    gs_uw = at_ref.shape[0] // 2
-    ins, outs = refs[:12], refs[12:]
-    outs[0][...] = at_ref[0:gs_uw, :]
-    outs[1][...] = at_ref[gs_uw:, :]
-    outs[2][...] = ge_ref[...].astype(f32)
-    for n in range(3):
-        new = adam_update(*[r[...] for r in ins[4 * n : 4 * n + 4]])
-        for ref, v in zip(outs[3 + 4 * n : 7 + 4 * n], new):
-            ref[...] = v
+def finish_kernel(*refs):
+    ins, outs = refs[:14], refs[14:29]
+    vin, vout = refs[29:43], refs[43:58]
+    isem, osem = refs[58:]
+    loads = [pltpu.make_async_copy(a, b, isem.at[i]) for i, (a, b) in enumerate(zip(ins, vin))]
+    stores = [pltpu.make_async_copy(a, b, osem.at[i]) for i, (a, b) in enumerate(zip(vout, outs))]
+    order = [1, 6, 7, 8, 9, 0, 2, 3, 4, 5, 10, 11, 12, 13]
+    for i in order:
+        loads[i].start()
+    loads[1].wait()
+    vout[2][...] = vin[1][...].astype(f32)
+    stores[2].start()
+
+    def layer(n):
+        for i in range(2 + 4 * n, 6 + 4 * n):
+            loads[i].wait()
+        new = adam_update(*[vin[i][...] for i in range(2 + 4 * n, 6 + 4 * n)])
+        for i, v in enumerate(new):
+            vout[3 + 4 * n + i][...] = v
+            stores[3 + 4 * n + i].start()
+
+    layer(1)
+    loads[0].wait()
+    uw = vin[0].shape[0] // 2
+    vout[0][...] = vin[0][0:uw, :]
+    vout[1][...] = vin[0][uw:, :]
+    stores[0].start()
+    stores[1].start()
+    layer(0)
+    layer(2)
+    for x in stores:
+        x.wait()
 
 
 def finish(at, ge, *layers):
@@ -888,13 +919,16 @@
     results = [half, half, jax.ShapeDtypeStruct(ge.shape, f32)]
     for n in range(3):
         results += [jax.ShapeDtypeStruct(layers[4 * n].shape, t) for t in (f32, f32, f32, bf)]
+    args = (at, ge, *layers)
     return pl.pallas_call(
         finish_kernel,
         out_shape=tuple(results),
-        in_specs=[pl.BlockSpec(memory_space=pltpu.VMEM)] * 14,
-        out_specs=(pl.BlockSpec(memory_space=pltpu.VMEM),) * 15,
+        in_specs=[pl.BlockSpec(memory_space=pl.ANY)] * 14,
+        out_specs=(pl.BlockSpec(memory_space=pl.ANY),) * 15,
+        scratch_shapes=[pltpu.VMEM(v.shape, v.dtype) for v in (*args, *results)]
+        + [pltpu.SemaphoreType.DMA((14,)), pltpu.SemaphoreType.DMA((15,))],
         compiler_params=pltpu.CompilerParams(vmem_limit_bytes=VMEM_LIMIT),
-    )(at, ge, *layers)
+    )(*args)
 
 
 def body(

time: 69.9 us -> 69.2 us (0.990)
  Pallas kernels: 68.9 us -> 68.2 us
where the time goes in v7:
time: 69.2 us; the launch traced here: 69 us
  Pallas kernels  68.2 us (99%)
  between operations  0.84 us (1%)
    pallas_call x1, Pallas kernels, whole_step(): pl.pallas_call(functools.partial(kernel, z), out_shape=(jax.ShapeDtypeStr...  65.3 us
    pallas_call x1, Pallas kernels, finish(): pl.pallas_call(finish_kernel, out_shape=tuple(results), in_specs=[pl.Bloc...  2.88 us

profile of v7, /device:TPU:0, one launch (start us, length us, event | category | flops | bytes accessed | tf_op | source)
XLA Modules:
  0.0 69.0 jit_solution(9841530687146304252)
XLA Ops:
  0.6 65.3 %shard_map.271 = (f32[16,4096]{1,0:T(8,128)}, f32[2,3,16,32]{3,2,1,0:T(8,128)}, f32[16,16]{1,0:T(8,128)}, f32[64,696]{1,0:T(8,128)}, bf16[16,19488]{1,0:T(8,128)(2,1)}) custom-call(f32[16,4096]{1,0:T(8,128)} %refs_6_.1, f32[16,16]{1,0:T(8,128)} %refs_2_.1, f32[2,3,16,32]{3,2,1,0:T(8,128)} %refs_10_.1, bf16[32,696]{1,0:T(8,128)(2,1)} %bitcast.5, ...), custom_call_target="tpu_custom_call" | custom-call | tf_op jit(solution)/shard_map/pallas_call | solution.py:780
  66.0 2.9 %shard_map.272 = (f32[32,696]{1,0:T(8,128)}, f32[32,696]{1,0:T(8,128)}, f32[16,19488]{1,0:T(8,128)}, f32[16,16]{1,0:T(8,128)}, f32[16,16]{1,0:T(8,128)}, /*index...) custom-call(f32[64,696]{1,0:T(8,128)} %get-tuple-element.35.refs_0_,, ...), custom_call_target="tpu_custom_call" | custom-call | tf_op jit(solution)/shard_map/pallas_call | solution.py:923

commit v8 on v7

--- a/solution.py
+++ b/solution.py
@@ -525,21 +525,22 @@
         tb[i] = (sb[1, i, ra:, :].astype(f32) + part_arrived(2, ra, col, 2)).astype(bf)
         go(rcopy(tb.at[i], r2b.at[col], p2s.at[1, i], p2r.at[1, col], px))
 
-    def column(i):
+    def column(i, k):
         col = cols[i]
-        core_arrived(half - 1, col)
-        q = grads[d, col].astype(f32) + rc[half - 1, col].astype(f32)
+        at = pl.ds(k * ra, ra)
+        if k == 0:
+            core_arrived(half - 1, col)
+        q = grads[d, col, at, :].astype(f32) + rc[half - 1, col, at, :].astype(f32)
         if not relay:
             for t in range(half - 1):
                 here = rp.at[t, col]
-                rcopy(here, here, fsem, pr.at[t, col], cp).wait_recv()
-                q = q + rp[t, col].astype(f32)
+                if k == 0:
+                    rcopy(here, here, fsem, pr.at[t, col], cp).wait_recv()
+                q = q + rp[t, col, at, :].astype(f32)
             return q
-        rcopy(r2a.at[col], r2a.at[col], fsem, p2r.at[0, col], cp).wait_recv()
-        rcopy(r2b.at[col], r2b.at[col], fsem, p2r.at[1, col], cp).wait_recv()
-        qa = q[:ra] + part_arrived(1, 0, col, 1) + r2a[col].astype(f32)
-        qb = q[ra:] + part_arrived(0, ra, col, 3) + r2b[col].astype(f32)
-        return jnp.concatenate([qa, qb], axis=0)
+        turned = (r2a, r2b)[k]
+        rcopy(turned.at[col], turned.at[col], fsem, p2r.at[k, col], cp).wait_recv()
+        return q + part_arrived(1 - k, k * ra, col, 1 + 2 * k) + turned[col].astype(f32)
 
     at_end = (m == 0) | (m == nmp - 1)
     between = (m > 0) & (m < nmp - 1)
@@ -547,11 +548,10 @@
     def z_piece(ref, k):
         return ref.at[pl.ds(k * ra, ra), :]
 
-    def z_arrived(way, col):
-        for k in (0, 1):
-            here = z_piece(rz.at[way, col], k)
-            rcopy(here, here, fsem, zr.at[way, col, k], cp).wait_recv()
-        return rz[way, col].astype(f32)
+    def z_arrived(way, col, k):
+        here = z_piece(rz.at[way, col], k)
+        rcopy(here, here, fsem, zr.at[way, col, k], cp).wait_recv()
+        return rz[way, col, k * ra : (k + 1) * ra, :].astype(f32)
 
     def z_copies(i):
         col = cols[i]
@@ -565,12 +565,12 @@
     def to_z(i, when, chained):
         @pl.when(when)
         def _():
-            q = column(i)
             way, copies = z_copies(i)
-            if chained:
-                q = q + z_arrived(way, cols[i])
-            zs[i] = q.astype(bf)
-            for x in copies:
+            for k, x in enumerate(copies):
+                q = column(i, k)
+                if chained:
+                    q = q + z_arrived(way, cols[i], k)
+                zs[i, k * ra : (k + 1) * ra, :] = q.astype(bf)
                 x.start()
 
     def by_eight(v, mask):
@@ -727,7 +727,8 @@
     at_out = pltpu.make_async_copy(at_ref, at_hbm, lsem.at[0])
     at_out.start()
 
-    fin[...] = column(nmp - 1)
+    for k in (0, 1):
+        fin[k * ra : (k + 1) * ra, :] = column(nmp - 1, k)
     edges_on(3)
     for j, lo in enumerate(z.starts):
         first = geo[j, :, 0:128]
@@ -747,11 +748,13 @@
 
     @pl.when(m > 0)
     def _():
-        fin[...] += z_arrived(0, m)
+        for k in (0, 1):
+            fin[k * ra : (k + 1) * ra, :] += z_arrived(0, m, k)
 
     @pl.when(m < nmp - 1)
     def _():
-        fin[...] += z_arrived(1, m)
+        for k in (0, 1):
+            fin[k * ra : (k + 1) * ra, :] += z_arrived(1, m, k)
 
     for s in range(2):
         for g in range(3):

time: 69.2 us -> 68.4 us (0.988)
  Pallas kernels: 68.2 us -> 67.4 us
    pallas_call x1, Pallas kernels: 65.3 us -> 64.5 us  [whole_step(): pl.pallas_call(functools.partial(kernel, z), out_shape=(jax.ShapeDtypeStr...]
where the time goes in v8:
time: 68.4 us; the launch traced here: 68.2 us
  Pallas kernels  67.4 us (99%)
  between operations  0.84 us (1%)
    pallas_call x1, Pallas kernels, whole_step(): pl.pallas_call(functools.partial(kernel, z), out_shape=(jax.ShapeDtypeStr...  64.5 us
    pallas_call x1, Pallas kernels, finish(): pl.pallas_call(finish_kernel, out_shape=tuple(results), in_specs=[pl.Bloc...  2.88 us

profile of v8, /device:TPU:0, one launch (start us, length us, event | category | flops | bytes accessed | tf_op | source)
XLA Modules:
  0.0 68.2 jit_solution(8912968897950729332)
XLA Ops:
  0.6 64.5 %shard_map.271 = (f32[16,4096]{1,0:T(8,128)}, f32[2,3,16,32]{3,2,1,0:T(8,128)}, f32[16,16]{1,0:T(8,128)}, f32[64,696]{1,0:T(8,128)}, bf16[16,19488]{1,0:T(8,128)(2,1)}) custom-call(f32[16,4096]{1,0:T(8,128)} %refs_6_.1, f32[16,16]{1,0:T(8,128)} %refs_2_.1, f32[2,3,16,32]{3,2,1,0:T(8,128)} %refs_10_.1, bf16[32,696]{1,0:T(8,128)(2,1)} %bitcast.5, ...), custom_call_target="tpu_custom_call" | custom-call | tf_op jit(solution)/shard_map/pallas_call | solution.py:783
  65.2 2.9 %shard_map.272 = (f32[32,696]{1,0:T(8,128)}, f32[32,696]{1,0:T(8,128)}, f32[16,19488]{1,0:T(8,128)}, f32[16,16]{1,0:T(8,128)}, f32[16,16]{1,0:T(8,128)}, /*index...) custom-call(f32[64,696]{1,0:T(8,128)} %get-tuple-element.35.refs_0_,, ...), custom_call_target="tpu_custom_call" | custom-call | tf_op jit(solution)/shard_map/pallas_call | solution.py:926
